TPU v7x, 32 devices: a whole 2x2x4 slice. The times are simulated.
32 devices in a mesh: seg: 16 (over z, x, core), rad: 2 (over y).
Axes of the slice: x: 2, y: 2, z: 4, core: 2. Of those that a mesh axis runs over, the one named last changes fastest.
Arguments:
- start_vector: float32 [16, 3, 2, 384, 768], P('seg', None, 'rad'), may hold values from -12 to 12
- coupling: bfloat16 [16, 3, 3, 2, 384, 768], P('seg', None, None, 'rad'), may hold values from -1.796875 to 1.796875
- advect: float32 [2], P('rad'), may hold values from 0.001 to 0.004
Outputs:
- next_basis: float32 [16, 3, 2, 384, 768], P('seg', None, 'rad')
- hessenberg: float32 [6], replicated
All inputs are finite; a program needn't handle non-finite values.
Results may differ from a plain program's by a relative error of at most 0.008.
Values may be sent and summed in bfloat16 or wider, within the bound.
No kernel may reach another device: no remote copies, remote signals or barrier semaphores. Data moves between devices by JAX's collectives and lax.ppermute only.
A program may use at most 128 MiB of HBM per device.

v0:
```python
import functools
import math

import jax
import jax.numpy as jnp
from jax import lax
from jax.experimental import pallas as pl
from jax.experimental.pallas import tpu as pltpu
from jax.sharding import PartitionSpec as P

RADIAL_ALL = 256
WINDOW_START = 124
RADIAL_GAIN = 0.25
VISC_AXIAL = 4.0
VISC_TURN = 0.05

F32 = jnp.float32
BF16 = jnp.bfloat16
VMEM_LIMIT = 8 * 1024 * 1024
TRANSFORM_LIMIT = 22 * 1024 * 1024
ROWS = 128
COLS = 256
BAND = 16
LONG = 10**11
MEDIUM = 15 * 10**9
CHUNK = 64
EARLY_ROWS = 128
LATE_ROWS = 128

IN_SMEM = pl.BlockSpec(memory_space=pltpu.SMEM)
IN_VMEM = pl.BlockSpec(memory_space=pltpu.VMEM)
IN_HBM = pl.BlockSpec(memory_space=pltpu.HBM)


def kernel_call(body, name, args, in_specs, outs, out_specs=None, scratch=(), limit=VMEM_LIMIT, flops=1000):
    held = [
        a if s is IN_SMEM else pltpu.with_memory_space_constraint(a, s.memory_space)
        for a, s in zip(args, in_specs)
    ]
    more = {} if out_specs is None else {"out_specs": out_specs}
    return pl.pallas_call(
        body,
        out_shape=outs,
        in_specs=in_specs,
        scratch_shapes=list(scratch),
        compiler_params=pltpu.CompilerParams(vmem_limit_bytes=limit),
        cost_estimate=pl.CostEstimate(flops=flops, bytes_accessed=1000, transcendentals=0),
        name=name,
        **more,
    )(*held)


def sine_turns(y):
    x = y * F32(2.0 * math.pi)
    x2 = x * x
    acc = F32(1.0 / 6227020800.0)
    for c in (-1.0 / 39916800.0, 1.0 / 362880.0, -1.0 / 5040.0, 1.0 / 120.0, -1.0 / 6.0, 1.0):
        acc = acc * x2 + F32(c)
    return acc * x


def trig_block(row0, rows, cols, mode_axis, count, weighted):
    half = count // 2
    r = lax.broadcasted_iota(jnp.int32, (rows, cols), 0) + row0
    c = lax.broadcasted_iota(jnp.int32, (rows, cols), 1)
    mode, point = (r, c) if mode_axis == 0 else (c, r)
    is_cos = mode <= half
    freq = jnp.where(is_cos, mode, mode - half).astype(F32)
    phase = freq * point.astype(F32) - jnp.where(is_cos, F32(0.0), F32(count // 4))
    phase = phase - F32(count) * jnp.floor(phase * F32(1.0 / count))
    value = -sine_turns(F32(0.25) - jnp.abs(phase * F32(1.0 / count) - F32(0.5)))
    if weighted:
        edge = (mode == 0) | (mode == half)
        value = value * jnp.where(edge, F32(1.0 / count), F32(2.0 / count))
    return value.astype(BF16)


def fill_table(ref, mode_axis, weighted):
    count = ref.shape[0]

    @pl.loop(0, count // ROWS)
    def _(i):
        at = pl.multiple_of(i * ROWS, ROWS)
        ref[pl.ds(at, ROWS), :] = trig_block(at, ROWS, count, mode_axis, count, weighted)


def taker(refs):
    refs = list(refs)

    def take(count=None):
        if count is None:
            return refs.pop(0)
        out, refs[:count] = refs[:count], []
        return out

    return take


def segments(modes_m, groups):
    ends, total = {modes_m}, 0
    for group in groups:
        total += group.shape[0]
        ends.add(total % modes_m or modes_m)
    ends = sorted(ends)
    return list(zip([0] + ends[:-1], ends))


def starts_of(groups):
    return [sum(g.shape[0] for g in groups[:n]) for n in range(len(groups))]


def band(groups, row, shift):
    for group in groups:
        if row < group.shape[0]:
            return group, pl.ds(pl.multiple_of(shift + row, BAND), BAND)
        row -= group.shape[0]


def read(groups, row, shift):
    group, at = band(groups, row, shift)
    return group[at, :]


def write(groups, row, shift, value):
    group, at = band(groups, row, shift)
    group[at, :] = value.astype(group.dtype)


def for_bands(lo, hi, body):
    @pl.loop(0, (hi - lo) // BAND)
    def _(i):
        body(pl.multiple_of(i * BAND, BAND))


def take_kernel(first, v, *refs):
    take = taker(refs)
    early = [] if first == 0 else [take()]
    field, rounded = take(), take()
    pieces, sems = take(len(refs) - len(early) - 3), take()
    count = field.shape[0]
    copies = []
    for n, r in enumerate(range(0, count, ROWS)):
        copies.append(
            pltpu.make_async_copy(v.at[pl.ds(first + r, ROWS)], field.at[pl.ds(r, ROWS)], sems.at[n])
        )
        copies[n].start()

    def lay(row, value):
        for n, piece in enumerate(pieces):
            at = row - n * piece.shape[0]
            if 0 <= at < piece.shape[0]:
                piece[at : at + ROWS, :] = value

    for r in range(0, first, ROWS):
        lay(r, early[0][r : r + ROWS, :])
    for n, r in enumerate(range(0, count, ROWS)):
        copies[n].wait()
        value = field[r : r + ROWS, :].astype(BF16)
        rounded[r : r + ROWS, :] = value
        lay(first + r, value)


def take_rows(v, first, count, early=(), pieces=0):
    rows, modes_k = v.shape
    shapes = [pltpu.VMEM((count, modes_k), F32), pltpu.VMEM((count, modes_k), BF16)]
    field, rounded, *by_channel = kernel_call(
        functools.partial(take_kernel, first),
        "take_rows",
        [v, *early],
        [IN_HBM] + [IN_VMEM] * len(early),
        shapes + [pltpu.VMEM((rows // max(pieces, 1), modes_k), BF16)] * pieces,
        scratch=[pltpu.SemaphoreType.DMA((count // ROWS,))],
    )
    return field, rounded, by_channel


def transform_kernel(build, awaited, *refs):
    take = taker(refs)
    chans = len(refs) - awaited - (14 if build else 13)
    x = take(chans)
    take(awaited)
    couple_far = take()
    tables_far = None if build else take(3)
    out = take()
    if build:
        tables_far, anal_m = take(3), take()
    one, phys, mixed, couple, synth_k, synth_mt, anal_kt, sems = take(8)
    near = (synth_k, synth_mt, anal_kt)
    _, modes_m, modes_k = out.shape
    load = pltpu.make_async_copy(couple_far, couple, sems.at[3])
    ends = [(n, f) if build else (f, n) for n, f in zip(near, tables_far)]
    moves = [pltpu.make_async_copy(src, dst, sems.at[i]) for i, (src, dst) in enumerate(ends)]
    if not build:
        for move in moves[:2]:
            move.start()
    load.start()
    if not build:
        moves[2].start()

    def ready(i, mode_axis, weighted):
        if build:
            fill_table(near[i], mode_axis, weighted)
            moves[i].start()
        else:
            moves[i].wait()

    ready(0, 0, False)
    for c in range(chans):

        @pl.loop(0, modes_m // ROWS)
        def _(i):
            at = pl.ds(pl.multiple_of(i * ROWS, ROWS), ROWS)
            one[c, at, :] = jnp.dot(x[c][at, :], synth_k[...], preferred_element_type=F32).astype(BF16)

    ready(1, 1, False)
    load.wait()

    @pl.loop(0, modes_k // COLS)
    def _(z):
        zs = pl.ds(pl.multiple_of(z * COLS, COLS), COLS)
        for j in range(chans):
            phys[j] = jnp.dot(synth_mt[...], one[j, :, zs], preferred_element_type=F32)

        @pl.loop(0, modes_m // BAND)
        def _(i):
            ts = pl.ds(pl.multiple_of(i * BAND, BAND), BAND)
            parts = [phys[j, ts, :] for j in range(chans)]
            for c in range(chans):
                total = couple[c, 0, ts, zs].astype(F32) * parts[0]
                for j in range(1, chans):
                    total += couple[c, j, ts, zs].astype(F32) * parts[j]
                mixed[c, ts, zs] = total.astype(BF16)

    ready(2, 1, True)
    for c in range(chans):

        @pl.loop(0, modes_m // ROWS)
        def _(i):
            at = pl.ds(pl.multiple_of(i * ROWS, ROWS), ROWS)
            out[c, at, :] = jnp.dot(mixed[c, at, :], anal_kt[...], preferred_element_type=F32).astype(BF16)

    if build:
        fill_table(anal_m, 0, True)
        for move in moves:
            move.wait()


def transform(x, couple, tables=None, awaited=()):
    chans, _, modes_m, modes_k = couple.shape
    shape = (chans, modes_m, modes_k)
    sizes = [(modes_k, modes_k), (modes_m, modes_m), (modes_k, modes_k)]
    build = tables is None
    far = [] if build else list(tables[:3])
    outs, out_specs = [pltpu.VMEM(shape, BF16)], [IN_VMEM]
    if build:
        outs += [pltpu.HBM(n, BF16) for n in sizes] + [pltpu.VMEM((modes_m, modes_m), BF16)]
        out_specs += [IN_HBM] * 3 + [IN_VMEM]
    result = kernel_call(
        functools.partial(transform_kernel, build, len(awaited)),
        "transform",
        [*x, *awaited, couple, *far],
        [IN_VMEM] * (chans + len(awaited)) + [IN_HBM] * (1 + len(far)),
        outs,
        out_specs=out_specs,
        scratch=[
            pltpu.VMEM(shape, BF16),
            pltpu.VMEM((chans, modes_m, COLS), F32),
            pltpu.VMEM(shape, BF16),
            pltpu.VMEM(couple.shape, BF16),
            *[pltpu.VMEM(n, BF16) for n in sizes],
            pltpu.SemaphoreType.DMA((4,)),
        ],
        limit=TRANSFORM_LIMIT,
        flops=MEDIUM if awaited else 1000,
    )
    return result[0], (result[1:] if build else tables)


def own_plane():
    return WINDOW_START + lax.axis_index("rad")


def paired_plane():
    return WINDOW_START + 1 - lax.axis_index("rad")


def inverse_divisor(row0, modes_m, modes_k, plane):
    m = lax.broadcasted_iota(jnp.int32, (BAND, 1), 0) + row0
    k = lax.broadcasted_iota(jnp.int32, (1, modes_k), 1)
    fm = jnp.where(m <= modes_m // 2, m, m - modes_m // 2).astype(F32) / F32(modes_m // 2)
    fk = jnp.where(k <= modes_k // 2, k, k - modes_k // 2).astype(F32) / F32(modes_k // 2)
    radius = (jnp.full((1, 1), plane, jnp.int32).astype(F32) + F32(0.5)) / F32(RADIAL_ALL)
    turning = F32(VISC_TURN) * fm * fm / (radius * radius)
    return F32(1.0) / (F32(1.0) + F32(VISC_AXIAL) * fk * fk + turning)


def add_tile(acc, n, value):
    value = sum(value[r : r + 8] for r in range(0, value.shape[0], 8))
    acc[n] += sum(value[:, k : k + 128] for k in range(0, value.shape[1], 128))


def local_kernel(counts, last, paired, advect, *refs):
    take = taker(refs)
    v, vb, recv = (take(n) for n in counts[:3])
    two, anal_m = take(), take()
    if last:
        u0, out_b = take(counts[3]), []
        out, scale, gram, spec, acc = take(5)
        acc[...] = jnp.zeros_like(acc)
    else:
        out, out_b, spec = take(), take(counts[3]), take()
    chans, modes_m, modes_k = two.shape
    half = modes_k // 2
    for c in range(chans):
        spec[c] = jnp.dot(anal_m[...], two[c], preferred_element_type=F32)
    wave = lax.broadcasted_iota(jnp.int32, (1, half), 1).astype(F32) * advect[0]

    def step(lo, shift):
        at = pl.ds(pl.multiple_of(shift + lo, BAND), BAND)
        inv = inverse_divisor(shift + lo, modes_m, modes_k, own_plane())
        if last:
            scale[at, :] = inv * F32(RADIAL_GAIN)
            if paired:
                mate = inverse_divisor(shift + lo, modes_m, modes_k, paired_plane()) * F32(RADIAL_GAIN**2)
        for c in range(chans):
            row = c * modes_m + lo
            own = read(v, row, shift)
            drift = jnp.concatenate([-wave * own[:, half:], wave * own[:, :half]], axis=1)
            mid = F32(-2.0 * RADIAL_GAIN) * read(vb, row, shift).astype(F32)
            total = own + spec[c, at, :] + drift + mid
            if last:
                x0 = read(u0, row, shift)
                if paired:
                    total += mate * x0
                for n, (a, b) in enumerate(((x0, x0), (x0, own), (own, own))):
                    add_tile(acc, n, a * b)
            value = total * inv - read(recv, row, shift).astype(F32)
            write([out], row, shift, value)
            if not last:
                write(out_b, row, shift, value)

    for lo, hi in segments(modes_m, [*v, *(u0 if last else out_b)]):
        for_bands(lo, hi, functools.partial(step, lo))

    if last:
        gram[...] = jnp.zeros_like(gram)
        for n in range(3):
            gram[n : n + 1, :] = jnp.sum(acc[n], axis=0, keepdims=True)


def local_first(advect, v, vb, recv, two, tables, sizes):
    chans, modes_m, modes_k = two.shape
    args = [advect, *v, *vb, *recv, two, tables[3]]
    part, *part_b = kernel_call(
        functools.partial(local_kernel, (len(v), len(vb), len(recv), len(sizes)), False, False),
        "local_first",
        args,
        [IN_SMEM] + [IN_VMEM] * (len(args) - 1),
        [pltpu.VMEM((chans * modes_m, modes_k), F32)] + [pltpu.VMEM((n, modes_k), BF16) for n in sizes],
        scratch=[pltpu.VMEM(two.shape, F32)],
    )
    return part, part_b


def local_last(advect, v, vb, recv, two, tables, u0, paired):
    chans, modes_m, modes_k = two.shape
    args = [advect, *v, *vb, *recv, two, tables[3], *u0]
    return kernel_call(
        functools.partial(local_kernel, (len(v), len(vb), len(recv), len(u0)), True, paired),
        "local_last",
        args,
        [IN_SMEM] + [IN_VMEM] * (len(args) - 1),
        [
            pltpu.VMEM((chans * modes_m, modes_k), F32),
            pltpu.VMEM((modes_m, modes_k), F32),
            pltpu.VMEM((8, 128), F32),
        ],
        scratch=[pltpu.VMEM(two.shape, F32), pltpu.VMEM((3, 8, 128), F32)],
    )


def added(sides, row, shift):
    return functools.reduce(lambda a, b: a + b, [read(s, row, shift).astype(F32) for s in sides])


def first_kernel(groups, count, part, *refs):
    take = taker(refs)
    sides = [take(groups) for _ in range(count)]
    out, out_b = take(), take(len(refs) - groups * count - 1)
    chans, (modes_m, modes_k) = len(out_b), out_b[0].shape

    def step(lo, shift):
        inv = inverse_divisor(shift + lo, modes_m, modes_k, own_plane()) * F32(RADIAL_GAIN)
        for c in range(chans):
            row = c * modes_m + lo
            value = read([part], row, shift) + added(sides, row, shift) * inv
            write([out], row, shift, value)
            write(out_b, row, shift, value)

    for lo, hi in segments(modes_m, sides[0]):
        for_bands(lo, hi, functools.partial(step, lo))


def first_image(part, sides, chans):
    rows, modes_k = part.shape
    args = [part, *(x for side in sides for x in side)]
    return kernel_call(
        functools.partial(first_kernel, len(sides[0]), len(sides)),
        "first_image",
        args,
        [IN_VMEM] * len(args),
        [pltpu.VMEM(part.shape, F32)] + [pltpu.VMEM((rows // chans, modes_k), BF16)] * chans,
        flops=LONG,
    )


def on_diagonal():
    rows, lanes = (lax.broadcasted_iota(jnp.int32, (8, 128), n) for n in (0, 1))
    return rows == lanes


def second_kernel(first, counts, done, scale, u1, part, before, *refs):
    take = taker(refs)
    u0, planes = take(counts[0]), take(counts[1])
    out, gram, acc = take(3)
    modes_m = scale.shape[0]
    acc[...] = jnp.zeros_like(acc)

    def step(row, shift):
        at = pl.ds(pl.multiple_of(shift + row % modes_m, BAND), BAND)
        near = added([[p] for p in planes], row - first, shift)
        x2 = read([part], row, shift) + near * scale[at, :]
        write([out], row - first, shift, x2)
        for n, x in enumerate((read(u0, row, shift), read([u1], row, shift), x2)):
            add_tile(acc, n, x * x2)

    end = first + out.shape[0]
    starts = {first, *starts_of(u0), *range(0, end, modes_m)}
    starts = [r for r in sorted(starts) if first <= r < end]
    for lo, hi in zip(starts, starts[1:] + [end]):
        for_bands(lo, hi, functools.partial(step, lo))

    rows = [jnp.sum(acc[n], axis=0, keepdims=True) for n in range(3)]
    total = before[...] + jnp.concatenate([jnp.zeros((3, 128), F32), *rows, jnp.zeros((2, 128), F32)], axis=0)
    if done:
        total = jnp.sum(total, axis=1, keepdims=True)
        total = jnp.sum(jnp.where(on_diagonal(), total, F32(0.0)), axis=0, keepdims=True)
    gram[...] = jnp.broadcast_to(total, gram.shape)


def second_image(first, scale, u0, u1, part, before, planes, slots=None):
    done = slots is not None
    tile = (slots, 128) if done else (8, 128)
    args = [scale, u1, part, before, *u0, *planes]
    return kernel_call(
        functools.partial(second_kernel, first, (len(u0), len(planes)), done),
        "second_image",
        args,
        [IN_VMEM] * len(args),
        [pltpu.VMEM(planes[0].shape, F32), pltpu.VMEM(tile, F32)],
        scratch=[pltpu.VMEM((3, 8, 128), F32)],
    )


def combine_kernel(cells, counts, grams, u1, *refs):
    take = taker(refs)
    u0, u2 = take(counts[0]), take(counts[1])
    out, hess, held, sems = take(4)
    total, modes_k = out.shape
    g = jnp.sum(grams[...], axis=0, keepdims=True) * F32(1.0 / cells)
    g = jnp.sum(jnp.where(on_diagonal(), g, F32(0.0)), axis=1, keepdims=True)
    g = jnp.broadcast_to(g, (8, 128))
    g00, g01, g11, g02, g12, g22 = (g[n : n + 1, :] for n in range(6))
    per_g00 = F32(1.0) / g00
    h11 = g01 * per_g00
    q = g11 - h11 * g01
    per_q = F32(1.0) / q
    w0 = g02 - h11 * g01
    w1 = g12 - h11 * g11
    ww = g22 - F32(2.0) * h11 * g12 + h11 * h11 * g11
    h22 = (w1 - h11 * w0) * per_q
    ratio = w0 * per_g00
    square = (ww - w0 * ratio) * per_q - h22 * h22
    c2 = F32(1.0) / jnp.sqrt(q * square)
    c1 = -(h11 + h22) * c2
    c0 = (h11 * h22 - ratio) * c2
    wide = [jnp.concatenate([x] * (modes_k // 128), axis=1) for x in (c0, c1, c2)]

    def copy_out(n):
        at = pl.ds(pl.multiple_of(n * CHUNK, CHUNK), CHUNK)
        return pltpu.make_async_copy(held.at[at], out.at[at], sems.at[n])

    def step(first, n):
        for r in range(0, CHUNK, BAND):
            row, shift = first + r, pl.multiple_of(n * CHUNK, CHUNK)
            value = wide[0] * read(u0, row, shift) + wide[1] * read([u1], row, shift)
            write([held], row, shift, value + wide[2] * read(u2, row, shift))
        copy_out(n + first // CHUNK).start()

    starts = sorted({*starts_of(u0), *starts_of(u2)})
    for first, end in zip(starts, starts[1:] + [total]):
        pl.loop(0, (end - first) // CHUNK)(functools.partial(step, first))
    n0, s = jnp.sqrt(g00), jnp.sqrt(q)
    for n, value in enumerate((n0, h11, s / n0, w0 / (s * n0), h22, jnp.sqrt(square))):
        hess[n] = value[0, 0]
    pl.loop(0, total // CHUNK)(lambda n: copy_out(n).wait())


def combine(cells, grams, u0, u1, u2):
    args = [grams, u1, *u0, *u2]
    return kernel_call(
        functools.partial(combine_kernel, cells, (len(u0), len(u2))),
        "combine",
        args,
        [IN_VMEM] * len(args),
        [jax.ShapeDtypeStruct(u1.shape, F32), jax.ShapeDtypeStruct((6,), F32)],
        out_specs=[IN_HBM, IN_SMEM],
        scratch=[pltpu.VMEM(u1.shape, F32), pltpu.SemaphoreType.DMA((u1.shape[0] // CHUNK,))],
    )


def shifted(value, axis, steps):
    count = lax.axis_size(axis)
    return lax.ppermute(value, axis, [(i, (i + steps) % count) for i in range(count)])


def neighbour_planes(value, axis):
    count = lax.axis_size(axis)
    if count == 2:
        return [lax.ppermute(value, axis, [(0, 1), (1, 0)])]
    up = [(i, i + 1) for i in range(count - 1)]
    return [lax.ppermute(value, axis, up), lax.ppermute(value, axis, [(b, a) for a, b in up])]


def on_device(start_vector, coupling, advect):
    _, chans, rows_here, modes_m, modes_k = start_vector.shape
    assert rows_here == 1
    rows = chans * modes_m
    start = start_vector.reshape(rows, modes_k)
    couple = coupling.reshape(chans, chans, modes_m, modes_k)
    devices = lax.axis_size("seg") * lax.axis_size("rad")
    cells = float(devices * start.size)
    paired = lax.axis_size("rad") == 2

    early = EARLY_ROWS
    sizes = (rows - LATE_ROWS, LATE_ROWS) if paired else (modes_m,) * chans

    u0, u0b, near_one, pieces = [], [], [], None
    for first, size, parts in ((0, early, 0), (early, rows - early, chans)):
        field, rounded, pieces = take_rows(start, first, size, u0b, parts)
        u0.append(field)
        u0b.append(rounded)
        near_one.append(neighbour_planes(rounded, "rad"))
    next_one = [shifted(x, "seg", -1) for x in pieces]
    two, tables = transform(pieces, couple, awaited=near_one[0])
    part, part_b = local_first(advect, u0, pieces, next_one, two, tables, sizes)
    if paired:
        near_two = [neighbour_planes(x, "rad") for x in part_b]
    u1, *u1b = first_image(part, list(zip(*near_one)), chans)
    if not paired:
        near_two = [neighbour_planes(x, "rad") for x in u1b]
    next_two = [shifted(x, "seg", -1) for x in u1b]
    two, _ = transform(u1b, couple, tables)
    part, scale, gram = local_last(advect, [u1], u1b, next_two, two, tables, u0, paired)
    u2, first = [], 0
    for size, planes in zip(sizes, near_two):
        slots = devices if first + size == rows else None
        field, gram = second_image(first, scale, u0, u1, part, gram, planes, slots)
        first += size
        u2.append(field)
    grams = lax.all_to_all(gram, ("rad", "seg"), 0, 0)
    basis, hess = combine(cells, grams, u0, u1, u2)
    return basis.reshape(start_vector.shape), hess


def solution(mesh):
    return jax.shard_map(
        on_device,
        mesh=mesh,
        in_specs=(
            P("seg", None, "rad", None, None),
            P("seg", None, None, "rad", None, None),
            P("rad"),
        ),
        out_specs=(P("seg", None, "rad", None, None), P()),
        check_vma=False,
    )
```

profile of v0, /device:TPU:0, one launch (start us, length us, event | category | flops | bytes accessed | tf_op | source)
XLA Modules:
  0.0 97.2 jit_solution(6748432995955432834)
XLA Ops:
  0.6 1.0 %take_rows.2 = (f32[128,768]{1,0:T(8,128)S(1)}, bf16[128,768]{1,0:T(8,128)(2,1)S(1)}) custom-call(f32[1152,768]{1,0:T(8,128)} %bitcast.11), custom_call_target="tpu_custom_call" | custom-call | flops 1000 | bytes 1000 | tf_op jit(solution)/shard_map/take_rows/pallas_call | solution.py:41
  1.7 3.0 %collective-permute-start.3 = (bf16[128,768]{1,0:T(8,128)(2,1)S(1)}, bf16[128,768]{1,0:T(8,128)(2,1)S(1)}, u32[]{:S(2)}, u32[]{:S(2)}) collective-permute-start(bf16[128,768]{1,0:T(8,128)(2,1)S(1)} %get-tuple-element.31.refs_0_), channel_id=1, source_target_pairs={{0,1},{1,0},{2,3},{3,2},{4,5},{5,4},{6,7},{7,6},{8,9},{9,8},{10,11... | collective-permute-start | bytes 589832 | tf_op jit(solution)/shard_map/ppermute | solution.py:530
  4.7 1.9 %take_rows.3 = (f32[1024,768]{1,0:T(8,128)S(1)}, bf16[1024,768]{1,0:T(8,128)(2,1)S(1)}, bf16[384,768]{1,0:T(8,128)(2,1)S(1)}, bf16[384,768]{1,0:T(8,128)(2,1)S(1)}, bf16[384,768]{1,0:T(8,128)(2,1)S(1)}) custom-call(f32[1152,768]{1,0:T(8,128)} %bitcast.12, bf16[128,768]{1,0:T(8,128)(2,1)S(1)} %get-tuple-element.31.refs_0_), custom_call_target="tpu_custom_call" | custom-call | flops 1000 | bytes 1000 | tf_op jit(solution)/shard_map/take_rows/pallas_call | solution.py:41
  6.6 0.1 collective-permute-start.4
  6.7 3.9 %collective-permute-start = (bf16[384,768]{1,0:T(8,128)(2,1)S(1)}, bf16[384,768]{1,0:T(8,128)(2,1)S(1)}, u32[]{:S(2)}, u32[]{:S(2)}) collective-permute-start(bf16[384,768]{1,0:T(8,128)(2,1)S(1)} %get-tuple-element.33.refs_0_.refs_2_), channel_id=1, source_target_pairs={{0,30},{2,0},{4,2},{6,4},{8,6},{10,8},{12,10},{14,12},{16,14},{18,... | collective-permute-start | bytes 1769480 | tf_op jit(solution)/shard_map/ppermute | solution.py:524
  10.6 1.2 %collective-permute-start.1 = (bf16[384,768]{1,0:T(8,128)(2,1)S(1)}, bf16[384,768]{1,0:T(8,128)(2,1)S(1)}, u32[]{:S(2)}, u32[]{:S(2)}) collective-permute-start(bf16[384,768]{1,0:T(8,128)(2,1)S(1)} %get-tuple-element.34.refs_1_.refs_3_), channel_id=1, source_target_pairs={{0,30},{2,0},{4,2},{6,4},{8,6},{10,8},{12,10},{14,12},{16,14},{18,... | collective-permute-start | bytes 1769480 | tf_op jit(solution)/shard_map/ppermute | solution.py:524
  11.8 0.0 collective-permute-start.2
  12.5 0.0 collective-permute-done.3.refs_3_.refs_0_
  12.5 14.5 %transform.2 = (bf16[3,384,768]{2,1,0:T(8,128)(2,1)S(1)}, bf16[768,768]{1,0:T(8,128)(2,1)}, bf16[384,384]{1,0:T(8,128)(2,1)}, bf16[768,768]{1,0:T(8,128)(2,1)}, bf16[384,384]{1,0:T(8,128)(2,1)S(1)}) custom-call(bf16[384,768]{1,0:T(8,128)(2,1)S(1)} %get-tuple-element.33.refs_0_.refs_2_, bf16[384,768]{1,0:T(8,128)(2,1)S(1)} %get-tuple-element.34.refs_1_.refs_3_, ...), custom_call_target="tpu_custom_call" | custom-call | flops 15000000512 | bytes 1000 | tf_op jit(solution)/shard_map/transform/pallas_call | solution.py:41
  27.1 0.0 collective-permute-done.refs_5_
  27.1 0.0 collective-permute-done.1.refs_6_
  27.1 3.6 %collective-permute-done.2.refs_7_ = bf16[384,768]{1,0:T(8,128)(2,1)S(1)} collective-permute-done((bf16[384,768]{1,0:T(8,128)(2,1)S(1)}, bf16[384,768]{1,0:T(8,128)(2,1)S(1)}, u32[]{:S(2)}, u32[]{:S(2)}) %collective-permute-start.2) | collective-permute-done | bytes 589856 | tf_op jit(solution)/shard_map/ppermute | solution.py:524
  30.6 2.8 %local_first.1 = (f32[1152,768]{1,0:T(8,128)S(1)}, bf16[1024,768]{1,0:T(8,128)(2,1)S(1)}, bf16[128,768]{1,0:T(8,128)(2,1)S(1)}) custom-call(f32[1]{0:T(128)S(6)} %copy.8.advect, f32[128,768]{1,0:T(8,128)S(1)} %get-tuple-element.30.refs_0_.refs_9_, f32[1024,768]{1,0:T(8,128)S(1)} %get-tuple-element.32.refs_1_.refs_10_, ...), custom_call_target="tpu_custom_call" | custom-call | flops 1000 | bytes 1000 | tf_op jit(solution)/shard_map/local_first/pallas_call | solution.py:41
  33.4 1.6 %collective-permute-start.8 = (bf16[1024,768]{1,0:T(8,128)(2,1)S(1)}, bf16[1024,768]{1,0:T(8,128)(2,1)S(1)}, u32[]{:S(2)}, u32[]{:S(2)}) collective-permute-start(bf16[1024,768]{1,0:T(8,128)(2,1)S(1)} %get-tuple-element.50), channel_id=1, source_target_pairs={{0,1},{1,0},{2,3},{3,2},{4,5},{5,4},{6,7},{7,6},{8,9},{9,8},{10,11... | collective-permute-start | bytes 4718600 | tf_op jit(solution)/shard_map/ppermute | solution.py:530
  35.0 9.0 %collective-permute-done.4.refs_1_ = bf16[1024,768]{1,0:T(8,128)(2,1)S(1)} collective-permute-done((bf16[1024,768]{1,0:T(8,128)(2,1)S(1)}, bf16[1024,768]{1,0:T(8,128)(2,1)S(1)}, u32[]{:S(2)}, u32[]{:S(2)}) %collective-permute-start.4) | collective-permute-done | bytes 1572896 | tf_op jit(solution)/shard_map/ppermute | solution.py:530
  44.0 1.2 %first_image.1 = (f32[1152,768]{1,0:T(8,128)S(1)}, bf16[384,768]{1,0:T(8,128)(2,1)S(1)}, bf16[384,768]{1,0:T(8,128)(2,1)S(1)}, bf16[384,768]{1,0:T(8,128)(2,1)S(1)}) custom-call(f32[1152,768]{1,0:T(8,128)S(1)} %get-tuple-element.38.part, bf16[128,768]{1,0:T(8,128)(2,1)S(1)} %collective-permute-done.3.refs_3_.refs_0_, ...), custom_call_target="tpu_custom_call" | custom-call | flops 99999997952 | bytes 1000 | tf_op jit(solution)/shard_map/first_image/pallas_call | solution.py:41
  45.2 2.9 %collective-permute-start.5 = (bf16[384,768]{1,0:T(8,128)(2,1)S(1)}, bf16[384,768]{1,0:T(8,128)(2,1)S(1)}, u32[]{:S(2)}, u32[]{:S(2)}) collective-permute-start(bf16[384,768]{1,0:T(8,128)(2,1)S(1)} %get-tuple-element.41.refs_0_.refs_1_), channel_id=1, source_target_pairs={{0,30},{2,0},{4,2},{6,4},{8,6},{10,8},{12,10},{14,12},{16,14},{18,... | collective-permute-start | bytes 1769480 | tf_op jit(solution)/shard_map/ppermute | solution.py:524
  48.1 2.2 %collective-permute-start.6 = (bf16[384,768]{1,0:T(8,128)(2,1)S(1)}, bf16[384,768]{1,0:T(8,128)(2,1)S(1)}, u32[]{:S(2)}, u32[]{:S(2)}) collective-permute-start(bf16[384,768]{1,0:T(8,128)(2,1)S(1)} %get-tuple-element.42.refs_1_.refs_2_), channel_id=1, source_target_pairs={{0,30},{2,0},{4,2},{6,4},{8,6},{10,8},{12,10},{14,12},{16,14},{18,... | collective-permute-start | bytes 1769480 | tf_op jit(solution)/shard_map/ppermute | solution.py:524
  50.4 0.1 collective-permute-start.7
  50.4 1.8 %collective-permute-start.9 = (bf16[128,768]{1,0:T(8,128)(2,1)S(1)}, bf16[128,768]{1,0:T(8,128)(2,1)S(1)}, u32[]{:S(2)}, u32[]{:S(2)}) collective-permute-start(bf16[128,768]{1,0:T(8,128)(2,1)S(1)} %get-tuple-element.52), channel_id=1, source_target_pairs={{0,1},{1,0},{2,3},{3,2},{4,5},{5,4},{6,7},{7,6},{8,9},{9,8},{10,11... | collective-permute-start | bytes 589832 | tf_op jit(solution)/shard_map/ppermute | solution.py:530
  52.2 10.2 %transform.3.refs_7_ = bf16[3,384,768]{2,1,0:T(8,128)(2,1)S(1)} custom-call(bf16[384,768]{1,0:T(8,128)(2,1)S(1)} %get-tuple-element.41.refs_0_.refs_1_, bf16[384,768]{1,0:T(8,128)(2,1)S(1)} %get-tuple-element.42.refs_1_.refs_2_, bf16[384,768]{1,0:T(8,128)(2,1)S(1)} %get-tuple-element.43.refs_2_.refs_3_, bf16[3,3,384,768]{3,2,1,0:T(8,128)(2,1)} %bitcast.14, ...), custom_call_target="tpu_custom_call" | custom-call | flops 1000 | bytes 1000 | tf_op jit(solution)/shard_map/transform/pallas_call | solution.py:41
  62.4 0.0 collective-permute-done.5.refs_4_
  62.4 0.0 collective-permute-done.6.refs_5_
  62.4 5.8 %collective-permute-done.7.refs_6_ = bf16[384,768]{1,0:T(8,128)(2,1)S(1)} collective-permute-done((bf16[384,768]{1,0:T(8,128)(2,1)S(1)}, bf16[384,768]{1,0:T(8,128)(2,1)S(1)}, u32[]{:S(2)}, u32[]{:S(2)}) %collective-permute-start.7) | collective-permute-done | bytes 589856 | tf_op jit(solution)/shard_map/ppermute | solution.py:524
  68.2 3.7 %local_last.1 = (f32[1152,768]{1,0:T(8,128)S(1)}, f32[384,768]{1,0:T(8,128)S(1)}, f32[8,128]{1,0:T(8,128)S(1)}) custom-call(f32[1]{0:T(128)S(6)} %copy.8.advect, f32[1152,768]{1,0:T(8,128)S(1)} %get-tuple-element.40.refs_0_.u1, bf16[384,768]{1,0:T(8,128)(2,1)S(1)} %get-tuple-element.41.refs_0_.refs_1_, ...), custom_call_target="tpu_custom_call" | custom-call | flops 1000 | bytes 1000 | tf_op jit(solution)/shard_map/local_last/pallas_call | solution.py:41
  71.9 5.8 %collective-permute-done.8.refs_2_ = bf16[1024,768]{1,0:T(8,128)(2,1)S(1)} collective-permute-done((bf16[1024,768]{1,0:T(8,128)(2,1)S(1)}, bf16[1024,768]{1,0:T(8,128)(2,1)S(1)}, u32[]{:S(2)}, u32[]{:S(2)}) %collective-permute-start.8) | collective-permute-done | bytes 1572896 | tf_op jit(solution)/shard_map/ppermute | solution.py:530
  77.7 1.6 %second_image.2 = (f32[1024,768]{1,0:T(8,128)S(1)}, f32[8,128]{1,0:T(8,128)S(1)}) custom-call(f32[384,768]{1,0:T(8,128)S(1)} %get-tuple-element.47.scale, f32[1152,768]{1,0:T(8,128)S(1)} %get-tuple-element.40.refs_0_.u1, f32[1152,768]{1,0:T(8,128)S(1)} %get-tuple-element.48.part, f32[8,128]{1,0:T(8,128)S(1)} %get-tuple-element.49.before, ...), custom_call_target="tpu_custom_call" | custom-call | flops 1000 | bytes 1000 | tf_op jit(solution)/shard_map/second_image/pallas_call | solution.py:41
  79.3 2.0 %collective-permute-done.9.refs_2_ = bf16[128,768]{1,0:T(8,128)(2,1)S(1)} collective-permute-done((bf16[128,768]{1,0:T(8,128)(2,1)S(1)}, bf16[128,768]{1,0:T(8,128)(2,1)S(1)}, u32[]{:S(2)}, u32[]{:S(2)}) %collective-permute-start.9) | collective-permute-done | bytes 196640 | tf_op jit(solution)/shard_map/ppermute | solution.py:530
  81.2 0.3 second_image.3
  81.5 13.0 %all_to_all.11 = f32[32,1,128]{2,1,0:T(1,128)S(1)} all-to-all(f32[32,1,128]{2,1,0:T(1,128)S(1)} %bitcast.10), channel_id=1, replica_groups=mesh['seg'=16,'rad'=2] {'rad','seg'}, dimensions={0} | all-to-all | bytes 32768 | tf_op jit(solution)/shard_map/all_to_all | solution.py:571
  94.5 2.6 %combine.1 = (f32[1152,768]{1,0:T(8,128)}, f32[6]{0:T(128)}) custom-call(f32[32,128]{1,0:T(8,128)S(1)} %bitcast.9, f32[1152,768]{1,0:T(8,128)S(1)} %get-tuple-element.40.refs_0_.u1, f32[128,768]{1,0:T(8,128)S(1)} %get-tuple-element.30.refs_0_.refs_9_, f32[1024,768]{1,0:T(8,128)S(1)} %get-tuple-element.32.refs_1_.refs_10_, ...), custom_call_target="tpu_custom_call" | custom-call | flops 1000 | bytes 1000 | tf_op jit(solution)/shard_map/combine/pallas_call | solution.py:41
Async XLA Ops:
  1.7 10.9 %collective-permute-start.3 = (bf16[128,768]{1,0:T(8,128)(2,1)S(1)}, bf16[128,768]{1,0:T(8,128)(2,1)S(1)}, u32[]{:S(2)}, u32[]{:S(2)}) collective-permute-start(bf16[128,768]{1,0:T(8,128)(2,1)S(1)} %get-tuple-element.31.refs_0_), channel_id=1, source_target_pairs={{0,1},{1,0},{2,3},{3,2},{4,5},{5,4},{6,7},{7,6},{8,9},{9,8},{10,11... | collective-permute-start | bytes 589832 | tf_op jit(solution)/shard_map/ppermute | solution.py:530
  6.6 37.4 %collective-permute-start.4 = (bf16[1024,768]{1,0:T(8,128)(2,1)S(1)}, bf16[1024,768]{1,0:T(8,128)(2,1)S(1)}, u32[]{:S(2)}, u32[]{:S(2)}) collective-permute-start(bf16[1024,768]{1,0:T(8,128)(2,1)S(1)} %get-tuple-element.39), channel_id=1, source_target_pairs={{0,1},{1,0},{2,3},{3,2},{4,5},{5,4},{6,7},{7,6},{8,9},{9,8},{10,11... | collective-permute-start | bytes 4718600 | tf_op jit(solution)/shard_map/ppermute | solution.py:530
  6.7 20.4 %collective-permute-start = (bf16[384,768]{1,0:T(8,128)(2,1)S(1)}, bf16[384,768]{1,0:T(8,128)(2,1)S(1)}, u32[]{:S(2)}, u32[]{:S(2)}) collective-permute-start(bf16[384,768]{1,0:T(8,128)(2,1)S(1)} %get-tuple-element.33.refs_0_.refs_2_), channel_id=1, source_target_pairs={{0,30},{2,0},{4,2},{6,4},{8,6},{10,8},{12,10},{14,12},{16,14},{18,... | collective-permute-start | bytes 1769480 | tf_op jit(solution)/shard_map/ppermute | solution.py:524
  10.6 16.5 %collective-permute-start.1 = (bf16[384,768]{1,0:T(8,128)(2,1)S(1)}, bf16[384,768]{1,0:T(8,128)(2,1)S(1)}, u32[]{:S(2)}, u32[]{:S(2)}) collective-permute-start(bf16[384,768]{1,0:T(8,128)(2,1)S(1)} %get-tuple-element.34.refs_1_.refs_3_), channel_id=1, source_target_pairs={{0,30},{2,0},{4,2},{6,4},{8,6},{10,8},{12,10},{14,12},{16,14},{18,... | collective-permute-start | bytes 1769480 | tf_op jit(solution)/shard_map/ppermute | solution.py:524
  11.8 18.8 %collective-permute-start.2 = (bf16[384,768]{1,0:T(8,128)(2,1)S(1)}, bf16[384,768]{1,0:T(8,128)(2,1)S(1)}, u32[]{:S(2)}, u32[]{:S(2)}) collective-permute-start(bf16[384,768]{1,0:T(8,128)(2,1)S(1)} %get-tuple-element.35.refs_2_.refs_4_), channel_id=1, source_target_pairs={{0,30},{2,0},{4,2},{6,4},{8,6},{10,8},{12,10},{14,12},{16,14},{18,... | collective-permute-start | bytes 1769480 | tf_op jit(solution)/shard_map/ppermute | solution.py:524
  33.4 44.3 %collective-permute-start.8 = (bf16[1024,768]{1,0:T(8,128)(2,1)S(1)}, bf16[1024,768]{1,0:T(8,128)(2,1)S(1)}, u32[]{:S(2)}, u32[]{:S(2)}) collective-permute-start(bf16[1024,768]{1,0:T(8,128)(2,1)S(1)} %get-tuple-element.50), channel_id=1, source_target_pairs={{0,1},{1,0},{2,3},{3,2},{4,5},{5,4},{6,7},{7,6},{8,9},{9,8},{10,11... | collective-permute-start | bytes 4718600 | tf_op jit(solution)/shard_map/ppermute | solution.py:530
  45.2 17.1 %collective-permute-start.5 = (bf16[384,768]{1,0:T(8,128)(2,1)S(1)}, bf16[384,768]{1,0:T(8,128)(2,1)S(1)}, u32[]{:S(2)}, u32[]{:S(2)}) collective-permute-start(bf16[384,768]{1,0:T(8,128)(2,1)S(1)} %get-tuple-element.41.refs_0_.refs_1_), channel_id=1, source_target_pairs={{0,30},{2,0},{4,2},{6,4},{8,6},{10,8},{12,10},{14,12},{16,14},{18,... | collective-permute-start | bytes 1769480 | tf_op jit(solution)/shard_map/ppermute | solution.py:524
  48.1 14.2 %collective-permute-start.6 = (bf16[384,768]{1,0:T(8,128)(2,1)S(1)}, bf16[384,768]{1,0:T(8,128)(2,1)S(1)}, u32[]{:S(2)}, u32[]{:S(2)}) collective-permute-start(bf16[384,768]{1,0:T(8,128)(2,1)S(1)} %get-tuple-element.42.refs_1_.refs_2_), channel_id=1, source_target_pairs={{0,30},{2,0},{4,2},{6,4},{8,6},{10,8},{12,10},{14,12},{16,14},{18,... | collective-permute-start | bytes 1769480 | tf_op jit(solution)/shard_map/ppermute | solution.py:524
  50.4 17.8 %collective-permute-start.7 = (bf16[384,768]{1,0:T(8,128)(2,1)S(1)}, bf16[384,768]{1,0:T(8,128)(2,1)S(1)}, u32[]{:S(2)}, u32[]{:S(2)}) collective-permute-start(bf16[384,768]{1,0:T(8,128)(2,1)S(1)} %get-tuple-element.43.refs_2_.refs_3_), channel_id=1, source_target_pairs={{0,30},{2,0},{4,2},{6,4},{8,6},{10,8},{12,10},{14,12},{16,14},{18,... | collective-permute-start | bytes 1769480 | tf_op jit(solution)/shard_map/ppermute | solution.py:524
  50.4 30.8 %collective-permute-start.9 = (bf16[128,768]{1,0:T(8,128)(2,1)S(1)}, bf16[128,768]{1,0:T(8,128)(2,1)S(1)}, u32[]{:S(2)}, u32[]{:S(2)}) collective-permute-start(bf16[128,768]{1,0:T(8,128)(2,1)S(1)} %get-tuple-element.52), channel_id=1, source_target_pairs={{0,1},{1,0},{2,3},{3,2},{4,5},{5,4},{6,7},{7,6},{8,9},{9,8},{10,11... | collective-permute-start | bytes 589832 | tf_op jit(solution)/shard_map/ppermute | solution.py:530
where the time goes:
time: 97.4 us; the launch traced here: 97.2 us
  Pallas kernels  39.9 us (41%)
  waiting for transfers between devices  26.1 us (27%)
  starting transfers between devices  16.8 us (17%)
  blocking collectives  13 us (13%)
  between operations  1.38 us (1%)
    pallas_call x10, Pallas kernels, kernel_call(): pl.pallas_call(body, out_shape=outs, in_specs=in_specs, scratch_shapes=li...  39.9 us
    ppermute x4, waiting for transfers between devices, neighbour_planes(): return [lax.ppermute(value, axis, [(0, 1), (1, 0)])]  16.7 us
    all_to_all x1, blocking collectives, on_device(): grams = lax.all_to_all(gram, ('rad', 'seg'), 0, 0)  13 us
    ppermute x6, starting transfers between devices, shifted(): lax.ppermute(value, axis, [(i, (i + steps) % count) for i in range(count)])  10.4 us
    ppermute x6, waiting for transfers between devices, shifted(): lax.ppermute(value, axis, [(i, (i + steps) % count) for i in range(count)])  9.36 us
    ppermute x4, starting transfers between devices, neighbour_planes(): return [lax.ppermute(value, axis, [(0, 1), (1, 0)])]  6.46 us
  transfers between devices with their start and end apart: 10, of which 5 were waited for; matrix products, arithmetic and copies ran while one was open for 0% of the time, Pallas kernels for 37%

commit v1 on v0

--- a/solution.py
+++ b/solution.py
@@ -532,6 +532,17 @@
     return [lax.ppermute(value, axis, up), lax.ppermute(value, axis, [(b, a) for a, b in up])]
 
 
+def summed(row, axes, devices):
+    step = 1
+    while step < devices and devices % (2 * step) == 0:
+        groups = [[i, i + step] for i in range(devices) if i // step % 2 == 0]
+        row = lax.psum(row, axes, axis_index_groups=groups)
+        step *= 2
+    if step < devices:
+        row = lax.psum(row, axes, axis_index_groups=[list(range(i, devices, step)) for i in range(step)])
+    return row
+
+
 def on_device(start_vector, coupling, advect):
     _, chans, rows_here, modes_m, modes_k = start_vector.shape
     assert rows_here == 1
@@ -564,11 +575,11 @@
     part, scale, gram = local_last(advect, [u1], u1b, next_two, two, tables, u0, paired)
     u2, first = [], 0
     for size, planes in zip(sizes, near_two):
-        slots = devices if first + size == rows else None
+        slots = 1 if first + size == rows else None
         field, gram = second_image(first, scale, u0, u1, part, gram, planes, slots)
         first += size
         u2.append(field)
-    grams = lax.all_to_all(gram, ("rad", "seg"), 0, 0)
+    grams = summed(gram, ("seg", "rad"), devices)
     basis, hess = combine(cells, grams, u0, u1, u2)
     return basis.reshape(start_vector.shape), hess
 

time: 97.4 us -> 113 us (1.16)
  blocking collectives: 13 us -> 23 us
  local copies, waits for them, and re-layouts: 0 us -> 5.65 us
    psum x0 -> x5, blocking collectives: none -> 23 us  [summed(): row = lax.psum(row, axes, axis_index_groups=groups)]
    all_to_all x1 -> x0, blocking collectives: 13 us -> none  [on_device(): grams = lax.all_to_all(gram, ('rad', 'seg'), 0, 0)]
    unnamed x0 -> x12, local copies, waits for them, and re-layouts: none -> 5.65 us
  transfers between devices with their start and end apart: 10 -> 10, of which waited for: 5 -> 5; matrix products, arithmetic and copies ran while one was open for 0% -> 0% of each run, Pallas kernels for 37% -> 32%
where the time goes in v1:
time: 113 us
  Pallas kernels  39.9 us (35%)
  waiting for transfers between devices  26 us (23%)
  blocking collectives  23 us (20%)
  starting transfers between devices  16.8 us (15%)
  local copies, waits for them, and re-layouts  5.65 us (5%)
  between operations  1.4 us (1%)
    pallas_call x10, Pallas kernels, kernel_call(): pl.pallas_call(body, out_shape=outs, in_specs=in_specs, scratch_shapes=li...  39.9 us
    psum x5, blocking collectives, summed(): row = lax.psum(row, axes, axis_index_groups=groups)  23 us
    ppermute x4, waiting for transfers between devices, neighbour_planes(): return [lax.ppermute(value, axis, [(0, 1), (1, 0)])]  16.7 us
    ppermute x6, starting transfers between devices, shifted(): lax.ppermute(value, axis, [(i, (i + steps) % count) for i in range(count)])  10.4 us
    ppermute x6, waiting for transfers between devices, shifted(): lax.ppermute(value, axis, [(i, (i + steps) % count) for i in range(count)])  9.33 us
    ppermute x4, starting transfers between devices, neighbour_planes(): return [lax.ppermute(value, axis, [(0, 1), (1, 0)])]  6.46 us
    unnamed x12, local copies, waits for them, and re-layouts  5.65 us
  transfers between devices with their start and end apart: 10, of which 5 were waited for; matrix products, arithmetic and copies ran while one was open for 0% of the time, Pallas kernels for 32%

profile of v1, /device:TPU:0, one launch (start us, length us, event | category | flops | bytes accessed | tf_op | source)
XLA Modules:
  0.0 112.8 jit_solution(4734316970189402909)
XLA Ops:
  0.6 1.0 take_rows.2
  1.7 3.0 %collective-permute-start.3 = (bf16[128,768]{1,0:T(8,128)(2,1)S(1)}, bf16[128,768]{1,0:T(8,128)(2,1)S(1)}, u32[]{:S(2)}, u32[]{:S(2)}) collective-permute-start(bf16[128,768]{1,0:T(8,128)(2,1)S(1)} %get-tuple-element.31.refs_0_), channel_id=1, source_target_pairs={{0,1},{1,0},{2,3},{3,2},{4,5},{5,4},{6,7},{7,6},{8,9},{9,8},{10,11... | collective-permute-start | bytes 589832 | tf_op jit(solution)/shard_map/ppermute | solution.py:530
  4.7 1.9 %take_rows.3 = (f32[1024,768]{1,0:T(8,128)S(1)}, bf16[1024,768]{1,0:T(8,128)(2,1)S(1)}, bf16[384,768]{1,0:T(8,128)(2,1)S(1)}, bf16[384,768]{1,0:T(8,128)(2,1)S(1)}, bf16[384,768]{1,0:T(8,128)(2,1)S(1)}) custom-call(f32[1152,768]{1,0:T(8,128)} %bitcast.6, bf16[128,768]{1,0:T(8,128)(2,1)S(1)} %get-tuple-element.31.refs_0_), custom_call_target="tpu_custom_call" | custom-call | flops 1000 | bytes 1000 | tf_op jit(solution)/shard_map/take_rows/pallas_call | solution.py:41
  6.6 0.1 collective-permute-start.4
  6.7 3.9 %collective-permute-start = (bf16[384,768]{1,0:T(8,128)(2,1)S(1)}, bf16[384,768]{1,0:T(8,128)(2,1)S(1)}, u32[]{:S(2)}, u32[]{:S(2)}) collective-permute-start(bf16[384,768]{1,0:T(8,128)(2,1)S(1)} %get-tuple-element.33.refs_0_.refs_2_), channel_id=1, source_target_pairs={{0,30},{2,0},{4,2},{6,4},{8,6},{10,8},{12,10},{14,12},{16,14},{18,... | collective-permute-start | bytes 1769480 | tf_op jit(solution)/shard_map/ppermute | solution.py:524
  10.6 1.2 %collective-permute-start.1 = (bf16[384,768]{1,0:T(8,128)(2,1)S(1)}, bf16[384,768]{1,0:T(8,128)(2,1)S(1)}, u32[]{:S(2)}, u32[]{:S(2)}) collective-permute-start(bf16[384,768]{1,0:T(8,128)(2,1)S(1)} %get-tuple-element.34.refs_1_.refs_3_), channel_id=1, source_target_pairs={{0,30},{2,0},{4,2},{6,4},{8,6},{10,8},{12,10},{14,12},{16,14},{18,... | collective-permute-start | bytes 1769480 | tf_op jit(solution)/shard_map/ppermute | solution.py:524
  11.8 0.0 collective-permute-start.2
  12.5 0.0 collective-permute-done.3.refs_3_.refs_0_
  12.5 14.5 %transform.2 = (bf16[3,384,768]{2,1,0:T(8,128)(2,1)S(1)}, bf16[768,768]{1,0:T(8,128)(2,1)}, bf16[384,384]{1,0:T(8,128)(2,1)}, bf16[768,768]{1,0:T(8,128)(2,1)}, bf16[384,384]{1,0:T(8,128)(2,1)S(1)}) custom-call(bf16[384,768]{1,0:T(8,128)(2,1)S(1)} %get-tuple-element.33.refs_0_.refs_2_, bf16[384,768]{1,0:T(8,128)(2,1)S(1)} %get-tuple-element.34.refs_1_.refs_3_, ...), custom_call_target="tpu_custom_call" | custom-call | flops 15000000512 | bytes 1000 | tf_op jit(solution)/shard_map/transform/pallas_call | solution.py:41
  27.1 0.0 collective-permute-done.refs_5_
  27.1 0.0 collective-permute-done.1.refs_6_
  27.1 3.6 %collective-permute-done.2.refs_7_ = bf16[384,768]{1,0:T(8,128)(2,1)S(1)} collective-permute-done((bf16[384,768]{1,0:T(8,128)(2,1)S(1)}, bf16[384,768]{1,0:T(8,128)(2,1)S(1)}, u32[]{:S(2)}, u32[]{:S(2)}) %collective-permute-start.2) | collective-permute-done | bytes 589856 | tf_op jit(solution)/shard_map/ppermute | solution.py:524
  30.6 2.8 %local_first.1 = (f32[1152,768]{1,0:T(8,128)S(1)}, bf16[1024,768]{1,0:T(8,128)(2,1)S(1)}, bf16[128,768]{1,0:T(8,128)(2,1)S(1)}) custom-call(f32[1]{0:T(128)S(6)} %copy.6.advect, f32[128,768]{1,0:T(8,128)S(1)} %get-tuple-element.30.refs_0_.refs_9_, f32[1024,768]{1,0:T(8,128)S(1)} %get-tuple-element.32.refs_1_.refs_10_, ...), custom_call_target="tpu_custom_call" | custom-call | flops 1000 | bytes 1000 | tf_op jit(solution)/shard_map/local_first/pallas_call | solution.py:41
  33.4 1.6 %collective-permute-start.8 = (bf16[1024,768]{1,0:T(8,128)(2,1)S(1)}, bf16[1024,768]{1,0:T(8,128)(2,1)S(1)}, u32[]{:S(2)}, u32[]{:S(2)}) collective-permute-start(bf16[1024,768]{1,0:T(8,128)(2,1)S(1)} %get-tuple-element.50), channel_id=1, source_target_pairs={{0,1},{1,0},{2,3},{3,2},{4,5},{5,4},{6,7},{7,6},{8,9},{9,8},{10,11... | collective-permute-start | bytes 4718600 | tf_op jit(solution)/shard_map/ppermute | solution.py:530
  35.0 9.0 %collective-permute-done.4.refs_1_ = bf16[1024,768]{1,0:T(8,128)(2,1)S(1)} collective-permute-done((bf16[1024,768]{1,0:T(8,128)(2,1)S(1)}, bf16[1024,768]{1,0:T(8,128)(2,1)S(1)}, u32[]{:S(2)}, u32[]{:S(2)}) %collective-permute-start.4) | collective-permute-done | bytes 1572896 | tf_op jit(solution)/shard_map/ppermute | solution.py:530
  44.0 1.2 %first_image.1 = (f32[1152,768]{1,0:T(8,128)S(1)}, bf16[384,768]{1,0:T(8,128)(2,1)S(1)}, bf16[384,768]{1,0:T(8,128)(2,1)S(1)}, bf16[384,768]{1,0:T(8,128)(2,1)S(1)}) custom-call(f32[1152,768]{1,0:T(8,128)S(1)} %get-tuple-element.38.part, bf16[128,768]{1,0:T(8,128)(2,1)S(1)} %collective-permute-done.3.refs_3_.refs_0_, ...), custom_call_target="tpu_custom_call" | custom-call | flops 99999997952 | bytes 1000 | tf_op jit(solution)/shard_map/first_image/pallas_call | solution.py:41
  45.2 0.0 copy-start
  45.2 2.9 %collective-permute-start.5 = (bf16[384,768]{1,0:T(8,128)(2,1)S(1)}, bf16[384,768]{1,0:T(8,128)(2,1)S(1)}, u32[]{:S(2)}, u32[]{:S(2)}) collective-permute-start(bf16[384,768]{1,0:T(8,128)(2,1)S(1)} %get-tuple-element.41.refs_0_.refs_1_), channel_id=1, source_target_pairs={{0,30},{2,0},{4,2},{6,4},{8,6},{10,8},{12,10},{14,12},{16,14},{18,... | collective-permute-start | bytes 1769480 | tf_op jit(solution)/shard_map/ppermute | solution.py:524
  48.2 2.2 %collective-permute-start.6 = (bf16[384,768]{1,0:T(8,128)(2,1)S(1)}, bf16[384,768]{1,0:T(8,128)(2,1)S(1)}, u32[]{:S(2)}, u32[]{:S(2)}) collective-permute-start(bf16[384,768]{1,0:T(8,128)(2,1)S(1)} %get-tuple-element.42.refs_1_.refs_2_), channel_id=1, source_target_pairs={{0,30},{2,0},{4,2},{6,4},{8,6},{10,8},{12,10},{14,12},{16,14},{18,... | collective-permute-start | bytes 1769480 | tf_op jit(solution)/shard_map/ppermute | solution.py:524
  50.4 0.1 collective-permute-start.7
  50.4 1.8 %collective-permute-start.9 = (bf16[128,768]{1,0:T(8,128)(2,1)S(1)}, bf16[128,768]{1,0:T(8,128)(2,1)S(1)}, u32[]{:S(2)}, u32[]{:S(2)}) collective-permute-start(bf16[128,768]{1,0:T(8,128)(2,1)S(1)} %get-tuple-element.52), channel_id=1, source_target_pairs={{0,1},{1,0},{2,3},{3,2},{4,5},{5,4},{6,7},{7,6},{8,9},{9,8},{10,11... | collective-permute-start | bytes 589832 | tf_op jit(solution)/shard_map/ppermute | solution.py:530
  52.2 10.2 %transform.3.refs_7_ = bf16[3,384,768]{2,1,0:T(8,128)(2,1)S(1)} custom-call(bf16[384,768]{1,0:T(8,128)(2,1)S(1)} %get-tuple-element.41.refs_0_.refs_1_, bf16[384,768]{1,0:T(8,128)(2,1)S(1)} %get-tuple-element.42.refs_1_.refs_2_, bf16[384,768]{1,0:T(8,128)(2,1)S(1)} %get-tuple-element.43.refs_2_.refs_3_, bf16[3,3,384,768]{3,2,1,0:T(8,128)(2,1)} %bitcast.8, ...), custom_call_target="tpu_custom_call" | custom-call | flops 1000 | bytes 1000 | tf_op jit(solution)/shard_map/transform/pallas_call | solution.py:41
  62.4 0.0 collective-permute-done.5.refs_4_
  62.4 0.0 collective-permute-done.6.refs_5_
  62.4 5.8 %collective-permute-done.7.refs_6_ = bf16[384,768]{1,0:T(8,128)(2,1)S(1)} collective-permute-done((bf16[384,768]{1,0:T(8,128)(2,1)S(1)}, bf16[384,768]{1,0:T(8,128)(2,1)S(1)}, u32[]{:S(2)}, u32[]{:S(2)}) %collective-permute-start.7) | collective-permute-done | bytes 589856 | tf_op jit(solution)/shard_map/ppermute | solution.py:524
  68.2 3.7 %local_last.1 = (f32[1152,768]{1,0:T(8,128)S(1)}, f32[384,768]{1,0:T(8,128)S(1)}, f32[8,128]{1,0:T(8,128)S(1)}) custom-call(f32[1]{0:T(128)S(6)} %copy.6.advect, f32[1152,768]{1,0:T(8,128)S(1)} %get-tuple-element.40.refs_0_.u1, bf16[384,768]{1,0:T(8,128)(2,1)S(1)} %get-tuple-element.41.refs_0_.refs_1_, ...), custom_call_target="tpu_custom_call" | custom-call | flops 1000 | bytes 1000 | tf_op jit(solution)/shard_map/local_last/pallas_call | solution.py:41
  71.9 5.8 %collective-permute-done.8.refs_2_ = bf16[1024,768]{1,0:T(8,128)(2,1)S(1)} collective-permute-done((bf16[1024,768]{1,0:T(8,128)(2,1)S(1)}, bf16[1024,768]{1,0:T(8,128)(2,1)S(1)}, u32[]{:S(2)}, u32[]{:S(2)}) %collective-permute-start.8) | collective-permute-done | bytes 1572896 | tf_op jit(solution)/shard_map/ppermute | solution.py:530
  77.7 1.6 %second_image.2 = (f32[1024,768]{1,0:T(8,128)S(1)}, f32[8,128]{1,0:T(8,128)S(1)}) custom-call(f32[384,768]{1,0:T(8,128)S(1)} %get-tuple-element.47.scale, f32[1152,768]{1,0:T(8,128)S(1)} %get-tuple-element.40.refs_0_.u1, f32[1152,768]{1,0:T(8,128)S(1)} %get-tuple-element.48.part, f32[8,128]{1,0:T(8,128)S(1)} %get-tuple-element.49.before, ...), custom_call_target="tpu_custom_call" | custom-call | flops 1000 | bytes 1000 | tf_op jit(solution)/shard_map/second_image/pallas_call | solution.py:41
  79.3 0.0 copy-start.2
  79.3 2.0 %collective-permute-done.9.refs_2_ = bf16[128,768]{1,0:T(8,128)(2,1)S(1)} collective-permute-done((bf16[128,768]{1,0:T(8,128)(2,1)S(1)}, bf16[128,768]{1,0:T(8,128)(2,1)S(1)}, u32[]{:S(2)}, u32[]{:S(2)}) %collective-permute-start.9) | collective-permute-done | bytes 196640 | tf_op jit(solution)/shard_map/ppermute | solution.py:530
  81.2 0.0 copy-done
  81.2 0.3 second_image.3
  81.5 0.0 copy-done.2
  81.5 0.0 copy-start.4
  81.5 0.8 copy-done.4
  82.3 4.9 %psum.35 = f32[1,128]{1,0:T(1,128)S(1)} all-reduce(f32[1,128]{1,0:T(1,128)S(1)} %get-tuple-element.53), channel_id=1, replica_groups={{0,1},{2,3},{4,5},{6,7},{8,9},{10,11},{12,13},{14,15},{16,17},{18,19},{..., use_global_device_ids=true, to_apply=%region_0.0 | all-reduce | flops 128 | bytes 1024 | tf_op jit(solution)/shard_map/psum | solution.py:539
  87.2 2.4 %psum.36 = f32[1,128]{1,0:T(1,128)S(1)} all-reduce(f32[1,128]{1,0:T(1,128)S(1)} %psum.35), channel_id=1, replica_groups={{0,2},{1,3},{4,6},{5,7},{8,10},{9,11},{12,14},{13,15},{16,18},{17,19},{..., use_global_device_ids=true, to_apply=%region_1.0 | all-reduce | flops 128 | bytes 1024 | tf_op jit(solution)/shard_map/psum | solution.py:539
  89.6 4.9 %psum.37 = f32[1,128]{1,0:T(1,128)S(1)} all-reduce(f32[1,128]{1,0:T(1,128)S(1)} %psum.36), channel_id=1, replica_groups={{0,4},{1,5},{2,6},{3,7},{8,12},{9,13},{10,14},{11,15},{16,20},{17,21},{..., use_global_device_ids=true, to_apply=%region_2.0 | all-reduce | flops 128 | bytes 1024 | tf_op jit(solution)/shard_map/psum | solution.py:539
  94.5 4.9 %psum.38 = f32[1,128]{1,0:T(1,128)S(1)} all-reduce(f32[1,128]{1,0:T(1,128)S(1)} %psum.37), channel_id=1, replica_groups={{0,8},{1,9},{2,10},{3,11},{4,12},{5,13},{6,14},{7,15},{16,24},{17,25},{..., use_global_device_ids=true, to_apply=%region_3.0 | all-reduce | flops 128 | bytes 1024 | tf_op jit(solution)/shard_map/psum | solution.py:539
  99.5 5.8 %psum.39.grams = f32[1,128]{1,0:T(1,128)S(1)} all-reduce(f32[1,128]{1,0:T(1,128)S(1)} %psum.38), channel_id=1, replica_groups={{0,16},{1,17},{2,18},{3,19},{4,20},{5,21},{6,22},{7,23},{8,24},{9,25},{..., use_global_device_ids=true, to_apply=%region_4.0 | all-reduce | flops 128 | bytes 1024 | tf_op jit(solution)/shard_map/psum | solution.py:539
  105.3 0.0 copy-start.1
  105.3 2.0 %copy-done.1 = f32[1152,768]{1,0:T(8,128)S(1)} copy-done((f32[1152,768]{1,0:T(8,128)S(1)}, f32[1152,768]{1,0:T(8,128)}, u32[]{:S(2)}) %copy-start.1) | copy-done | bytes 3538968
  107.3 0.0 copy-start.3
  107.3 1.9 %copy-done.3 = f32[1024,768]{1,0:T(8,128)S(1)} copy-done((f32[1024,768]{1,0:T(8,128)S(1)}, f32[1024,768]{1,0:T(8,128)}, u32[]{:S(2)}) %copy-start.3) | copy-done | bytes 3145752
  109.2 0.0 copy-start.5
  109.2 1.0 copy-done.5
  110.2 2.6 %combine.1 = (f32[1152,768]{1,0:T(8,128)}, f32[6]{0:T(128)}) custom-call(f32[1,128]{1,0:T(1,128)S(1)} %psum.39.grams, f32[1152,768]{1,0:T(8,128)S(1)} %copy-done.1, f32[128,768]{1,0:T(8,128)S(1)} %get-tuple-element.30.refs_0_.refs_9_, f32[1024,768]{1,0:T(8,128)S(1)} %get-tuple-element.32.refs_1_.refs_10_, f32[1024,768]{1,0:T(8,128)S(1)} %copy-done.3, ...), custom_call_target="tpu_custom_call" | custom-call | flops 1000 | bytes 1000 | tf_op jit(solution)/shard_map/combine/pallas_call | solution.py:41
Async XLA Ops:
  1.7 10.9 %collective-permute-start.3 = (bf16[128,768]{1,0:T(8,128)(2,1)S(1)}, bf16[128,768]{1,0:T(8,128)(2,1)S(1)}, u32[]{:S(2)}, u32[]{:S(2)}) collective-permute-start(bf16[128,768]{1,0:T(8,128)(2,1)S(1)} %get-tuple-element.31.refs_0_), channel_id=1, source_target_pairs={{0,1},{1,0},{2,3},{3,2},{4,5},{5,4},{6,7},{7,6},{8,9},{9,8},{10,11... | collective-permute-start | bytes 589832 | tf_op jit(solution)/shard_map/ppermute | solution.py:530
  6.6 37.4 %collective-permute-start.4 = (bf16[1024,768]{1,0:T(8,128)(2,1)S(1)}, bf16[1024,768]{1,0:T(8,128)(2,1)S(1)}, u32[]{:S(2)}, u32[]{:S(2)}) collective-permute-start(bf16[1024,768]{1,0:T(8,128)(2,1)S(1)} %get-tuple-element.39), channel_id=1, source_target_pairs={{0,1},{1,0},{2,3},{3,2},{4,5},{5,4},{6,7},{7,6},{8,9},{9,8},{10,11... | collective-permute-start | bytes 4718600 | tf_op jit(solution)/shard_map/ppermute | solution.py:530
  6.7 20.4 %collective-permute-start = (bf16[384,768]{1,0:T(8,128)(2,1)S(1)}, bf16[384,768]{1,0:T(8,128)(2,1)S(1)}, u32[]{:S(2)}, u32[]{:S(2)}) collective-permute-start(bf16[384,768]{1,0:T(8,128)(2,1)S(1)} %get-tuple-element.33.refs_0_.refs_2_), channel_id=1, source_target_pairs={{0,30},{2,0},{4,2},{6,4},{8,6},{10,8},{12,10},{14,12},{16,14},{18,... | collective-permute-start | bytes 1769480 | tf_op jit(solution)/shard_map/ppermute | solution.py:524
  10.6 16.5 %collective-permute-start.1 = (bf16[384,768]{1,0:T(8,128)(2,1)S(1)}, bf16[384,768]{1,0:T(8,128)(2,1)S(1)}, u32[]{:S(2)}, u32[]{:S(2)}) collective-permute-start(bf16[384,768]{1,0:T(8,128)(2,1)S(1)} %get-tuple-element.34.refs_1_.refs_3_), channel_id=1, source_target_pairs={{0,30},{2,0},{4,2},{6,4},{8,6},{10,8},{12,10},{14,12},{16,14},{18,... | collective-permute-start | bytes 1769480 | tf_op jit(solution)/shard_map/ppermute | solution.py:524
  11.8 18.8 %collective-permute-start.2 = (bf16[384,768]{1,0:T(8,128)(2,1)S(1)}, bf16[384,768]{1,0:T(8,128)(2,1)S(1)}, u32[]{:S(2)}, u32[]{:S(2)}) collective-permute-start(bf16[384,768]{1,0:T(8,128)(2,1)S(1)} %get-tuple-element.35.refs_2_.refs_4_), channel_id=1, source_target_pairs={{0,30},{2,0},{4,2},{6,4},{8,6},{10,8},{12,10},{14,12},{16,14},{18,... | collective-permute-start | bytes 1769480 | tf_op jit(solution)/shard_map/ppermute | solution.py:524
  33.4 44.3 %collective-permute-start.8 = (bf16[1024,768]{1,0:T(8,128)(2,1)S(1)}, bf16[1024,768]{1,0:T(8,128)(2,1)S(1)}, u32[]{:S(2)}, u32[]{:S(2)}) collective-permute-start(bf16[1024,768]{1,0:T(8,128)(2,1)S(1)} %get-tuple-element.50), channel_id=1, source_target_pairs={{0,1},{1,0},{2,3},{3,2},{4,5},{5,4},{6,7},{7,6},{8,9},{9,8},{10,11... | collective-permute-start | bytes 4718600 | tf_op jit(solution)/shard_map/ppermute | solution.py:530
  45.2 36.0 %copy-start = (f32[1152,768]{1,0:T(8,128)}, f32[1152,768]{1,0:T(8,128)S(1)}, u32[]{:S(2)}) copy-start(f32[1152,768]{1,0:T(8,128)S(1)} %get-tuple-element.40.refs_0_.u1) | copy-start | bytes 10616836
  45.2 17.2 %collective-permute-start.5 = (bf16[384,768]{1,0:T(8,128)(2,1)S(1)}, bf16[384,768]{1,0:T(8,128)(2,1)S(1)}, u32[]{:S(2)}, u32[]{:S(2)}) collective-permute-start(bf16[384,768]{1,0:T(8,128)(2,1)S(1)} %get-tuple-element.41.refs_0_.refs_1_), channel_id=1, source_target_pairs={{0,30},{2,0},{4,2},{6,4},{8,6},{10,8},{12,10},{14,12},{16,14},{18,... | collective-permute-start | bytes 1769480 | tf_op jit(solution)/shard_map/ppermute | solution.py:524
  48.2 14.3 %collective-permute-start.6 = (bf16[384,768]{1,0:T(8,128)(2,1)S(1)}, bf16[384,768]{1,0:T(8,128)(2,1)S(1)}, u32[]{:S(2)}, u32[]{:S(2)}) collective-permute-start(bf16[384,768]{1,0:T(8,128)(2,1)S(1)} %get-tuple-element.42.refs_1_.refs_2_), channel_id=1, source_target_pairs={{0,30},{2,0},{4,2},{6,4},{8,6},{10,8},{12,10},{14,12},{16,14},{18,... | collective-permute-start | bytes 1769480 | tf_op jit(solution)/shard_map/ppermute | solution.py:524
  50.4 17.8 %collective-permute-start.7 = (bf16[384,768]{1,0:T(8,128)(2,1)S(1)}, bf16[384,768]{1,0:T(8,128)(2,1)S(1)}, u32[]{:S(2)}, u32[]{:S(2)}) collective-permute-start(bf16[384,768]{1,0:T(8,128)(2,1)S(1)} %get-tuple-element.43.refs_2_.refs_3_), channel_id=1, source_target_pairs={{0,30},{2,0},{4,2},{6,4},{8,6},{10,8},{12,10},{14,12},{16,14},{18,... | collective-permute-start | bytes 1769480 | tf_op jit(solution)/shard_map/ppermute | solution.py:524
  50.4 30.8 %collective-permute-start.9 = (bf16[128,768]{1,0:T(8,128)(2,1)S(1)}, bf16[128,768]{1,0:T(8,128)(2,1)S(1)}, u32[]{:S(2)}, u32[]{:S(2)}) collective-permute-start(bf16[128,768]{1,0:T(8,128)(2,1)S(1)} %get-tuple-element.52), channel_id=1, source_target_pairs={{0,1},{1,0},{2,3},{3,2},{4,5},{5,4},{6,7},{7,6},{8,9},{9,8},{10,11... | collective-permute-start | bytes 589832 | tf_op jit(solution)/shard_map/ppermute | solution.py:530
  79.3 2.3 %copy-start.2 = (f32[1024,768]{1,0:T(8,128)}, f32[1024,768]{1,0:T(8,128)S(1)}, u32[]{:S(2)}) copy-start(f32[1024,768]{1,0:T(8,128)S(1)} %get-tuple-element.54.refs_2_) | copy-start | bytes 9437188
  81.5 0.8 copy-start.4
  105.3 2.0 %copy-start.1 = (f32[1152,768]{1,0:T(8,128)S(1)}, f32[1152,768]{1,0:T(8,128)}, u32[]{:S(2)}) copy-start(f32[1152,768]{1,0:T(8,128)} %copy-done) | copy-start | bytes 10616836
  107.3 1.9 %copy-start.3 = (f32[1024,768]{1,0:T(8,128)S(1)}, f32[1024,768]{1,0:T(8,128)}, u32[]{:S(2)}) copy-start(f32[1024,768]{1,0:T(8,128)} %copy-done.2) | copy-start | bytes 9437188
  109.2 1.0 copy-start.5

commit v2 on v0

--- a/solution.py
+++ b/solution.py
@@ -568,7 +568,7 @@
         field, gram = second_image(first, scale, u0, u1, part, gram, planes, slots)
         first += size
         u2.append(field)
-    grams = lax.all_to_all(gram, ("rad", "seg"), 0, 0)
+    grams = lax.all_to_all(gram, ("seg", "rad"), 0, 0)
     basis, hess = combine(cells, grams, u0, u1, u2)
     return basis.reshape(start_vector.shape), hess
 

time: 97.4 us -> 97.4 us (level)
  no operation moved by 1% of the time
where the time goes in v2:
time: 97.4 us; the launch traced here: 97.2 us
  Pallas kernels  39.9 us (41%)
  waiting for transfers between devices  26.1 us (27%)
  starting transfers between devices  16.8 us (17%)
  blocking collectives  13.1 us (13%)
  between operations  1.38 us (1%)
    pallas_call x10, Pallas kernels, kernel_call(): pl.pallas_call(body, out_shape=outs, in_specs=in_specs, scratch_shapes=li...  39.9 us
    ppermute x4, waiting for transfers between devices, neighbour_planes(): return [lax.ppermute(value, axis, [(0, 1), (1, 0)])]  16.7 us
    all_to_all x1, blocking collectives, on_device(): grams = lax.all_to_all(gram, ('seg', 'rad'), 0, 0)  13.1 us
    ppermute x6, starting transfers between devices, shifted(): lax.ppermute(value, axis, [(i, (i + steps) % count) for i in range(count)])  10.4 us
    ppermute x6, waiting for transfers between devices, shifted(): lax.ppermute(value, axis, [(i, (i + steps) % count) for i in range(count)])  9.36 us
    ppermute x4, starting transfers between devices, neighbour_planes(): return [lax.ppermute(value, axis, [(0, 1), (1, 0)])]  6.46 us
  transfers between devices with their start and end apart: 10, of which 5 were waited for; matrix products, arithmetic and copies ran while one was open for 0% of the time, Pallas kernels for 37%

profile of v2, /device:TPU:0, one launch (start us, length us, event | category | flops | bytes accessed | tf_op | source)
XLA Modules:
  0.0 97.2 jit_solution(16979478030670783454)
XLA Ops:
  0.6 1.0 %take_rows.2 = (f32[128,768]{1,0:T(8,128)S(1)}, bf16[128,768]{1,0:T(8,128)(2,1)S(1)}) custom-call(f32[1152,768]{1,0:T(8,128)} %bitcast.11), custom_call_target="tpu_custom_call" | custom-call | flops 1000 | bytes 1000 | tf_op jit(solution)/shard_map/take_rows/pallas_call | solution.py:41
  1.7 3.0 %collective-permute-start.3 = (bf16[128,768]{1,0:T(8,128)(2,1)S(1)}, bf16[128,768]{1,0:T(8,128)(2,1)S(1)}, u32[]{:S(2)}, u32[]{:S(2)}) collective-permute-start(bf16[128,768]{1,0:T(8,128)(2,1)S(1)} %get-tuple-element.31.refs_0_), channel_id=1, source_target_pairs={{0,1},{1,0},{2,3},{3,2},{4,5},{5,4},{6,7},{7,6},{8,9},{9,8},{10,11... | collective-permute-start | bytes 589832 | tf_op jit(solution)/shard_map/ppermute | solution.py:530
  4.7 1.9 %take_rows.3 = (f32[1024,768]{1,0:T(8,128)S(1)}, bf16[1024,768]{1,0:T(8,128)(2,1)S(1)}, bf16[384,768]{1,0:T(8,128)(2,1)S(1)}, bf16[384,768]{1,0:T(8,128)(2,1)S(1)}, bf16[384,768]{1,0:T(8,128)(2,1)S(1)}) custom-call(f32[1152,768]{1,0:T(8,128)} %bitcast.12, bf16[128,768]{1,0:T(8,128)(2,1)S(1)} %get-tuple-element.31.refs_0_), custom_call_target="tpu_custom_call" | custom-call | flops 1000 | bytes 1000 | tf_op jit(solution)/shard_map/take_rows/pallas_call | solution.py:41
  6.6 0.1 collective-permute-start.4
  6.7 3.9 %collective-permute-start = (bf16[384,768]{1,0:T(8,128)(2,1)S(1)}, bf16[384,768]{1,0:T(8,128)(2,1)S(1)}, u32[]{:S(2)}, u32[]{:S(2)}) collective-permute-start(bf16[384,768]{1,0:T(8,128)(2,1)S(1)} %get-tuple-element.33.refs_0_.refs_2_), channel_id=1, source_target_pairs={{0,30},{2,0},{4,2},{6,4},{8,6},{10,8},{12,10},{14,12},{16,14},{18,... | collective-permute-start | bytes 1769480 | tf_op jit(solution)/shard_map/ppermute | solution.py:524
  10.6 1.2 %collective-permute-start.1 = (bf16[384,768]{1,0:T(8,128)(2,1)S(1)}, bf16[384,768]{1,0:T(8,128)(2,1)S(1)}, u32[]{:S(2)}, u32[]{:S(2)}) collective-permute-start(bf16[384,768]{1,0:T(8,128)(2,1)S(1)} %get-tuple-element.34.refs_1_.refs_3_), channel_id=1, source_target_pairs={{0,30},{2,0},{4,2},{6,4},{8,6},{10,8},{12,10},{14,12},{16,14},{18,... | collective-permute-start | bytes 1769480 | tf_op jit(solution)/shard_map/ppermute | solution.py:524
  11.8 0.0 collective-permute-start.2
  12.5 0.0 collective-permute-done.3.refs_3_.refs_0_
  12.5 14.5 %transform.2 = (bf16[3,384,768]{2,1,0:T(8,128)(2,1)S(1)}, bf16[768,768]{1,0:T(8,128)(2,1)}, bf16[384,384]{1,0:T(8,128)(2,1)}, bf16[768,768]{1,0:T(8,128)(2,1)}, bf16[384,384]{1,0:T(8,128)(2,1)S(1)}) custom-call(bf16[384,768]{1,0:T(8,128)(2,1)S(1)} %get-tuple-element.33.refs_0_.refs_2_, bf16[384,768]{1,0:T(8,128)(2,1)S(1)} %get-tuple-element.34.refs_1_.refs_3_, ...), custom_call_target="tpu_custom_call" | custom-call | flops 15000000512 | bytes 1000 | tf_op jit(solution)/shard_map/transform/pallas_call | solution.py:41
  27.1 0.0 collective-permute-done.refs_5_
  27.1 0.0 collective-permute-done.1.refs_6_
  27.1 3.6 %collective-permute-done.2.refs_7_ = bf16[384,768]{1,0:T(8,128)(2,1)S(1)} collective-permute-done((bf16[384,768]{1,0:T(8,128)(2,1)S(1)}, bf16[384,768]{1,0:T(8,128)(2,1)S(1)}, u32[]{:S(2)}, u32[]{:S(2)}) %collective-permute-start.2) | collective-permute-done | bytes 589856 | tf_op jit(solution)/shard_map/ppermute | solution.py:524
  30.6 2.8 %local_first.1 = (f32[1152,768]{1,0:T(8,128)S(1)}, bf16[1024,768]{1,0:T(8,128)(2,1)S(1)}, bf16[128,768]{1,0:T(8,128)(2,1)S(1)}) custom-call(f32[1]{0:T(128)S(6)} %copy.8.advect, f32[128,768]{1,0:T(8,128)S(1)} %get-tuple-element.30.refs_0_.refs_9_, f32[1024,768]{1,0:T(8,128)S(1)} %get-tuple-element.32.refs_1_.refs_10_, ...), custom_call_target="tpu_custom_call" | custom-call | flops 1000 | bytes 1000 | tf_op jit(solution)/shard_map/local_first/pallas_call | solution.py:41
  33.4 1.6 %collective-permute-start.8 = (bf16[1024,768]{1,0:T(8,128)(2,1)S(1)}, bf16[1024,768]{1,0:T(8,128)(2,1)S(1)}, u32[]{:S(2)}, u32[]{:S(2)}) collective-permute-start(bf16[1024,768]{1,0:T(8,128)(2,1)S(1)} %get-tuple-element.50), channel_id=1, source_target_pairs={{0,1},{1,0},{2,3},{3,2},{4,5},{5,4},{6,7},{7,6},{8,9},{9,8},{10,11... | collective-permute-start | bytes 4718600 | tf_op jit(solution)/shard_map/ppermute | solution.py:530
  35.0 9.0 %collective-permute-done.4.refs_1_ = bf16[1024,768]{1,0:T(8,128)(2,1)S(1)} collective-permute-done((bf16[1024,768]{1,0:T(8,128)(2,1)S(1)}, bf16[1024,768]{1,0:T(8,128)(2,1)S(1)}, u32[]{:S(2)}, u32[]{:S(2)}) %collective-permute-start.4) | collective-permute-done | bytes 1572896 | tf_op jit(solution)/shard_map/ppermute | solution.py:530
  44.0 1.2 %first_image.1 = (f32[1152,768]{1,0:T(8,128)S(1)}, bf16[384,768]{1,0:T(8,128)(2,1)S(1)}, bf16[384,768]{1,0:T(8,128)(2,1)S(1)}, bf16[384,768]{1,0:T(8,128)(2,1)S(1)}) custom-call(f32[1152,768]{1,0:T(8,128)S(1)} %get-tuple-element.38.part, bf16[128,768]{1,0:T(8,128)(2,1)S(1)} %collective-permute-done.3.refs_3_.refs_0_, ...), custom_call_target="tpu_custom_call" | custom-call | flops 99999997952 | bytes 1000 | tf_op jit(solution)/shard_map/first_image/pallas_call | solution.py:41
  45.2 2.9 %collective-permute-start.5 = (bf16[384,768]{1,0:T(8,128)(2,1)S(1)}, bf16[384,768]{1,0:T(8,128)(2,1)S(1)}, u32[]{:S(2)}, u32[]{:S(2)}) collective-permute-start(bf16[384,768]{1,0:T(8,128)(2,1)S(1)} %get-tuple-element.41.refs_0_.refs_1_), channel_id=1, source_target_pairs={{0,30},{2,0},{4,2},{6,4},{8,6},{10,8},{12,10},{14,12},{16,14},{18,... | collective-permute-start | bytes 1769480 | tf_op jit(solution)/shard_map/ppermute | solution.py:524
  48.1 2.2 %collective-permute-start.6 = (bf16[384,768]{1,0:T(8,128)(2,1)S(1)}, bf16[384,768]{1,0:T(8,128)(2,1)S(1)}, u32[]{:S(2)}, u32[]{:S(2)}) collective-permute-start(bf16[384,768]{1,0:T(8,128)(2,1)S(1)} %get-tuple-element.42.refs_1_.refs_2_), channel_id=1, source_target_pairs={{0,30},{2,0},{4,2},{6,4},{8,6},{10,8},{12,10},{14,12},{16,14},{18,... | collective-permute-start | bytes 1769480 | tf_op jit(solution)/shard_map/ppermute | solution.py:524
  50.4 0.1 collective-permute-start.7
  50.4 1.8 %collective-permute-start.9 = (bf16[128,768]{1,0:T(8,128)(2,1)S(1)}, bf16[128,768]{1,0:T(8,128)(2,1)S(1)}, u32[]{:S(2)}, u32[]{:S(2)}) collective-permute-start(bf16[128,768]{1,0:T(8,128)(2,1)S(1)} %get-tuple-element.52), channel_id=1, source_target_pairs={{0,1},{1,0},{2,3},{3,2},{4,5},{5,4},{6,7},{7,6},{8,9},{9,8},{10,11... | collective-permute-start | bytes 589832 | tf_op jit(solution)/shard_map/ppermute | solution.py:530
  52.2 10.2 %transform.3.refs_7_ = bf16[3,384,768]{2,1,0:T(8,128)(2,1)S(1)} custom-call(bf16[384,768]{1,0:T(8,128)(2,1)S(1)} %get-tuple-element.41.refs_0_.refs_1_, bf16[384,768]{1,0:T(8,128)(2,1)S(1)} %get-tuple-element.42.refs_1_.refs_2_, bf16[384,768]{1,0:T(8,128)(2,1)S(1)} %get-tuple-element.43.refs_2_.refs_3_, bf16[3,3,384,768]{3,2,1,0:T(8,128)(2,1)} %bitcast.14, ...), custom_call_target="tpu_custom_call" | custom-call | flops 1000 | bytes 1000 | tf_op jit(solution)/shard_map/transform/pallas_call | solution.py:41
  62.4 0.0 collective-permute-done.5.refs_4_
  62.4 0.0 collective-permute-done.6.refs_5_
  62.4 5.8 %collective-permute-done.7.refs_6_ = bf16[384,768]{1,0:T(8,128)(2,1)S(1)} collective-permute-done((bf16[384,768]{1,0:T(8,128)(2,1)S(1)}, bf16[384,768]{1,0:T(8,128)(2,1)S(1)}, u32[]{:S(2)}, u32[]{:S(2)}) %collective-permute-start.7) | collective-permute-done | bytes 589856 | tf_op jit(solution)/shard_map/ppermute | solution.py:524
  68.2 3.7 %local_last.1 = (f32[1152,768]{1,0:T(8,128)S(1)}, f32[384,768]{1,0:T(8,128)S(1)}, f32[8,128]{1,0:T(8,128)S(1)}) custom-call(f32[1]{0:T(128)S(6)} %copy.8.advect, f32[1152,768]{1,0:T(8,128)S(1)} %get-tuple-element.40.refs_0_.u1, bf16[384,768]{1,0:T(8,128)(2,1)S(1)} %get-tuple-element.41.refs_0_.refs_1_, ...), custom_call_target="tpu_custom_call" | custom-call | flops 1000 | bytes 1000 | tf_op jit(solution)/shard_map/local_last/pallas_call | solution.py:41
  71.9 5.8 %collective-permute-done.8.refs_2_ = bf16[1024,768]{1,0:T(8,128)(2,1)S(1)} collective-permute-done((bf16[1024,768]{1,0:T(8,128)(2,1)S(1)}, bf16[1024,768]{1,0:T(8,128)(2,1)S(1)}, u32[]{:S(2)}, u32[]{:S(2)}) %collective-permute-start.8) | collective-permute-done | bytes 1572896 | tf_op jit(solution)/shard_map/ppermute | solution.py:530
  77.7 1.6 %second_image.2 = (f32[1024,768]{1,0:T(8,128)S(1)}, f32[8,128]{1,0:T(8,128)S(1)}) custom-call(f32[384,768]{1,0:T(8,128)S(1)} %get-tuple-element.47.scale, f32[1152,768]{1,0:T(8,128)S(1)} %get-tuple-element.40.refs_0_.u1, f32[1152,768]{1,0:T(8,128)S(1)} %get-tuple-element.48.part, f32[8,128]{1,0:T(8,128)S(1)} %get-tuple-element.49.before, ...), custom_call_target="tpu_custom_call" | custom-call | flops 1000 | bytes 1000 | tf_op jit(solution)/shard_map/second_image/pallas_call | solution.py:41
  79.3 2.0 %collective-permute-done.9.refs_2_ = bf16[128,768]{1,0:T(8,128)(2,1)S(1)} collective-permute-done((bf16[128,768]{1,0:T(8,128)(2,1)S(1)}, bf16[128,768]{1,0:T(8,128)(2,1)S(1)}, u32[]{:S(2)}, u32[]{:S(2)}) %collective-permute-start.9) | collective-permute-done | bytes 196640 | tf_op jit(solution)/shard_map/ppermute | solution.py:530
  81.2 0.3 second_image.3
  81.5 13.1 %all_to_all.11 = f32[32,1,128]{2,1,0:T(1,128)S(1)} all-to-all(f32[32,1,128]{2,1,0:T(1,128)S(1)} %bitcast.10), channel_id=1, replica_groups=mesh['seg'=16,'rad'=2] {'seg','rad'}, dimensions={0} | all-to-all | bytes 32768 | tf_op jit(solution)/shard_map/all_to_all | solution.py:571
  94.6 2.6 %combine.1 = (f32[1152,768]{1,0:T(8,128)}, f32[6]{0:T(128)}) custom-call(f32[32,128]{1,0:T(8,128)S(1)} %bitcast.9, f32[1152,768]{1,0:T(8,128)S(1)} %get-tuple-element.40.refs_0_.u1, f32[128,768]{1,0:T(8,128)S(1)} %get-tuple-element.30.refs_0_.refs_9_, f32[1024,768]{1,0:T(8,128)S(1)} %get-tuple-element.32.refs_1_.refs_10_, ...), custom_call_target="tpu_custom_call" | custom-call | flops 1000 | bytes 1000 | tf_op jit(solution)/shard_map/combine/pallas_call | solution.py:41
Async XLA Ops:
  1.7 10.9 %collective-permute-start.3 = (bf16[128,768]{1,0:T(8,128)(2,1)S(1)}, bf16[128,768]{1,0:T(8,128)(2,1)S(1)}, u32[]{:S(2)}, u32[]{:S(2)}) collective-permute-start(bf16[128,768]{1,0:T(8,128)(2,1)S(1)} %get-tuple-element.31.refs_0_), channel_id=1, source_target_pairs={{0,1},{1,0},{2,3},{3,2},{4,5},{5,4},{6,7},{7,6},{8,9},{9,8},{10,11... | collective-permute-start | bytes 589832 | tf_op jit(solution)/shard_map/ppermute | solution.py:530
  6.6 37.4 %collective-permute-start.4 = (bf16[1024,768]{1,0:T(8,128)(2,1)S(1)}, bf16[1024,768]{1,0:T(8,128)(2,1)S(1)}, u32[]{:S(2)}, u32[]{:S(2)}) collective-permute-start(bf16[1024,768]{1,0:T(8,128)(2,1)S(1)} %get-tuple-element.39), channel_id=1, source_target_pairs={{0,1},{1,0},{2,3},{3,2},{4,5},{5,4},{6,7},{7,6},{8,9},{9,8},{10,11... | collective-permute-start | bytes 4718600 | tf_op jit(solution)/shard_map/ppermute | solution.py:530
  6.7 20.4 %collective-permute-start = (bf16[384,768]{1,0:T(8,128)(2,1)S(1)}, bf16[384,768]{1,0:T(8,128)(2,1)S(1)}, u32[]{:S(2)}, u32[]{:S(2)}) collective-permute-start(bf16[384,768]{1,0:T(8,128)(2,1)S(1)} %get-tuple-element.33.refs_0_.refs_2_), channel_id=1, source_target_pairs={{0,30},{2,0},{4,2},{6,4},{8,6},{10,8},{12,10},{14,12},{16,14},{18,... | collective-permute-start | bytes 1769480 | tf_op jit(solution)/shard_map/ppermute | solution.py:524
  10.6 16.5 %collective-permute-start.1 = (bf16[384,768]{1,0:T(8,128)(2,1)S(1)}, bf16[384,768]{1,0:T(8,128)(2,1)S(1)}, u32[]{:S(2)}, u32[]{:S(2)}) collective-permute-start(bf16[384,768]{1,0:T(8,128)(2,1)S(1)} %get-tuple-element.34.refs_1_.refs_3_), channel_id=1, source_target_pairs={{0,30},{2,0},{4,2},{6,4},{8,6},{10,8},{12,10},{14,12},{16,14},{18,... | collective-permute-start | bytes 1769480 | tf_op jit(solution)/shard_map/ppermute | solution.py:524
  11.8 18.8 %collective-permute-start.2 = (bf16[384,768]{1,0:T(8,128)(2,1)S(1)}, bf16[384,768]{1,0:T(8,128)(2,1)S(1)}, u32[]{:S(2)}, u32[]{:S(2)}) collective-permute-start(bf16[384,768]{1,0:T(8,128)(2,1)S(1)} %get-tuple-element.35.refs_2_.refs_4_), channel_id=1, source_target_pairs={{0,30},{2,0},{4,2},{6,4},{8,6},{10,8},{12,10},{14,12},{16,14},{18,... | collective-permute-start | bytes 1769480 | tf_op jit(solution)/shard_map/ppermute | solution.py:524
  33.4 44.3 %collective-permute-start.8 = (bf16[1024,768]{1,0:T(8,128)(2,1)S(1)}, bf16[1024,768]{1,0:T(8,128)(2,1)S(1)}, u32[]{:S(2)}, u32[]{:S(2)}) collective-permute-start(bf16[1024,768]{1,0:T(8,128)(2,1)S(1)} %get-tuple-element.50), channel_id=1, source_target_pairs={{0,1},{1,0},{2,3},{3,2},{4,5},{5,4},{6,7},{7,6},{8,9},{9,8},{10,11... | collective-permute-start | bytes 4718600 | tf_op jit(solution)/shard_map/ppermute | solution.py:530
  45.2 17.1 %collective-permute-start.5 = (bf16[384,768]{1,0:T(8,128)(2,1)S(1)}, bf16[384,768]{1,0:T(8,128)(2,1)S(1)}, u32[]{:S(2)}, u32[]{:S(2)}) collective-permute-start(bf16[384,768]{1,0:T(8,128)(2,1)S(1)} %get-tuple-element.41.refs_0_.refs_1_), channel_id=1, source_target_pairs={{0,30},{2,0},{4,2},{6,4},{8,6},{10,8},{12,10},{14,12},{16,14},{18,... | collective-permute-start | bytes 1769480 | tf_op jit(solution)/shard_map/ppermute | solution.py:524
  48.1 14.2 %collective-permute-start.6 = (bf16[384,768]{1,0:T(8,128)(2,1)S(1)}, bf16[384,768]{1,0:T(8,128)(2,1)S(1)}, u32[]{:S(2)}, u32[]{:S(2)}) collective-permute-start(bf16[384,768]{1,0:T(8,128)(2,1)S(1)} %get-tuple-element.42.refs_1_.refs_2_), channel_id=1, source_target_pairs={{0,30},{2,0},{4,2},{6,4},{8,6},{10,8},{12,10},{14,12},{16,14},{18,... | collective-permute-start | bytes 1769480 | tf_op jit(solution)/shard_map/ppermute | solution.py:524
  50.4 17.8 %collective-permute-start.7 = (bf16[384,768]{1,0:T(8,128)(2,1)S(1)}, bf16[384,768]{1,0:T(8,128)(2,1)S(1)}, u32[]{:S(2)}, u32[]{:S(2)}) collective-permute-start(bf16[384,768]{1,0:T(8,128)(2,1)S(1)} %get-tuple-element.43.refs_2_.refs_3_), channel_id=1, source_target_pairs={{0,30},{2,0},{4,2},{6,4},{8,6},{10,8},{12,10},{14,12},{16,14},{18,... | collective-permute-start | bytes 1769480 | tf_op jit(solution)/shard_map/ppermute | solution.py:524
  50.4 30.8 %collective-permute-start.9 = (bf16[128,768]{1,0:T(8,128)(2,1)S(1)}, bf16[128,768]{1,0:T(8,128)(2,1)S(1)}, u32[]{:S(2)}, u32[]{:S(2)}) collective-permute-start(bf16[128,768]{1,0:T(8,128)(2,1)S(1)} %get-tuple-element.52), channel_id=1, source_target_pairs={{0,1},{1,0},{2,3},{3,2},{4,5},{5,4},{6,7},{7,6},{8,9},{9,8},{10,11... | collective-permute-start | bytes 589832 | tf_op jit(solution)/shard_map/ppermute | solution.py:530

commit v3 on v2

--- a/solution.py
+++ b/solution.py
@@ -23,7 +23,7 @@
 BAND = 16
 LONG = 10**11
 MEDIUM = 15 * 10**9
-CHUNK = 64
+HALF = 32
 EARLY_ROWS = 128
 LATE_ROWS = 128
 
@@ -143,7 +143,7 @@
         copies.append(
             pltpu.make_async_copy(v.at[pl.ds(first + r, ROWS)], field.at[pl.ds(r, ROWS)], sems.at[n])
         )
-        copies[n].start()
+        copies[n].start(priority=n % 2)
 
     def lay(row, value):
         for n, piece in enumerate(pieces):
@@ -487,23 +487,24 @@
     wide = [jnp.concatenate([x] * (modes_k // 128), axis=1) for x in (c0, c1, c2)]
 
     def copy_out(n):
-        at = pl.ds(pl.multiple_of(n * CHUNK, CHUNK), CHUNK)
+        at = pl.ds(pl.multiple_of(n * HALF, HALF), HALF)
         return pltpu.make_async_copy(held.at[at], out.at[at], sems.at[n])
 
     def step(first, n):
-        for r in range(0, CHUNK, BAND):
-            row, shift = first + r, pl.multiple_of(n * CHUNK, CHUNK)
-            value = wide[0] * read(u0, row, shift) + wide[1] * read([u1], row, shift)
-            write([held], row, shift, value + wide[2] * read(u2, row, shift))
-        copy_out(n + first // CHUNK).start()
+        for half in range(2):
+            for r in range(0, HALF, BAND):
+                row, shift = first + half * HALF + r, pl.multiple_of(n * 2 * HALF, 2 * HALF)
+                value = wide[0] * read(u0, row, shift) + wide[1] * read([u1], row, shift)
+                write([held], row, shift, value + wide[2] * read(u2, row, shift))
+            copy_out(2 * n + half + first // HALF).start(priority=half)
 
     starts = sorted({*starts_of(u0), *starts_of(u2)})
     for first, end in zip(starts, starts[1:] + [total]):
-        pl.loop(0, (end - first) // CHUNK)(functools.partial(step, first))
+        pl.loop(0, (end - first) // (2 * HALF))(functools.partial(step, first))
     n0, s = jnp.sqrt(g00), jnp.sqrt(q)
     for n, value in enumerate((n0, h11, s / n0, w0 / (s * n0), h22, jnp.sqrt(square))):
         hess[n] = value[0, 0]
-    pl.loop(0, total // CHUNK)(lambda n: copy_out(n).wait())
+    pl.loop(0, total // HALF)(lambda n: copy_out(n).wait())
 
 
 def combine(cells, grams, u0, u1, u2):
@@ -515,7 +516,7 @@
         [IN_VMEM] * len(args),
         [jax.ShapeDtypeStruct(u1.shape, F32), jax.ShapeDtypeStruct((6,), F32)],
         out_specs=[IN_HBM, IN_SMEM],
-        scratch=[pltpu.VMEM(u1.shape, F32), pltpu.SemaphoreType.DMA((u1.shape[0] // CHUNK,))],
+        scratch=[pltpu.VMEM(u1.shape, F32), pltpu.SemaphoreType.DMA((u1.shape[0] // HALF,))],
     )
 
 

time: 97.4 us -> 97.6 us (level)
  no operation moved by 1% of the time
where the time goes in v3:
time: 97.6 us; the launch traced here: 97.4 us
  Pallas kernels  40 us (41%)
  waiting for transfers between devices  26.1 us (27%)
  starting transfers between devices  16.8 us (17%)
  blocking collectives  13.1 us (13%)
  between operations  1.38 us (1%)
    pallas_call x10, Pallas kernels, kernel_call(): pl.pallas_call(body, out_shape=outs, in_specs=in_specs, scratch_shapes=li...  40 us
    ppermute x4, waiting for transfers between devices, neighbour_planes(): return [lax.ppermute(value, axis, [(0, 1), (1, 0)])]  16.7 us
    all_to_all x1, blocking collectives, on_device(): grams = lax.all_to_all(gram, ('seg', 'rad'), 0, 0)  13.1 us
    ppermute x6, starting transfers between devices, shifted(): lax.ppermute(value, axis, [(i, (i + steps) % count) for i in range(count)])  10.4 us
    ppermute x6, waiting for transfers between devices, shifted(): lax.ppermute(value, axis, [(i, (i + steps) % count) for i in range(count)])  9.36 us
    ppermute x4, starting transfers between devices, neighbour_planes(): return [lax.ppermute(value, axis, [(0, 1), (1, 0)])]  6.46 us
  transfers between devices with their start and end apart: 10, of which 5 were waited for; matrix products, arithmetic and copies ran while one was open for 0% of the time, Pallas kernels for 37%

profile of v3, /device:TPU:0, one launch (start us, length us, event | category | flops | bytes accessed | tf_op | source)
XLA Modules:
  0.0 97.4 jit_solution(13635764339072828128)
XLA Ops:
  0.6 1.0 %take_rows.2 = (f32[128,768]{1,0:T(8,128)S(1)}, bf16[128,768]{1,0:T(8,128)(2,1)S(1)}) custom-call(f32[1152,768]{1,0:T(8,128)} %bitcast.11), custom_call_target="tpu_custom_call" | custom-call | flops 1000 | bytes 1000 | tf_op jit(solution)/shard_map/take_rows/pallas_call | solution.py:41
  1.7 3.0 %collective-permute-start.3 = (bf16[128,768]{1,0:T(8,128)(2,1)S(1)}, bf16[128,768]{1,0:T(8,128)(2,1)S(1)}, u32[]{:S(2)}, u32[]{:S(2)}) collective-permute-start(bf16[128,768]{1,0:T(8,128)(2,1)S(1)} %get-tuple-element.31.refs_0_), channel_id=1, source_target_pairs={{0,1},{1,0},{2,3},{3,2},{4,5},{5,4},{6,7},{7,6},{8,9},{9,8},{10,11... | collective-permute-start | bytes 589832 | tf_op jit(solution)/shard_map/ppermute | solution.py:531
  4.7 1.9 %take_rows.3 = (f32[1024,768]{1,0:T(8,128)S(1)}, bf16[1024,768]{1,0:T(8,128)(2,1)S(1)}, bf16[384,768]{1,0:T(8,128)(2,1)S(1)}, bf16[384,768]{1,0:T(8,128)(2,1)S(1)}, bf16[384,768]{1,0:T(8,128)(2,1)S(1)}) custom-call(f32[1152,768]{1,0:T(8,128)} %bitcast.12, bf16[128,768]{1,0:T(8,128)(2,1)S(1)} %get-tuple-element.31.refs_0_), custom_call_target="tpu_custom_call" | custom-call | flops 1000 | bytes 1000 | tf_op jit(solution)/shard_map/take_rows/pallas_call | solution.py:41
  6.6 0.1 collective-permute-start.4
  6.7 3.9 %collective-permute-start = (bf16[384,768]{1,0:T(8,128)(2,1)S(1)}, bf16[384,768]{1,0:T(8,128)(2,1)S(1)}, u32[]{:S(2)}, u32[]{:S(2)}) collective-permute-start(bf16[384,768]{1,0:T(8,128)(2,1)S(1)} %get-tuple-element.33.refs_0_.refs_2_), channel_id=1, source_target_pairs={{0,30},{2,0},{4,2},{6,4},{8,6},{10,8},{12,10},{14,12},{16,14},{18,... | collective-permute-start | bytes 1769480 | tf_op jit(solution)/shard_map/ppermute | solution.py:525
  10.6 1.2 %collective-permute-start.1 = (bf16[384,768]{1,0:T(8,128)(2,1)S(1)}, bf16[384,768]{1,0:T(8,128)(2,1)S(1)}, u32[]{:S(2)}, u32[]{:S(2)}) collective-permute-start(bf16[384,768]{1,0:T(8,128)(2,1)S(1)} %get-tuple-element.34.refs_1_.refs_3_), channel_id=1, source_target_pairs={{0,30},{2,0},{4,2},{6,4},{8,6},{10,8},{12,10},{14,12},{16,14},{18,... | collective-permute-start | bytes 1769480 | tf_op jit(solution)/shard_map/ppermute | solution.py:525
  11.8 0.0 collective-permute-start.2
  12.5 0.0 collective-permute-done.3.refs_3_.refs_0_
  12.5 14.5 %transform.2 = (bf16[3,384,768]{2,1,0:T(8,128)(2,1)S(1)}, bf16[768,768]{1,0:T(8,128)(2,1)}, bf16[384,384]{1,0:T(8,128)(2,1)}, bf16[768,768]{1,0:T(8,128)(2,1)}, bf16[384,384]{1,0:T(8,128)(2,1)S(1)}) custom-call(bf16[384,768]{1,0:T(8,128)(2,1)S(1)} %get-tuple-element.33.refs_0_.refs_2_, bf16[384,768]{1,0:T(8,128)(2,1)S(1)} %get-tuple-element.34.refs_1_.refs_3_, ...), custom_call_target="tpu_custom_call" | custom-call | flops 15000000512 | bytes 1000 | tf_op jit(solution)/shard_map/transform/pallas_call | solution.py:41
  27.1 0.0 collective-permute-done.refs_5_
  27.1 0.0 collective-permute-done.1.refs_6_
  27.1 3.5 %collective-permute-done.2.refs_7_ = bf16[384,768]{1,0:T(8,128)(2,1)S(1)} collective-permute-done((bf16[384,768]{1,0:T(8,128)(2,1)S(1)}, bf16[384,768]{1,0:T(8,128)(2,1)S(1)}, u32[]{:S(2)}, u32[]{:S(2)}) %collective-permute-start.2) | collective-permute-done | bytes 589856 | tf_op jit(solution)/shard_map/ppermute | solution.py:525
  30.6 2.8 %local_first.1 = (f32[1152,768]{1,0:T(8,128)S(1)}, bf16[1024,768]{1,0:T(8,128)(2,1)S(1)}, bf16[128,768]{1,0:T(8,128)(2,1)S(1)}) custom-call(f32[1]{0:T(128)S(6)} %copy.8.advect, f32[128,768]{1,0:T(8,128)S(1)} %get-tuple-element.30.refs_0_.refs_9_, f32[1024,768]{1,0:T(8,128)S(1)} %get-tuple-element.32.refs_1_.refs_10_, ...), custom_call_target="tpu_custom_call" | custom-call | flops 1000 | bytes 1000 | tf_op jit(solution)/shard_map/local_first/pallas_call | solution.py:41
  33.4 1.6 %collective-permute-start.8 = (bf16[1024,768]{1,0:T(8,128)(2,1)S(1)}, bf16[1024,768]{1,0:T(8,128)(2,1)S(1)}, u32[]{:S(2)}, u32[]{:S(2)}) collective-permute-start(bf16[1024,768]{1,0:T(8,128)(2,1)S(1)} %get-tuple-element.50), channel_id=1, source_target_pairs={{0,1},{1,0},{2,3},{3,2},{4,5},{5,4},{6,7},{7,6},{8,9},{9,8},{10,11... | collective-permute-start | bytes 4718600 | tf_op jit(solution)/shard_map/ppermute | solution.py:531
  35.0 9.0 %collective-permute-done.4.refs_1_ = bf16[1024,768]{1,0:T(8,128)(2,1)S(1)} collective-permute-done((bf16[1024,768]{1,0:T(8,128)(2,1)S(1)}, bf16[1024,768]{1,0:T(8,128)(2,1)S(1)}, u32[]{:S(2)}, u32[]{:S(2)}) %collective-permute-start.4) | collective-permute-done | bytes 1572896 | tf_op jit(solution)/shard_map/ppermute | solution.py:531
  44.0 1.2 %first_image.1 = (f32[1152,768]{1,0:T(8,128)S(1)}, bf16[384,768]{1,0:T(8,128)(2,1)S(1)}, bf16[384,768]{1,0:T(8,128)(2,1)S(1)}, bf16[384,768]{1,0:T(8,128)(2,1)S(1)}) custom-call(f32[1152,768]{1,0:T(8,128)S(1)} %get-tuple-element.38.part, bf16[128,768]{1,0:T(8,128)(2,1)S(1)} %collective-permute-done.3.refs_3_.refs_0_, ...), custom_call_target="tpu_custom_call" | custom-call | flops 99999997952 | bytes 1000 | tf_op jit(solution)/shard_map/first_image/pallas_call | solution.py:41
  45.2 2.9 %collective-permute-start.5 = (bf16[384,768]{1,0:T(8,128)(2,1)S(1)}, bf16[384,768]{1,0:T(8,128)(2,1)S(1)}, u32[]{:S(2)}, u32[]{:S(2)}) collective-permute-start(bf16[384,768]{1,0:T(8,128)(2,1)S(1)} %get-tuple-element.41.refs_0_.refs_1_), channel_id=1, source_target_pairs={{0,30},{2,0},{4,2},{6,4},{8,6},{10,8},{12,10},{14,12},{16,14},{18,... | collective-permute-start | bytes 1769480 | tf_op jit(solution)/shard_map/ppermute | solution.py:525
  48.1 2.2 %collective-permute-start.6 = (bf16[384,768]{1,0:T(8,128)(2,1)S(1)}, bf16[384,768]{1,0:T(8,128)(2,1)S(1)}, u32[]{:S(2)}, u32[]{:S(2)}) collective-permute-start(bf16[384,768]{1,0:T(8,128)(2,1)S(1)} %get-tuple-element.42.refs_1_.refs_2_), channel_id=1, source_target_pairs={{0,30},{2,0},{4,2},{6,4},{8,6},{10,8},{12,10},{14,12},{16,14},{18,... | collective-permute-start | bytes 1769480 | tf_op jit(solution)/shard_map/ppermute | solution.py:525
  50.4 0.1 collective-permute-start.7
  50.4 1.8 %collective-permute-start.9 = (bf16[128,768]{1,0:T(8,128)(2,1)S(1)}, bf16[128,768]{1,0:T(8,128)(2,1)S(1)}, u32[]{:S(2)}, u32[]{:S(2)}) collective-permute-start(bf16[128,768]{1,0:T(8,128)(2,1)S(1)} %get-tuple-element.52), channel_id=1, source_target_pairs={{0,1},{1,0},{2,3},{3,2},{4,5},{5,4},{6,7},{7,6},{8,9},{9,8},{10,11... | collective-permute-start | bytes 589832 | tf_op jit(solution)/shard_map/ppermute | solution.py:531
  52.2 10.2 %transform.3.refs_7_ = bf16[3,384,768]{2,1,0:T(8,128)(2,1)S(1)} custom-call(bf16[384,768]{1,0:T(8,128)(2,1)S(1)} %get-tuple-element.41.refs_0_.refs_1_, bf16[384,768]{1,0:T(8,128)(2,1)S(1)} %get-tuple-element.42.refs_1_.refs_2_, bf16[384,768]{1,0:T(8,128)(2,1)S(1)} %get-tuple-element.43.refs_2_.refs_3_, bf16[3,3,384,768]{3,2,1,0:T(8,128)(2,1)} %bitcast.14, ...), custom_call_target="tpu_custom_call" | custom-call | flops 1000 | bytes 1000 | tf_op jit(solution)/shard_map/transform/pallas_call | solution.py:41
  62.4 0.0 collective-permute-done.5.refs_4_
  62.4 0.0 collective-permute-done.6.refs_5_
  62.4 5.8 %collective-permute-done.7.refs_6_ = bf16[384,768]{1,0:T(8,128)(2,1)S(1)} collective-permute-done((bf16[384,768]{1,0:T(8,128)(2,1)S(1)}, bf16[384,768]{1,0:T(8,128)(2,1)S(1)}, u32[]{:S(2)}, u32[]{:S(2)}) %collective-permute-start.7) | collective-permute-done | bytes 589856 | tf_op jit(solution)/shard_map/ppermute | solution.py:525
  68.2 3.7 %local_last.1 = (f32[1152,768]{1,0:T(8,128)S(1)}, f32[384,768]{1,0:T(8,128)S(1)}, f32[8,128]{1,0:T(8,128)S(1)}) custom-call(f32[1]{0:T(128)S(6)} %copy.8.advect, f32[1152,768]{1,0:T(8,128)S(1)} %get-tuple-element.40.refs_0_.u1, bf16[384,768]{1,0:T(8,128)(2,1)S(1)} %get-tuple-element.41.refs_0_.refs_1_, ...), custom_call_target="tpu_custom_call" | custom-call | flops 1000 | bytes 1000 | tf_op jit(solution)/shard_map/local_last/pallas_call | solution.py:41
  71.9 5.8 %collective-permute-done.8.refs_2_ = bf16[1024,768]{1,0:T(8,128)(2,1)S(1)} collective-permute-done((bf16[1024,768]{1,0:T(8,128)(2,1)S(1)}, bf16[1024,768]{1,0:T(8,128)(2,1)S(1)}, u32[]{:S(2)}, u32[]{:S(2)}) %collective-permute-start.8) | collective-permute-done | bytes 1572896 | tf_op jit(solution)/shard_map/ppermute | solution.py:531
  77.7 1.6 %second_image.2 = (f32[1024,768]{1,0:T(8,128)S(1)}, f32[8,128]{1,0:T(8,128)S(1)}) custom-call(f32[384,768]{1,0:T(8,128)S(1)} %get-tuple-element.47.scale, f32[1152,768]{1,0:T(8,128)S(1)} %get-tuple-element.40.refs_0_.u1, f32[1152,768]{1,0:T(8,128)S(1)} %get-tuple-element.48.part, f32[8,128]{1,0:T(8,128)S(1)} %get-tuple-element.49.before, ...), custom_call_target="tpu_custom_call" | custom-call | flops 1000 | bytes 1000 | tf_op jit(solution)/shard_map/second_image/pallas_call | solution.py:41
  79.3 2.0 %collective-permute-done.9.refs_2_ = bf16[128,768]{1,0:T(8,128)(2,1)S(1)} collective-permute-done((bf16[128,768]{1,0:T(8,128)(2,1)S(1)}, bf16[128,768]{1,0:T(8,128)(2,1)S(1)}, u32[]{:S(2)}, u32[]{:S(2)}) %collective-permute-start.9) | collective-permute-done | bytes 196640 | tf_op jit(solution)/shard_map/ppermute | solution.py:531
  81.2 0.3 second_image.3
  81.5 13.1 %all_to_all.11 = f32[32,1,128]{2,1,0:T(1,128)S(1)} all-to-all(f32[32,1,128]{2,1,0:T(1,128)S(1)} %bitcast.10), channel_id=1, replica_groups=mesh['seg'=16,'rad'=2] {'seg','rad'}, dimensions={0} | all-to-all | bytes 32768 | tf_op jit(solution)/shard_map/all_to_all | solution.py:572
  94.6 2.8 %combine.1 = (f32[1152,768]{1,0:T(8,128)}, f32[6]{0:T(128)}) custom-call(f32[32,128]{1,0:T(8,128)S(1)} %bitcast.9, f32[1152,768]{1,0:T(8,128)S(1)} %get-tuple-element.40.refs_0_.u1, f32[128,768]{1,0:T(8,128)S(1)} %get-tuple-element.30.refs_0_.refs_9_, f32[1024,768]{1,0:T(8,128)S(1)} %get-tuple-element.32.refs_1_.refs_10_, ...), custom_call_target="tpu_custom_call" | custom-call | flops 1000 | bytes 1000 | tf_op jit(solution)/shard_map/combine/pallas_call | solution.py:41
Async XLA Ops:
  1.7 10.9 %collective-permute-start.3 = (bf16[128,768]{1,0:T(8,128)(2,1)S(1)}, bf16[128,768]{1,0:T(8,128)(2,1)S(1)}, u32[]{:S(2)}, u32[]{:S(2)}) collective-permute-start(bf16[128,768]{1,0:T(8,128)(2,1)S(1)} %get-tuple-element.31.refs_0_), channel_id=1, source_target_pairs={{0,1},{1,0},{2,3},{3,2},{4,5},{5,4},{6,7},{7,6},{8,9},{9,8},{10,11... | collective-permute-start | bytes 589832 | tf_op jit(solution)/shard_map/ppermute | solution.py:531
  6.6 37.4 %collective-permute-start.4 = (bf16[1024,768]{1,0:T(8,128)(2,1)S(1)}, bf16[1024,768]{1,0:T(8,128)(2,1)S(1)}, u32[]{:S(2)}, u32[]{:S(2)}) collective-permute-start(bf16[1024,768]{1,0:T(8,128)(2,1)S(1)} %get-tuple-element.39), channel_id=1, source_target_pairs={{0,1},{1,0},{2,3},{3,2},{4,5},{5,4},{6,7},{7,6},{8,9},{9,8},{10,11... | collective-permute-start | bytes 4718600 | tf_op jit(solution)/shard_map/ppermute | solution.py:531
  6.7 20.4 %collective-permute-start = (bf16[384,768]{1,0:T(8,128)(2,1)S(1)}, bf16[384,768]{1,0:T(8,128)(2,1)S(1)}, u32[]{:S(2)}, u32[]{:S(2)}) collective-permute-start(bf16[384,768]{1,0:T(8,128)(2,1)S(1)} %get-tuple-element.33.refs_0_.refs_2_), channel_id=1, source_target_pairs={{0,30},{2,0},{4,2},{6,4},{8,6},{10,8},{12,10},{14,12},{16,14},{18,... | collective-permute-start | bytes 1769480 | tf_op jit(solution)/shard_map/ppermute | solution.py:525
  10.6 16.5 %collective-permute-start.1 = (bf16[384,768]{1,0:T(8,128)(2,1)S(1)}, bf16[384,768]{1,0:T(8,128)(2,1)S(1)}, u32[]{:S(2)}, u32[]{:S(2)}) collective-permute-start(bf16[384,768]{1,0:T(8,128)(2,1)S(1)} %get-tuple-element.34.refs_1_.refs_3_), channel_id=1, source_target_pairs={{0,30},{2,0},{4,2},{6,4},{8,6},{10,8},{12,10},{14,12},{16,14},{18,... | collective-permute-start | bytes 1769480 | tf_op jit(solution)/shard_map/ppermute | solution.py:525
  11.8 18.8 %collective-permute-start.2 = (bf16[384,768]{1,0:T(8,128)(2,1)S(1)}, bf16[384,768]{1,0:T(8,128)(2,1)S(1)}, u32[]{:S(2)}, u32[]{:S(2)}) collective-permute-start(bf16[384,768]{1,0:T(8,128)(2,1)S(1)} %get-tuple-element.35.refs_2_.refs_4_), channel_id=1, source_target_pairs={{0,30},{2,0},{4,2},{6,4},{8,6},{10,8},{12,10},{14,12},{16,14},{18,... | collective-permute-start | bytes 1769480 | tf_op jit(solution)/shard_map/ppermute | solution.py:525
  33.4 44.3 %collective-permute-start.8 = (bf16[1024,768]{1,0:T(8,128)(2,1)S(1)}, bf16[1024,768]{1,0:T(8,128)(2,1)S(1)}, u32[]{:S(2)}, u32[]{:S(2)}) collective-permute-start(bf16[1024,768]{1,0:T(8,128)(2,1)S(1)} %get-tuple-element.50), channel_id=1, source_target_pairs={{0,1},{1,0},{2,3},{3,2},{4,5},{5,4},{6,7},{7,6},{8,9},{9,8},{10,11... | collective-permute-start | bytes 4718600 | tf_op jit(solution)/shard_map/ppermute | solution.py:531
  45.2 17.1 %collective-permute-start.5 = (bf16[384,768]{1,0:T(8,128)(2,1)S(1)}, bf16[384,768]{1,0:T(8,128)(2,1)S(1)}, u32[]{:S(2)}, u32[]{:S(2)}) collective-permute-start(bf16[384,768]{1,0:T(8,128)(2,1)S(1)} %get-tuple-element.41.refs_0_.refs_1_), channel_id=1, source_target_pairs={{0,30},{2,0},{4,2},{6,4},{8,6},{10,8},{12,10},{14,12},{16,14},{18,... | collective-permute-start | bytes 1769480 | tf_op jit(solution)/shard_map/ppermute | solution.py:525
  48.1 14.2 %collective-permute-start.6 = (bf16[384,768]{1,0:T(8,128)(2,1)S(1)}, bf16[384,768]{1,0:T(8,128)(2,1)S(1)}, u32[]{:S(2)}, u32[]{:S(2)}) collective-permute-start(bf16[384,768]{1,0:T(8,128)(2,1)S(1)} %get-tuple-element.42.refs_1_.refs_2_), channel_id=1, source_target_pairs={{0,30},{2,0},{4,2},{6,4},{8,6},{10,8},{12,10},{14,12},{16,14},{18,... | collective-permute-start | bytes 1769480 | tf_op jit(solution)/shard_map/ppermute | solution.py:525
  50.4 17.8 %collective-permute-start.7 = (bf16[384,768]{1,0:T(8,128)(2,1)S(1)}, bf16[384,768]{1,0:T(8,128)(2,1)S(1)}, u32[]{:S(2)}, u32[]{:S(2)}) collective-permute-start(bf16[384,768]{1,0:T(8,128)(2,1)S(1)} %get-tuple-element.43.refs_2_.refs_3_), channel_id=1, source_target_pairs={{0,30},{2,0},{4,2},{6,4},{8,6},{10,8},{12,10},{14,12},{16,14},{18,... | collective-permute-start | bytes 1769480 | tf_op jit(solution)/shard_map/ppermute | solution.py:525
  50.4 30.8 %collective-permute-start.9 = (bf16[128,768]{1,0:T(8,128)(2,1)S(1)}, bf16[128,768]{1,0:T(8,128)(2,1)S(1)}, u32[]{:S(2)}, u32[]{:S(2)}) collective-permute-start(bf16[128,768]{1,0:T(8,128)(2,1)S(1)} %get-tuple-element.52), channel_id=1, source_target_pairs={{0,1},{1,0},{2,3},{3,2},{4,5},{5,4},{6,7},{7,6},{8,9},{9,8},{10,11... | collective-permute-start | bytes 589832 | tf_op jit(solution)/shard_map/ppermute | solution.py:531

commit v4 on v0

--- a/solution.py
+++ b/solution.py
@@ -25,7 +25,7 @@
 MEDIUM = 15 * 10**9
 CHUNK = 64
 EARLY_ROWS = 128
-LATE_ROWS = 128
+LATE_ROWS = 64
 
 IN_SMEM = pl.BlockSpec(memory_space=pltpu.SMEM)
 IN_VMEM = pl.BlockSpec(memory_space=pltpu.VMEM)
@@ -132,46 +132,35 @@
         body(pl.multiple_of(i * BAND, BAND))
 
 
-def take_kernel(first, v, *refs):
-    take = taker(refs)
-    early = [] if first == 0 else [take()]
-    field, rounded = take(), take()
-    pieces, sems = take(len(refs) - len(early) - 3), take()
-    count = field.shape[0]
+def take_kernel(v, field, late, *refs):
+    pieces, sems = refs[:-1], refs[-1]
+    rows, early = field.shape[0], field.shape[0] - late.shape[0]
     copies = []
-    for n, r in enumerate(range(0, count, ROWS)):
-        copies.append(
-            pltpu.make_async_copy(v.at[pl.ds(first + r, ROWS)], field.at[pl.ds(r, ROWS)], sems.at[n])
-        )
+    for n, r in enumerate(range(0, rows, ROWS)):
+        copies.append(pltpu.make_async_copy(v.at[pl.ds(r, ROWS)], field.at[pl.ds(r, ROWS)], sems.at[n]))
         copies[n].start()
-
-    def lay(row, value):
-        for n, piece in enumerate(pieces):
-            at = row - n * piece.shape[0]
-            if 0 <= at < piece.shape[0]:
-                piece[at : at + ROWS, :] = value
-
-    for r in range(0, first, ROWS):
-        lay(r, early[0][r : r + ROWS, :])
-    for n, r in enumerate(range(0, count, ROWS)):
+    for n, r in enumerate(range(0, rows, ROWS)):
         copies[n].wait()
         value = field[r : r + ROWS, :].astype(BF16)
-        rounded[r : r + ROWS, :] = value
-        lay(first + r, value)
-
-
-def take_rows(v, first, count, early=(), pieces=0):
+        if r >= early:
+            late[r - early : r - early + ROWS, :] = value
+        piece = pieces[r // pieces[0].shape[0]]
+        at = r % piece.shape[0]
+        piece[at : at + ROWS, :] = value
+
+
+def take_start(v, chans):
     rows, modes_k = v.shape
-    shapes = [pltpu.VMEM((count, modes_k), F32), pltpu.VMEM((count, modes_k), BF16)]
-    field, rounded, *by_channel = kernel_call(
-        functools.partial(take_kernel, first),
-        "take_rows",
-        [v, *early],
-        [IN_HBM] + [IN_VMEM] * len(early),
-        shapes + [pltpu.VMEM((rows // max(pieces, 1), modes_k), BF16)] * pieces,
-        scratch=[pltpu.SemaphoreType.DMA((count // ROWS,))],
-    )
-    return field, rounded, by_channel
+    field, late, *pieces = kernel_call(
+        take_kernel,
+        "take_start",
+        [v],
+        [IN_HBM],
+        [pltpu.VMEM(v.shape, F32), pltpu.VMEM((rows - EARLY_ROWS, modes_k), BF16)]
+        + [pltpu.VMEM((rows // chans, modes_k), BF16)] * chans,
+        scratch=[pltpu.SemaphoreType.DMA((rows // ROWS,))],
+    )
+    return field, late, pieces
 
 
 def transform_kernel(build, awaited, *refs):
@@ -542,15 +531,12 @@
     cells = float(devices * start.size)
     paired = lax.axis_size("rad") == 2
 
-    early = EARLY_ROWS
     sizes = (rows - LATE_ROWS, LATE_ROWS) if paired else (modes_m,) * chans
 
-    u0, u0b, near_one, pieces = [], [], [], None
-    for first, size, parts in ((0, early, 0), (early, rows - early, chans)):
-        field, rounded, pieces = take_rows(start, first, size, u0b, parts)
-        u0.append(field)
-        u0b.append(rounded)
-        near_one.append(neighbour_planes(rounded, "rad"))
+    near_one = [neighbour_planes(start[:EARLY_ROWS].astype(BF16), "rad")]
+    field, late, pieces = take_start(start, chans)
+    near_one.append(neighbour_planes(late, "rad"))
+    u0 = [field]
     next_one = [shifted(x, "seg", -1) for x in pieces]
     two, tables = transform(pieces, couple, awaited=near_one[0])
     part, part_b = local_first(advect, u0, pieces, next_one, two, tables, sizes)

time: 97.4 us -> 97.9 us (level)
  local copies, waits for them, and re-layouts: 0 us -> 1.02 us
    slice x0 -> x1, local copies, waits for them, and re-layouts: none -> 1.02 us  [on_device(): near_one = [neighbour_planes(start[:EARLY_ROWS].astype(BF16), 'rad')]]
    pallas_call x10 -> x9, Pallas kernels: 39.9 us -> 39 us  [kernel_call(): pl.pallas_call(body, out_shape=outs, in_specs=in_specs, scratch_shapes=li...]
  transfers between devices with their start and end apart: 10 -> 10, of which waited for: 5 -> 4; matrix products, arithmetic and copies ran while one was open for 0% -> 0% of each run, Pallas kernels for 37% -> 37%
where the time goes in v4:
time: 97.9 us; the launch traced here: 97.7 us
  Pallas kernels  39 us (40%)
  waiting for transfers between devices  26.3 us (27%)
  starting transfers between devices  16.7 us (17%)
  blocking collectives  13.2 us (13%)
  between operations  1.38 us (1%)
  local copies, waits for them, and re-layouts  1.02 us (1%)
    pallas_call x9, Pallas kernels, kernel_call(): pl.pallas_call(body, out_shape=outs, in_specs=in_specs, scratch_shapes=li...  39 us
    ppermute x4, waiting for transfers between devices, neighbour_planes(): return [lax.ppermute(value, axis, [(0, 1), (1, 0)])]  16.8 us
    all_to_all x1, blocking collectives, on_device(): grams = lax.all_to_all(gram, ('rad', 'seg'), 0, 0)  13.2 us
    ppermute x6, starting transfers between devices, shifted(): lax.ppermute(value, axis, [(i, (i + steps) % count) for i in range(count)])  10.1 us
    ppermute x6, waiting for transfers between devices, shifted(): lax.ppermute(value, axis, [(i, (i + steps) % count) for i in range(count)])  9.49 us
    ppermute x4, starting transfers between devices, neighbour_planes(): return [lax.ppermute(value, axis, [(0, 1), (1, 0)])]  6.58 us
  transfers between devices with their start and end apart: 10, of which 4 were waited for; matrix products, arithmetic and copies ran while one was open for 0% of the time, Pallas kernels for 37%

profile of v4, /device:TPU:0, one launch (start us, length us, event | category | flops | bytes accessed | tf_op | source)
XLA Modules:
  0.0 97.7 jit_solution(9719197388534744930)
XLA Ops:
  0.6 1.0 %slice.7 = bf16[128,768]{1,0:T(8,128)(2,1)S(1)} slice(f32[1152,768]{1,0:T(8,128)} %bitcast.13), slice={[0:128], [0:768]} | slice | bytes 393216 | tf_op jit(solution)/shard_map/slice | solution.py:536
  1.7 3.0 %collective-permute-start.3 = (bf16[128,768]{1,0:T(8,128)(2,1)S(1)}, bf16[128,768]{1,0:T(8,128)(2,1)S(1)}, u32[]{:S(2)}, u32[]{:S(2)}) collective-permute-start(bf16[128,768]{1,0:T(8,128)(2,1)S(1)} %slice.7), channel_id=1, source_target_pairs={{0,1},{1,0},{2,3},{3,2},{4,5},{5,4},{6,7},{7,6},{8,9},{9,8},{10,11... | collective-permute-start | bytes 589832 | tf_op jit(solution)/shard_map/ppermute | solution.py:519
  4.7 2.0 %take_start.1 = (f32[1152,768]{1,0:T(8,128)S(1)}, bf16[1024,768]{1,0:T(8,128)(2,1)S(1)}, bf16[384,768]{1,0:T(8,128)(2,1)S(1)}, bf16[384,768]{1,0:T(8,128)(2,1)S(1)}, bf16[384,768]{1,0:T(8,128)(2,1)S(1)}) custom-call(f32[1152,768]{1,0:T(8,128)} %bitcast.14), custom_call_target="tpu_custom_call" | custom-call | flops 1000 | bytes 1000 | tf_op jit(solution)/shard_map/take_start/pallas_call | solution.py:41
  6.7 0.1 collective-permute-start.4
  6.8 3.9 %collective-permute-start = (bf16[384,768]{1,0:T(8,128)(2,1)S(1)}, bf16[384,768]{1,0:T(8,128)(2,1)S(1)}, u32[]{:S(2)}, u32[]{:S(2)}) collective-permute-start(bf16[384,768]{1,0:T(8,128)(2,1)S(1)} %get-tuple-element.29.refs_0_.refs_1_), channel_id=1, source_target_pairs={{0,30},{2,0},{4,2},{6,4},{8,6},{10,8},{12,10},{14,12},{16,14},{18,... | collective-permute-start | bytes 1769480 | tf_op jit(solution)/shard_map/ppermute | solution.py:513
  10.7 1.2 %collective-permute-start.1 = (bf16[384,768]{1,0:T(8,128)(2,1)S(1)}, bf16[384,768]{1,0:T(8,128)(2,1)S(1)}, u32[]{:S(2)}, u32[]{:S(2)}) collective-permute-start(bf16[384,768]{1,0:T(8,128)(2,1)S(1)} %get-tuple-element.30.refs_1_.refs_2_), channel_id=1, source_target_pairs={{0,30},{2,0},{4,2},{6,4},{8,6},{10,8},{12,10},{14,12},{16,14},{18,... | collective-permute-start | bytes 1769480 | tf_op jit(solution)/shard_map/ppermute | solution.py:513
  12.0 0.0 collective-permute-start.2
  12.6 0.0 collective-permute-done.3.refs_3_.refs_0_
  12.7 14.5 %transform.2 = (bf16[3,384,768]{2,1,0:T(8,128)(2,1)S(1)}, bf16[768,768]{1,0:T(8,128)(2,1)}, bf16[384,384]{1,0:T(8,128)(2,1)}, bf16[768,768]{1,0:T(8,128)(2,1)}, bf16[384,384]{1,0:T(8,128)(2,1)S(1)}) custom-call(bf16[384,768]{1,0:T(8,128)(2,1)S(1)} %get-tuple-element.29.refs_0_.refs_1_, bf16[384,768]{1,0:T(8,128)(2,1)S(1)} %get-tuple-element.30.refs_1_.refs_2_, ...), custom_call_target="tpu_custom_call" | custom-call | flops 15000000512 | bytes 1000 | tf_op jit(solution)/shard_map/transform/pallas_call | solution.py:41
  27.2 0.0 collective-permute-done.refs_4_
  27.2 0.0 collective-permute-done.1.refs_5_
  27.2 3.6 %collective-permute-done.2.refs_6_ = bf16[384,768]{1,0:T(8,128)(2,1)S(1)} collective-permute-done((bf16[384,768]{1,0:T(8,128)(2,1)S(1)}, bf16[384,768]{1,0:T(8,128)(2,1)S(1)}, u32[]{:S(2)}, u32[]{:S(2)}) %collective-permute-start.2) | collective-permute-done | bytes 589856 | tf_op jit(solution)/shard_map/ppermute | solution.py:513
  30.8 2.8 %local_first.1 = (f32[1152,768]{1,0:T(8,128)S(1)}, bf16[1088,768]{1,0:T(8,128)(2,1)S(1)}, bf16[64,768]{1,0:T(8,128)(2,1)S(1)}) custom-call(f32[1]{0:T(128)S(6)} %copy.8.advect, f32[1152,768]{1,0:T(8,128)S(1)} %get-tuple-element.28.refs_0_.refs_9_, bf16[384,768]{1,0:T(8,128)(2,1)S(1)} %get-tuple-element.29.refs_0_.refs_1_, ...), custom_call_target="tpu_custom_call" | custom-call | flops 1000 | bytes 1000 | tf_op jit(solution)/shard_map/local_first/pallas_call | solution.py:41
  33.6 1.6 %collective-permute-start.8 = (bf16[1088,768]{1,0:T(8,128)(2,1)S(1)}, bf16[1088,768]{1,0:T(8,128)(2,1)S(1)}, u32[]{:S(2)}, u32[]{:S(2)}) collective-permute-start(bf16[1088,768]{1,0:T(8,128)(2,1)S(1)} %get-tuple-element.46), channel_id=1, source_target_pairs={{0,1},{1,0},{2,3},{3,2},{4,5},{5,4},{6,7},{7,6},{8,9},{9,8},{10,11... | collective-permute-start | bytes 5013512 | tf_op jit(solution)/shard_map/ppermute | solution.py:519
  35.2 9.0 %collective-permute-done.4.refs_1_ = bf16[1024,768]{1,0:T(8,128)(2,1)S(1)} collective-permute-done((bf16[1024,768]{1,0:T(8,128)(2,1)S(1)}, bf16[1024,768]{1,0:T(8,128)(2,1)S(1)}, u32[]{:S(2)}, u32[]{:S(2)}) %collective-permute-start.4) | collective-permute-done | bytes 1572896 | tf_op jit(solution)/shard_map/ppermute | solution.py:519
  44.1 1.2 %first_image.1 = (f32[1152,768]{1,0:T(8,128)S(1)}, bf16[384,768]{1,0:T(8,128)(2,1)S(1)}, bf16[384,768]{1,0:T(8,128)(2,1)S(1)}, bf16[384,768]{1,0:T(8,128)(2,1)S(1)}) custom-call(f32[1152,768]{1,0:T(8,128)S(1)} %get-tuple-element.34.part, bf16[128,768]{1,0:T(8,128)(2,1)S(1)} %collective-permute-done.3.refs_3_.refs_0_, ...), custom_call_target="tpu_custom_call" | custom-call | flops 99999997952 | bytes 1000 | tf_op jit(solution)/shard_map/first_image/pallas_call | solution.py:41
  45.4 2.9 %collective-permute-start.5 = (bf16[384,768]{1,0:T(8,128)(2,1)S(1)}, bf16[384,768]{1,0:T(8,128)(2,1)S(1)}, u32[]{:S(2)}, u32[]{:S(2)}) collective-permute-start(bf16[384,768]{1,0:T(8,128)(2,1)S(1)} %get-tuple-element.37.refs_0_.refs_1_), channel_id=1, source_target_pairs={{0,30},{2,0},{4,2},{6,4},{8,6},{10,8},{12,10},{14,12},{16,14},{18,... | collective-permute-start | bytes 1769480 | tf_op jit(solution)/shard_map/ppermute | solution.py:513
  48.3 2.0 %collective-permute-start.6 = (bf16[384,768]{1,0:T(8,128)(2,1)S(1)}, bf16[384,768]{1,0:T(8,128)(2,1)S(1)}, u32[]{:S(2)}, u32[]{:S(2)}) collective-permute-start(bf16[384,768]{1,0:T(8,128)(2,1)S(1)} %get-tuple-element.38.refs_1_.refs_2_), channel_id=1, source_target_pairs={{0,30},{2,0},{4,2},{6,4},{8,6},{10,8},{12,10},{14,12},{16,14},{18,... | collective-permute-start | bytes 1769480 | tf_op jit(solution)/shard_map/ppermute | solution.py:513
  50.2 0.1 collective-permute-start.7
  50.3 1.9 %collective-permute-start.9 = (bf16[64,768]{1,0:T(8,128)(2,1)S(1)}, bf16[64,768]{1,0:T(8,128)(2,1)S(1)}, u32[]{:S(2)}, u32[]{:S(2)}) collective-permute-start(bf16[64,768]{1,0:T(8,128)(2,1)S(1)} %get-tuple-element.48), channel_id=1, source_target_pairs={{0,1},{1,0},{2,3},{3,2},{4,5},{5,4},{6,7},{7,6},{8,9},{9,8},{10,11... | collective-permute-start | bytes 294920 | tf_op jit(solution)/shard_map/ppermute | solution.py:519
  52.2 10.2 %transform.3.refs_7_ = bf16[3,384,768]{2,1,0:T(8,128)(2,1)S(1)} custom-call(bf16[384,768]{1,0:T(8,128)(2,1)S(1)} %get-tuple-element.37.refs_0_.refs_1_, bf16[384,768]{1,0:T(8,128)(2,1)S(1)} %get-tuple-element.38.refs_1_.refs_2_, bf16[384,768]{1,0:T(8,128)(2,1)S(1)} %get-tuple-element.39.refs_2_.refs_3_, bf16[3,3,384,768]{3,2,1,0:T(8,128)(2,1)} %bitcast.12, ...), custom_call_target="tpu_custom_call" | custom-call | flops 1000 | bytes 1000 | tf_op jit(solution)/shard_map/transform/pallas_call | solution.py:41
  62.4 0.0 collective-permute-done.5.refs_4_
  62.4 0.0 collective-permute-done.6.refs_5_
  62.4 5.9 %collective-permute-done.7.refs_6_ = bf16[384,768]{1,0:T(8,128)(2,1)S(1)} collective-permute-done((bf16[384,768]{1,0:T(8,128)(2,1)S(1)}, bf16[384,768]{1,0:T(8,128)(2,1)S(1)}, u32[]{:S(2)}, u32[]{:S(2)}) %collective-permute-start.7) | collective-permute-done | bytes 589856 | tf_op jit(solution)/shard_map/ppermute | solution.py:513
  68.3 3.8 %local_last.1 = (f32[1152,768]{1,0:T(8,128)S(1)}, f32[384,768]{1,0:T(8,128)S(1)}, f32[8,128]{1,0:T(8,128)S(1)}) custom-call(f32[1]{0:T(128)S(6)} %copy.8.advect, f32[1152,768]{1,0:T(8,128)S(1)} %get-tuple-element.36.refs_0_.u1, bf16[384,768]{1,0:T(8,128)(2,1)S(1)} %get-tuple-element.37.refs_0_.refs_1_, ...), custom_call_target="tpu_custom_call" | custom-call | flops 1000 | bytes 1000 | tf_op jit(solution)/shard_map/local_last/pallas_call | solution.py:41
  72.1 7.9 %collective-permute-done.8.refs_1_ = bf16[1088,768]{1,0:T(8,128)(2,1)S(1)} collective-permute-done((bf16[1088,768]{1,0:T(8,128)(2,1)S(1)}, bf16[1088,768]{1,0:T(8,128)(2,1)S(1)}, u32[]{:S(2)}, u32[]{:S(2)}) %collective-permute-start.8) | collective-permute-done | bytes 1671200 | tf_op jit(solution)/shard_map/ppermute | solution.py:519
  79.9 1.6 %second_image.2 = (f32[1088,768]{1,0:T(8,128)S(1)}, f32[8,128]{1,0:T(8,128)S(1)}) custom-call(f32[384,768]{1,0:T(8,128)S(1)} %get-tuple-element.43.scale, f32[1152,768]{1,0:T(8,128)S(1)} %get-tuple-element.36.refs_0_.u1, f32[1152,768]{1,0:T(8,128)S(1)} %get-tuple-element.44.part, f32[8,128]{1,0:T(8,128)S(1)} %get-tuple-element.45.before, ...), custom_call_target="tpu_custom_call" | custom-call | flops 1000 | bytes 1000 | tf_op jit(solution)/shard_map/second_image/pallas_call | solution.py:41
  81.6 0.0 collective-permute-done.9.refs_1_
  81.6 0.2 second_image.3
  81.8 13.2 %all_to_all.11 = f32[32,1,128]{2,1,0:T(1,128)S(1)} all-to-all(f32[32,1,128]{2,1,0:T(1,128)S(1)} %bitcast.10), channel_id=1, replica_groups=mesh['seg'=16,'rad'=2] {'rad','seg'}, dimensions={0} | all-to-all | bytes 32768 | tf_op jit(solution)/shard_map/all_to_all | solution.py:557
  95.0 2.6 %combine.1 = (f32[1152,768]{1,0:T(8,128)}, f32[6]{0:T(128)}) custom-call(f32[32,128]{1,0:T(8,128)S(1)} %bitcast.9, f32[1152,768]{1,0:T(8,128)S(1)} %get-tuple-element.36.refs_0_.u1, f32[1152,768]{1,0:T(8,128)S(1)} %get-tuple-element.28.refs_0_.refs_9_, f32[1088,768]{1,0:T(8,128)S(1)} %get-tuple-element.50.refs_1_, f32[64,768]{1,0:T(8,128)S(1)} %get-tuple-element.51.refs_2_), custom_call_target="tpu_custom_call" | custom-call | flops 1000 | bytes 1000 | tf_op jit(solution)/shard_map/combine/pallas_call | solution.py:41
Async XLA Ops:
  1.7 11.0 %collective-permute-start.3 = (bf16[128,768]{1,0:T(8,128)(2,1)S(1)}, bf16[128,768]{1,0:T(8,128)(2,1)S(1)}, u32[]{:S(2)}, u32[]{:S(2)}) collective-permute-start(bf16[128,768]{1,0:T(8,128)(2,1)S(1)} %slice.7), channel_id=1, source_target_pairs={{0,1},{1,0},{2,3},{3,2},{4,5},{5,4},{6,7},{7,6},{8,9},{9,8},{10,11... | collective-permute-start | bytes 589832 | tf_op jit(solution)/shard_map/ppermute | solution.py:519
  6.7 37.4 %collective-permute-start.4 = (bf16[1024,768]{1,0:T(8,128)(2,1)S(1)}, bf16[1024,768]{1,0:T(8,128)(2,1)S(1)}, u32[]{:S(2)}, u32[]{:S(2)}) collective-permute-start(bf16[1024,768]{1,0:T(8,128)(2,1)S(1)} %get-tuple-element.35), channel_id=1, source_target_pairs={{0,1},{1,0},{2,3},{3,2},{4,5},{5,4},{6,7},{7,6},{8,9},{9,8},{10,11... | collective-permute-start | bytes 4718600 | tf_op jit(solution)/shard_map/ppermute | solution.py:519
  6.8 20.4 %collective-permute-start = (bf16[384,768]{1,0:T(8,128)(2,1)S(1)}, bf16[384,768]{1,0:T(8,128)(2,1)S(1)}, u32[]{:S(2)}, u32[]{:S(2)}) collective-permute-start(bf16[384,768]{1,0:T(8,128)(2,1)S(1)} %get-tuple-element.29.refs_0_.refs_1_), channel_id=1, source_target_pairs={{0,30},{2,0},{4,2},{6,4},{8,6},{10,8},{12,10},{14,12},{16,14},{18,... | collective-permute-start | bytes 1769480 | tf_op jit(solution)/shard_map/ppermute | solution.py:513
  10.7 16.5 %collective-permute-start.1 = (bf16[384,768]{1,0:T(8,128)(2,1)S(1)}, bf16[384,768]{1,0:T(8,128)(2,1)S(1)}, u32[]{:S(2)}, u32[]{:S(2)}) collective-permute-start(bf16[384,768]{1,0:T(8,128)(2,1)S(1)} %get-tuple-element.30.refs_1_.refs_2_), channel_id=1, source_target_pairs={{0,30},{2,0},{4,2},{6,4},{8,6},{10,8},{12,10},{14,12},{16,14},{18,... | collective-permute-start | bytes 1769480 | tf_op jit(solution)/shard_map/ppermute | solution.py:513
  12.0 18.8 %collective-permute-start.2 = (bf16[384,768]{1,0:T(8,128)(2,1)S(1)}, bf16[384,768]{1,0:T(8,128)(2,1)S(1)}, u32[]{:S(2)}, u32[]{:S(2)}) collective-permute-start(bf16[384,768]{1,0:T(8,128)(2,1)S(1)} %get-tuple-element.31.refs_2_.refs_3_), channel_id=1, source_target_pairs={{0,30},{2,0},{4,2},{6,4},{8,6},{10,8},{12,10},{14,12},{16,14},{18,... | collective-permute-start | bytes 1769480 | tf_op jit(solution)/shard_map/ppermute | solution.py:513
  33.6 46.4 %collective-permute-start.8 = (bf16[1088,768]{1,0:T(8,128)(2,1)S(1)}, bf16[1088,768]{1,0:T(8,128)(2,1)S(1)}, u32[]{:S(2)}, u32[]{:S(2)}) collective-permute-start(bf16[1088,768]{1,0:T(8,128)(2,1)S(1)} %get-tuple-element.46), channel_id=1, source_target_pairs={{0,1},{1,0},{2,3},{3,2},{4,5},{5,4},{6,7},{7,6},{8,9},{9,8},{10,11... | collective-permute-start | bytes 5013512 | tf_op jit(solution)/shard_map/ppermute | solution.py:519
  45.4 17.0 %collective-permute-start.5 = (bf16[384,768]{1,0:T(8,128)(2,1)S(1)}, bf16[384,768]{1,0:T(8,128)(2,1)S(1)}, u32[]{:S(2)}, u32[]{:S(2)}) collective-permute-start(bf16[384,768]{1,0:T(8,128)(2,1)S(1)} %get-tuple-element.37.refs_0_.refs_1_), channel_id=1, source_target_pairs={{0,30},{2,0},{4,2},{6,4},{8,6},{10,8},{12,10},{14,12},{16,14},{18,... | collective-permute-start | bytes 1769480 | tf_op jit(solution)/shard_map/ppermute | solution.py:513
  48.3 14.1 %collective-permute-start.6 = (bf16[384,768]{1,0:T(8,128)(2,1)S(1)}, bf16[384,768]{1,0:T(8,128)(2,1)S(1)}, u32[]{:S(2)}, u32[]{:S(2)}) collective-permute-start(bf16[384,768]{1,0:T(8,128)(2,1)S(1)} %get-tuple-element.38.refs_1_.refs_2_), channel_id=1, source_target_pairs={{0,30},{2,0},{4,2},{6,4},{8,6},{10,8},{12,10},{14,12},{16,14},{18,... | collective-permute-start | bytes 1769480 | tf_op jit(solution)/shard_map/ppermute | solution.py:513
  50.2 18.1 %collective-permute-start.7 = (bf16[384,768]{1,0:T(8,128)(2,1)S(1)}, bf16[384,768]{1,0:T(8,128)(2,1)S(1)}, u32[]{:S(2)}, u32[]{:S(2)}) collective-permute-start(bf16[384,768]{1,0:T(8,128)(2,1)S(1)} %get-tuple-element.39.refs_2_.refs_3_), channel_id=1, source_target_pairs={{0,30},{2,0},{4,2},{6,4},{8,6},{10,8},{12,10},{14,12},{16,14},{18,... | collective-permute-start | bytes 1769480 | tf_op jit(solution)/shard_map/ppermute | solution.py:513
  50.3 31.3 %collective-permute-start.9 = (bf16[64,768]{1,0:T(8,128)(2,1)S(1)}, bf16[64,768]{1,0:T(8,128)(2,1)S(1)}, u32[]{:S(2)}, u32[]{:S(2)}) collective-permute-start(bf16[64,768]{1,0:T(8,128)(2,1)S(1)} %get-tuple-element.48), channel_id=1, source_target_pairs={{0,1},{1,0},{2,3},{3,2},{4,5},{5,4},{6,7},{7,6},{8,9},{9,8},{10,11... | collective-permute-start | bytes 294920 | tf_op jit(solution)/shard_map/ppermute | solution.py:519

commit v5 on v0

--- a/solution.py
+++ b/solution.py
@@ -465,7 +465,7 @@
 def combine_kernel(cells, counts, grams, u1, *refs):
     take = taker(refs)
     u0, u2 = take(counts[0]), take(counts[1])
-    out, hess, held, sems = take(4)
+    out, hess_out, held, hess, sems = take(5)
     total, modes_k = out.shape
     g = jnp.sum(grams[...], axis=0, keepdims=True) * F32(1.0 / cells)
     g = jnp.sum(jnp.where(on_diagonal(), g, F32(0.0)), axis=1, keepdims=True)
@@ -503,7 +503,10 @@
     n0, s = jnp.sqrt(g00), jnp.sqrt(q)
     for n, value in enumerate((n0, h11, s / n0, w0 / (s * n0), h22, jnp.sqrt(square))):
         hess[n] = value[0, 0]
+    last = pltpu.make_async_copy(hess, hess_out, sems.at[total // CHUNK])
+    last.start()
     pl.loop(0, total // CHUNK)(lambda n: copy_out(n).wait())
+    last.wait()
 
 
 def combine(cells, grams, u0, u1, u2):
@@ -514,8 +517,12 @@
         args,
         [IN_VMEM] * len(args),
         [jax.ShapeDtypeStruct(u1.shape, F32), jax.ShapeDtypeStruct((6,), F32)],
-        out_specs=[IN_HBM, IN_SMEM],
-        scratch=[pltpu.VMEM(u1.shape, F32), pltpu.SemaphoreType.DMA((u1.shape[0] // CHUNK,))],
+        out_specs=[IN_HBM, IN_HBM],
+        scratch=[
+            pltpu.VMEM(u1.shape, F32),
+            pltpu.SMEM((6,), F32),
+            pltpu.SemaphoreType.DMA((u1.shape[0] // CHUNK + 1,)),
+        ],
     )
 
 

time: 97.4 us -> 96.9 us (level)
  no operation moved by 1% of the time
where the time goes in v5:
time: 96.9 us; the launch traced here: 96.7 us
  Pallas kernels  39.4 us (41%)
  waiting for transfers between devices  26.1 us (27%)
  starting transfers between devices  16.8 us (17%)
  blocking collectives  13 us (13%)
  between operations  1.38 us (1%)
    pallas_call x10, Pallas kernels, kernel_call(): pl.pallas_call(body, out_shape=outs, in_specs=in_specs, scratch_shapes=li...  39.4 us
    ppermute x4, waiting for transfers between devices, neighbour_planes(): return [lax.ppermute(value, axis, [(0, 1), (1, 0)])]  16.7 us
    all_to_all x1, blocking collectives, on_device(): grams = lax.all_to_all(gram, ('rad', 'seg'), 0, 0)  13 us
    ppermute x6, starting transfers between devices, shifted(): lax.ppermute(value, axis, [(i, (i + steps) % count) for i in range(count)])  10.4 us
    ppermute x6, waiting for transfers between devices, shifted(): lax.ppermute(value, axis, [(i, (i + steps) % count) for i in range(count)])  9.36 us
    ppermute x4, starting transfers between devices, neighbour_planes(): return [lax.ppermute(value, axis, [(0, 1), (1, 0)])]  6.46 us
  transfers between devices with their start and end apart: 10, of which 5 were waited for; matrix products, arithmetic and copies ran while one was open for 0% of the time, Pallas kernels for 37%

profile of v5, /device:TPU:0, one launch (start us, length us, event | category | flops | bytes accessed | tf_op | source)
XLA Modules:
  0.0 96.7 jit_solution(9353141224435112414)
XLA Ops:
  0.6 1.0 %take_rows.2 = (f32[128,768]{1,0:T(8,128)S(1)}, bf16[128,768]{1,0:T(8,128)(2,1)S(1)}) custom-call(f32[1152,768]{1,0:T(8,128)} %bitcast.11), custom_call_target="tpu_custom_call" | custom-call | flops 1000 | bytes 1000 | tf_op jit(solution)/shard_map/take_rows/pallas_call | solution.py:41
  1.7 3.0 %collective-permute-start.3 = (bf16[128,768]{1,0:T(8,128)(2,1)S(1)}, bf16[128,768]{1,0:T(8,128)(2,1)S(1)}, u32[]{:S(2)}, u32[]{:S(2)}) collective-permute-start(bf16[128,768]{1,0:T(8,128)(2,1)S(1)} %get-tuple-element.31.refs_0_), channel_id=1, source_target_pairs={{0,1},{1,0},{2,3},{3,2},{4,5},{5,4},{6,7},{7,6},{8,9},{9,8},{10,11... | collective-permute-start | bytes 589832 | tf_op jit(solution)/shard_map/ppermute | solution.py:537
  4.7 1.9 %take_rows.3 = (f32[1024,768]{1,0:T(8,128)S(1)}, bf16[1024,768]{1,0:T(8,128)(2,1)S(1)}, bf16[384,768]{1,0:T(8,128)(2,1)S(1)}, bf16[384,768]{1,0:T(8,128)(2,1)S(1)}, bf16[384,768]{1,0:T(8,128)(2,1)S(1)}) custom-call(f32[1152,768]{1,0:T(8,128)} %bitcast.12, bf16[128,768]{1,0:T(8,128)(2,1)S(1)} %get-tuple-element.31.refs_0_), custom_call_target="tpu_custom_call" | custom-call | flops 1000 | bytes 1000 | tf_op jit(solution)/shard_map/take_rows/pallas_call | solution.py:41
  6.6 0.1 collective-permute-start.4
  6.7 3.9 %collective-permute-start = (bf16[384,768]{1,0:T(8,128)(2,1)S(1)}, bf16[384,768]{1,0:T(8,128)(2,1)S(1)}, u32[]{:S(2)}, u32[]{:S(2)}) collective-permute-start(bf16[384,768]{1,0:T(8,128)(2,1)S(1)} %get-tuple-element.33.refs_0_.refs_2_), channel_id=1, source_target_pairs={{0,30},{2,0},{4,2},{6,4},{8,6},{10,8},{12,10},{14,12},{16,14},{18,... | collective-permute-start | bytes 1769480 | tf_op jit(solution)/shard_map/ppermute | solution.py:531
  10.6 1.2 %collective-permute-start.1 = (bf16[384,768]{1,0:T(8,128)(2,1)S(1)}, bf16[384,768]{1,0:T(8,128)(2,1)S(1)}, u32[]{:S(2)}, u32[]{:S(2)}) collective-permute-start(bf16[384,768]{1,0:T(8,128)(2,1)S(1)} %get-tuple-element.34.refs_1_.refs_3_), channel_id=1, source_target_pairs={{0,30},{2,0},{4,2},{6,4},{8,6},{10,8},{12,10},{14,12},{16,14},{18,... | collective-permute-start | bytes 1769480 | tf_op jit(solution)/shard_map/ppermute | solution.py:531
  11.8 0.0 collective-permute-start.2
  12.5 0.0 collective-permute-done.3.refs_3_.refs_0_
  12.5 14.5 %transform.2 = (bf16[3,384,768]{2,1,0:T(8,128)(2,1)S(1)}, bf16[768,768]{1,0:T(8,128)(2,1)}, bf16[384,384]{1,0:T(8,128)(2,1)}, bf16[768,768]{1,0:T(8,128)(2,1)}, bf16[384,384]{1,0:T(8,128)(2,1)S(1)}) custom-call(bf16[384,768]{1,0:T(8,128)(2,1)S(1)} %get-tuple-element.33.refs_0_.refs_2_, bf16[384,768]{1,0:T(8,128)(2,1)S(1)} %get-tuple-element.34.refs_1_.refs_3_, ...), custom_call_target="tpu_custom_call" | custom-call | flops 15000000512 | bytes 1000 | tf_op jit(solution)/shard_map/transform/pallas_call | solution.py:41
  27.1 0.0 collective-permute-done.refs_5_
  27.1 0.0 collective-permute-done.1.refs_6_
  27.1 3.6 %collective-permute-done.2.refs_7_ = bf16[384,768]{1,0:T(8,128)(2,1)S(1)} collective-permute-done((bf16[384,768]{1,0:T(8,128)(2,1)S(1)}, bf16[384,768]{1,0:T(8,128)(2,1)S(1)}, u32[]{:S(2)}, u32[]{:S(2)}) %collective-permute-start.2) | collective-permute-done | bytes 589856 | tf_op jit(solution)/shard_map/ppermute | solution.py:531
  30.6 2.8 %local_first.1 = (f32[1152,768]{1,0:T(8,128)S(1)}, bf16[1024,768]{1,0:T(8,128)(2,1)S(1)}, bf16[128,768]{1,0:T(8,128)(2,1)S(1)}) custom-call(f32[1]{0:T(128)S(6)} %copy.8.advect, f32[128,768]{1,0:T(8,128)S(1)} %get-tuple-element.30.refs_0_.refs_9_, f32[1024,768]{1,0:T(8,128)S(1)} %get-tuple-element.32.refs_1_.refs_10_, ...), custom_call_target="tpu_custom_call" | custom-call | flops 1000 | bytes 1000 | tf_op jit(solution)/shard_map/local_first/pallas_call | solution.py:41
  33.4 1.6 %collective-permute-start.8 = (bf16[1024,768]{1,0:T(8,128)(2,1)S(1)}, bf16[1024,768]{1,0:T(8,128)(2,1)S(1)}, u32[]{:S(2)}, u32[]{:S(2)}) collective-permute-start(bf16[1024,768]{1,0:T(8,128)(2,1)S(1)} %get-tuple-element.50), channel_id=1, source_target_pairs={{0,1},{1,0},{2,3},{3,2},{4,5},{5,4},{6,7},{7,6},{8,9},{9,8},{10,11... | collective-permute-start | bytes 4718600 | tf_op jit(solution)/shard_map/ppermute | solution.py:537
  35.0 9.0 %collective-permute-done.4.refs_1_ = bf16[1024,768]{1,0:T(8,128)(2,1)S(1)} collective-permute-done((bf16[1024,768]{1,0:T(8,128)(2,1)S(1)}, bf16[1024,768]{1,0:T(8,128)(2,1)S(1)}, u32[]{:S(2)}, u32[]{:S(2)}) %collective-permute-start.4) | collective-permute-done | bytes 1572896 | tf_op jit(solution)/shard_map/ppermute | solution.py:537
  44.0 1.2 %first_image.1 = (f32[1152,768]{1,0:T(8,128)S(1)}, bf16[384,768]{1,0:T(8,128)(2,1)S(1)}, bf16[384,768]{1,0:T(8,128)(2,1)S(1)}, bf16[384,768]{1,0:T(8,128)(2,1)S(1)}) custom-call(f32[1152,768]{1,0:T(8,128)S(1)} %get-tuple-element.38.part, bf16[128,768]{1,0:T(8,128)(2,1)S(1)} %collective-permute-done.3.refs_3_.refs_0_, ...), custom_call_target="tpu_custom_call" | custom-call | flops 99999997952 | bytes 1000 | tf_op jit(solution)/shard_map/first_image/pallas_call | solution.py:41
  45.2 2.9 %collective-permute-start.5 = (bf16[384,768]{1,0:T(8,128)(2,1)S(1)}, bf16[384,768]{1,0:T(8,128)(2,1)S(1)}, u32[]{:S(2)}, u32[]{:S(2)}) collective-permute-start(bf16[384,768]{1,0:T(8,128)(2,1)S(1)} %get-tuple-element.41.refs_0_.refs_1_), channel_id=1, source_target_pairs={{0,30},{2,0},{4,2},{6,4},{8,6},{10,8},{12,10},{14,12},{16,14},{18,... | collective-permute-start | bytes 1769480 | tf_op jit(solution)/shard_map/ppermute | solution.py:531
  48.1 2.2 %collective-permute-start.6 = (bf16[384,768]{1,0:T(8,128)(2,1)S(1)}, bf16[384,768]{1,0:T(8,128)(2,1)S(1)}, u32[]{:S(2)}, u32[]{:S(2)}) collective-permute-start(bf16[384,768]{1,0:T(8,128)(2,1)S(1)} %get-tuple-element.42.refs_1_.refs_2_), channel_id=1, source_target_pairs={{0,30},{2,0},{4,2},{6,4},{8,6},{10,8},{12,10},{14,12},{16,14},{18,... | collective-permute-start | bytes 1769480 | tf_op jit(solution)/shard_map/ppermute | solution.py:531
  50.4 0.1 collective-permute-start.7
  50.4 1.8 %collective-permute-start.9 = (bf16[128,768]{1,0:T(8,128)(2,1)S(1)}, bf16[128,768]{1,0:T(8,128)(2,1)S(1)}, u32[]{:S(2)}, u32[]{:S(2)}) collective-permute-start(bf16[128,768]{1,0:T(8,128)(2,1)S(1)} %get-tuple-element.52), channel_id=1, source_target_pairs={{0,1},{1,0},{2,3},{3,2},{4,5},{5,4},{6,7},{7,6},{8,9},{9,8},{10,11... | collective-permute-start | bytes 589832 | tf_op jit(solution)/shard_map/ppermute | solution.py:537
  52.2 10.2 %transform.3.refs_7_ = bf16[3,384,768]{2,1,0:T(8,128)(2,1)S(1)} custom-call(bf16[384,768]{1,0:T(8,128)(2,1)S(1)} %get-tuple-element.41.refs_0_.refs_1_, bf16[384,768]{1,0:T(8,128)(2,1)S(1)} %get-tuple-element.42.refs_1_.refs_2_, bf16[384,768]{1,0:T(8,128)(2,1)S(1)} %get-tuple-element.43.refs_2_.refs_3_, bf16[3,3,384,768]{3,2,1,0:T(8,128)(2,1)} %bitcast.14, ...), custom_call_target="tpu_custom_call" | custom-call | flops 1000 | bytes 1000 | tf_op jit(solution)/shard_map/transform/pallas_call | solution.py:41
  62.4 0.0 collective-permute-done.5.refs_4_
  62.4 0.0 collective-permute-done.6.refs_5_
  62.4 5.8 %collective-permute-done.7.refs_6_ = bf16[384,768]{1,0:T(8,128)(2,1)S(1)} collective-permute-done((bf16[384,768]{1,0:T(8,128)(2,1)S(1)}, bf16[384,768]{1,0:T(8,128)(2,1)S(1)}, u32[]{:S(2)}, u32[]{:S(2)}) %collective-permute-start.7) | collective-permute-done | bytes 589856 | tf_op jit(solution)/shard_map/ppermute | solution.py:531
  68.2 3.7 %local_last.1 = (f32[1152,768]{1,0:T(8,128)S(1)}, f32[384,768]{1,0:T(8,128)S(1)}, f32[8,128]{1,0:T(8,128)S(1)}) custom-call(f32[1]{0:T(128)S(6)} %copy.8.advect, f32[1152,768]{1,0:T(8,128)S(1)} %get-tuple-element.40.refs_0_.u1, bf16[384,768]{1,0:T(8,128)(2,1)S(1)} %get-tuple-element.41.refs_0_.refs_1_, ...), custom_call_target="tpu_custom_call" | custom-call | flops 1000 | bytes 1000 | tf_op jit(solution)/shard_map/local_last/pallas_call | solution.py:41
  71.9 5.8 %collective-permute-done.8.refs_2_ = bf16[1024,768]{1,0:T(8,128)(2,1)S(1)} collective-permute-done((bf16[1024,768]{1,0:T(8,128)(2,1)S(1)}, bf16[1024,768]{1,0:T(8,128)(2,1)S(1)}, u32[]{:S(2)}, u32[]{:S(2)}) %collective-permute-start.8) | collective-permute-done | bytes 1572896 | tf_op jit(solution)/shard_map/ppermute | solution.py:537
  77.7 1.6 %second_image.2 = (f32[1024,768]{1,0:T(8,128)S(1)}, f32[8,128]{1,0:T(8,128)S(1)}) custom-call(f32[384,768]{1,0:T(8,128)S(1)} %get-tuple-element.47.scale, f32[1152,768]{1,0:T(8,128)S(1)} %get-tuple-element.40.refs_0_.u1, f32[1152,768]{1,0:T(8,128)S(1)} %get-tuple-element.48.part, f32[8,128]{1,0:T(8,128)S(1)} %get-tuple-element.49.before, ...), custom_call_target="tpu_custom_call" | custom-call | flops 1000 | bytes 1000 | tf_op jit(solution)/shard_map/second_image/pallas_call | solution.py:41
  79.3 2.0 %collective-permute-done.9.refs_2_ = bf16[128,768]{1,0:T(8,128)(2,1)S(1)} collective-permute-done((bf16[128,768]{1,0:T(8,128)(2,1)S(1)}, bf16[128,768]{1,0:T(8,128)(2,1)S(1)}, u32[]{:S(2)}, u32[]{:S(2)}) %collective-permute-start.9) | collective-permute-done | bytes 196640 | tf_op jit(solution)/shard_map/ppermute | solution.py:537
  81.2 0.3 second_image.3
  81.5 13.0 %all_to_all.11 = f32[32,1,128]{2,1,0:T(1,128)S(1)} all-to-all(f32[32,1,128]{2,1,0:T(1,128)S(1)} %bitcast.10), channel_id=1, replica_groups=mesh['seg'=16,'rad'=2] {'rad','seg'}, dimensions={0} | all-to-all | bytes 32768 | tf_op jit(solution)/shard_map/all_to_all | solution.py:578
  94.5 2.1 %combine.1 = (f32[1152,768]{1,0:T(8,128)}, f32[6]{0:T(128)}) custom-call(f32[32,128]{1,0:T(8,128)S(1)} %bitcast.9, f32[1152,768]{1,0:T(8,128)S(1)} %get-tuple-element.40.refs_0_.u1, f32[128,768]{1,0:T(8,128)S(1)} %get-tuple-element.30.refs_0_.refs_9_, f32[1024,768]{1,0:T(8,128)S(1)} %get-tuple-element.32.refs_1_.refs_10_, ...), custom_call_target="tpu_custom_call" | custom-call | flops 1000 | bytes 1000 | tf_op jit(solution)/shard_map/combine/pallas_call | solution.py:41
Async XLA Ops:
  1.7 10.9 %collective-permute-start.3 = (bf16[128,768]{1,0:T(8,128)(2,1)S(1)}, bf16[128,768]{1,0:T(8,128)(2,1)S(1)}, u32[]{:S(2)}, u32[]{:S(2)}) collective-permute-start(bf16[128,768]{1,0:T(8,128)(2,1)S(1)} %get-tuple-element.31.refs_0_), channel_id=1, source_target_pairs={{0,1},{1,0},{2,3},{3,2},{4,5},{5,4},{6,7},{7,6},{8,9},{9,8},{10,11... | collective-permute-start | bytes 589832 | tf_op jit(solution)/shard_map/ppermute | solution.py:537
  6.6 37.4 %collective-permute-start.4 = (bf16[1024,768]{1,0:T(8,128)(2,1)S(1)}, bf16[1024,768]{1,0:T(8,128)(2,1)S(1)}, u32[]{:S(2)}, u32[]{:S(2)}) collective-permute-start(bf16[1024,768]{1,0:T(8,128)(2,1)S(1)} %get-tuple-element.39), channel_id=1, source_target_pairs={{0,1},{1,0},{2,3},{3,2},{4,5},{5,4},{6,7},{7,6},{8,9},{9,8},{10,11... | collective-permute-start | bytes 4718600 | tf_op jit(solution)/shard_map/ppermute | solution.py:537
  6.7 20.4 %collective-permute-start = (bf16[384,768]{1,0:T(8,128)(2,1)S(1)}, bf16[384,768]{1,0:T(8,128)(2,1)S(1)}, u32[]{:S(2)}, u32[]{:S(2)}) collective-permute-start(bf16[384,768]{1,0:T(8,128)(2,1)S(1)} %get-tuple-element.33.refs_0_.refs_2_), channel_id=1, source_target_pairs={{0,30},{2,0},{4,2},{6,4},{8,6},{10,8},{12,10},{14,12},{16,14},{18,... | collective-permute-start | bytes 1769480 | tf_op jit(solution)/shard_map/ppermute | solution.py:531
  10.6 16.5 %collective-permute-start.1 = (bf16[384,768]{1,0:T(8,128)(2,1)S(1)}, bf16[384,768]{1,0:T(8,128)(2,1)S(1)}, u32[]{:S(2)}, u32[]{:S(2)}) collective-permute-start(bf16[384,768]{1,0:T(8,128)(2,1)S(1)} %get-tuple-element.34.refs_1_.refs_3_), channel_id=1, source_target_pairs={{0,30},{2,0},{4,2},{6,4},{8,6},{10,8},{12,10},{14,12},{16,14},{18,... | collective-permute-start | bytes 1769480 | tf_op jit(solution)/shard_map/ppermute | solution.py:531
  11.8 18.8 %collective-permute-start.2 = (bf16[384,768]{1,0:T(8,128)(2,1)S(1)}, bf16[384,768]{1,0:T(8,128)(2,1)S(1)}, u32[]{:S(2)}, u32[]{:S(2)}) collective-permute-start(bf16[384,768]{1,0:T(8,128)(2,1)S(1)} %get-tuple-element.35.refs_2_.refs_4_), channel_id=1, source_target_pairs={{0,30},{2,0},{4,2},{6,4},{8,6},{10,8},{12,10},{14,12},{16,14},{18,... | collective-permute-start | bytes 1769480 | tf_op jit(solution)/shard_map/ppermute | solution.py:531
  33.4 44.3 %collective-permute-start.8 = (bf16[1024,768]{1,0:T(8,128)(2,1)S(1)}, bf16[1024,768]{1,0:T(8,128)(2,1)S(1)}, u32[]{:S(2)}, u32[]{:S(2)}) collective-permute-start(bf16[1024,768]{1,0:T(8,128)(2,1)S(1)} %get-tuple-element.50), channel_id=1, source_target_pairs={{0,1},{1,0},{2,3},{3,2},{4,5},{5,4},{6,7},{7,6},{8,9},{9,8},{10,11... | collective-permute-start | bytes 4718600 | tf_op jit(solution)/shard_map/ppermute | solution.py:537
  45.2 17.1 %collective-permute-start.5 = (bf16[384,768]{1,0:T(8,128)(2,1)S(1)}, bf16[384,768]{1,0:T(8,128)(2,1)S(1)}, u32[]{:S(2)}, u32[]{:S(2)}) collective-permute-start(bf16[384,768]{1,0:T(8,128)(2,1)S(1)} %get-tuple-element.41.refs_0_.refs_1_), channel_id=1, source_target_pairs={{0,30},{2,0},{4,2},{6,4},{8,6},{10,8},{12,10},{14,12},{16,14},{18,... | collective-permute-start | bytes 1769480 | tf_op jit(solution)/shard_map/ppermute | solution.py:531
  48.1 14.2 %collective-permute-start.6 = (bf16[384,768]{1,0:T(8,128)(2,1)S(1)}, bf16[384,768]{1,0:T(8,128)(2,1)S(1)}, u32[]{:S(2)}, u32[]{:S(2)}) collective-permute-start(bf16[384,768]{1,0:T(8,128)(2,1)S(1)} %get-tuple-element.42.refs_1_.refs_2_), channel_id=1, source_target_pairs={{0,30},{2,0},{4,2},{6,4},{8,6},{10,8},{12,10},{14,12},{16,14},{18,... | collective-permute-start | bytes 1769480 | tf_op jit(solution)/shard_map/ppermute | solution.py:531
  50.4 17.8 %collective-permute-start.7 = (bf16[384,768]{1,0:T(8,128)(2,1)S(1)}, bf16[384,768]{1,0:T(8,128)(2,1)S(1)}, u32[]{:S(2)}, u32[]{:S(2)}) collective-permute-start(bf16[384,768]{1,0:T(8,128)(2,1)S(1)} %get-tuple-element.43.refs_2_.refs_3_), channel_id=1, source_target_pairs={{0,30},{2,0},{4,2},{6,4},{8,6},{10,8},{12,10},{14,12},{16,14},{18,... | collective-permute-start | bytes 1769480 | tf_op jit(solution)/shard_map/ppermute | solution.py:531
  50.4 30.8 %collective-permute-start.9 = (bf16[128,768]{1,0:T(8,128)(2,1)S(1)}, bf16[128,768]{1,0:T(8,128)(2,1)S(1)}, u32[]{:S(2)}, u32[]{:S(2)}) collective-permute-start(bf16[128,768]{1,0:T(8,128)(2,1)S(1)} %get-tuple-element.52), channel_id=1, source_target_pairs={{0,1},{1,0},{2,3},{3,2},{4,5},{5,4},{6,7},{7,6},{8,9},{9,8},{10,11... | collective-permute-start | bytes 589832 | tf_op jit(solution)/shard_map/ppermute | solution.py:537

commit v6 on v5

--- a/solution.py
+++ b/solution.py
@@ -23,7 +23,7 @@
 BAND = 16
 LONG = 10**11
 MEDIUM = 15 * 10**9
-CHUNK = 64
+CHUNK = 32
 EARLY_ROWS = 128
 LATE_ROWS = 128
 
@@ -484,7 +484,7 @@
     c2 = F32(1.0) / jnp.sqrt(q * square)
     c1 = -(h11 + h22) * c2
     c0 = (h11 * h22 - ratio) * c2
-    wide = [jnp.concatenate([x] * (modes_k // 128), axis=1) for x in (c0, c1, c2)]
+    c0, c1, c2 = (x[0, 0] for x in (c0, c1, c2))
 
     def copy_out(n):
         at = pl.ds(pl.multiple_of(n * CHUNK, CHUNK), CHUNK)
@@ -493,8 +493,8 @@
     def step(first, n):
         for r in range(0, CHUNK, BAND):
             row, shift = first + r, pl.multiple_of(n * CHUNK, CHUNK)
-            value = wide[0] * read(u0, row, shift) + wide[1] * read([u1], row, shift)
-            write([held], row, shift, value + wide[2] * read(u2, row, shift))
+            value = c0 * read(u0, row, shift) + c1 * read([u1], row, shift)
+            write([held], row, shift, value + c2 * read(u2, row, shift))
         copy_out(n + first // CHUNK).start()
 
     starts = sorted({*starts_of(u0), *starts_of(u2)})

time: 96.9 us -> 97 us (level)
  no operation moved by 1% of the time
where the time goes in v6:
time: 97 us; the launch traced here: 96.8 us
  Pallas kernels  39.5 us (41%)
  waiting for transfers between devices  26.1 us (27%)
  starting transfers between devices  16.8 us (17%)
  blocking collectives  13 us (13%)
  between operations  1.38 us (1%)
    pallas_call x10, Pallas kernels, kernel_call(): pl.pallas_call(body, out_shape=outs, in_specs=in_specs, scratch_shapes=li...  39.5 us
    ppermute x4, waiting for transfers between devices, neighbour_planes(): return [lax.ppermute(value, axis, [(0, 1), (1, 0)])]  16.7 us
    all_to_all x1, blocking collectives, on_device(): grams = lax.all_to_all(gram, ('rad', 'seg'), 0, 0)  13 us
    ppermute x6, starting transfers between devices, shifted(): lax.ppermute(value, axis, [(i, (i + steps) % count) for i in range(count)])  10.4 us
    ppermute x6, waiting for transfers between devices, shifted(): lax.ppermute(value, axis, [(i, (i + steps) % count) for i in range(count)])  9.36 us
    ppermute x4, starting transfers between devices, neighbour_planes(): return [lax.ppermute(value, axis, [(0, 1), (1, 0)])]  6.46 us
  transfers between devices with their start and end apart: 10, of which 5 were waited for; matrix products, arithmetic and copies ran while one was open for 0% of the time, Pallas kernels for 37%

profile of v6, /device:TPU:0, one launch (start us, length us, event | category | flops | bytes accessed | tf_op | source)
XLA Modules:
  0.0 96.8 jit_solution(39820313142830727)
XLA Ops:
  0.6 1.0 %take_rows.2 = (f32[128,768]{1,0:T(8,128)S(1)}, bf16[128,768]{1,0:T(8,128)(2,1)S(1)}) custom-call(f32[1152,768]{1,0:T(8,128)} %bitcast.11), custom_call_target="tpu_custom_call" | custom-call | flops 1000 | bytes 1000 | tf_op jit(solution)/shard_map/take_rows/pallas_call | solution.py:41
  1.7 3.0 %collective-permute-start.3 = (bf16[128,768]{1,0:T(8,128)(2,1)S(1)}, bf16[128,768]{1,0:T(8,128)(2,1)S(1)}, u32[]{:S(2)}, u32[]{:S(2)}) collective-permute-start(bf16[128,768]{1,0:T(8,128)(2,1)S(1)} %get-tuple-element.31.refs_0_), channel_id=1, source_target_pairs={{0,1},{1,0},{2,3},{3,2},{4,5},{5,4},{6,7},{7,6},{8,9},{9,8},{10,11... | collective-permute-start | bytes 589832 | tf_op jit(solution)/shard_map/ppermute | solution.py:537
  4.7 1.9 %take_rows.3 = (f32[1024,768]{1,0:T(8,128)S(1)}, bf16[1024,768]{1,0:T(8,128)(2,1)S(1)}, bf16[384,768]{1,0:T(8,128)(2,1)S(1)}, bf16[384,768]{1,0:T(8,128)(2,1)S(1)}, bf16[384,768]{1,0:T(8,128)(2,1)S(1)}) custom-call(f32[1152,768]{1,0:T(8,128)} %bitcast.12, bf16[128,768]{1,0:T(8,128)(2,1)S(1)} %get-tuple-element.31.refs_0_), custom_call_target="tpu_custom_call" | custom-call | flops 1000 | bytes 1000 | tf_op jit(solution)/shard_map/take_rows/pallas_call | solution.py:41
  6.6 0.1 collective-permute-start.4
  6.7 3.9 %collective-permute-start = (bf16[384,768]{1,0:T(8,128)(2,1)S(1)}, bf16[384,768]{1,0:T(8,128)(2,1)S(1)}, u32[]{:S(2)}, u32[]{:S(2)}) collective-permute-start(bf16[384,768]{1,0:T(8,128)(2,1)S(1)} %get-tuple-element.33.refs_0_.refs_2_), channel_id=1, source_target_pairs={{0,30},{2,0},{4,2},{6,4},{8,6},{10,8},{12,10},{14,12},{16,14},{18,... | collective-permute-start | bytes 1769480 | tf_op jit(solution)/shard_map/ppermute | solution.py:531
  10.6 1.2 %collective-permute-start.1 = (bf16[384,768]{1,0:T(8,128)(2,1)S(1)}, bf16[384,768]{1,0:T(8,128)(2,1)S(1)}, u32[]{:S(2)}, u32[]{:S(2)}) collective-permute-start(bf16[384,768]{1,0:T(8,128)(2,1)S(1)} %get-tuple-element.34.refs_1_.refs_3_), channel_id=1, source_target_pairs={{0,30},{2,0},{4,2},{6,4},{8,6},{10,8},{12,10},{14,12},{16,14},{18,... | collective-permute-start | bytes 1769480 | tf_op jit(solution)/shard_map/ppermute | solution.py:531
  11.8 0.0 collective-permute-start.2
  12.5 0.0 collective-permute-done.3.refs_3_.refs_0_
  12.5 14.5 %transform.2 = (bf16[3,384,768]{2,1,0:T(8,128)(2,1)S(1)}, bf16[768,768]{1,0:T(8,128)(2,1)}, bf16[384,384]{1,0:T(8,128)(2,1)}, bf16[768,768]{1,0:T(8,128)(2,1)}, bf16[384,384]{1,0:T(8,128)(2,1)S(1)}) custom-call(bf16[384,768]{1,0:T(8,128)(2,1)S(1)} %get-tuple-element.33.refs_0_.refs_2_, bf16[384,768]{1,0:T(8,128)(2,1)S(1)} %get-tuple-element.34.refs_1_.refs_3_, ...), custom_call_target="tpu_custom_call" | custom-call | flops 15000000512 | bytes 1000 | tf_op jit(solution)/shard_map/transform/pallas_call | solution.py:41
  27.1 0.0 collective-permute-done.refs_5_
  27.1 0.0 collective-permute-done.1.refs_6_
  27.1 3.6 %collective-permute-done.2.refs_7_ = bf16[384,768]{1,0:T(8,128)(2,1)S(1)} collective-permute-done((bf16[384,768]{1,0:T(8,128)(2,1)S(1)}, bf16[384,768]{1,0:T(8,128)(2,1)S(1)}, u32[]{:S(2)}, u32[]{:S(2)}) %collective-permute-start.2) | collective-permute-done | bytes 589856 | tf_op jit(solution)/shard_map/ppermute | solution.py:531
  30.6 2.8 %local_first.1 = (f32[1152,768]{1,0:T(8,128)S(1)}, bf16[1024,768]{1,0:T(8,128)(2,1)S(1)}, bf16[128,768]{1,0:T(8,128)(2,1)S(1)}) custom-call(f32[1]{0:T(128)S(6)} %copy.8.advect, f32[128,768]{1,0:T(8,128)S(1)} %get-tuple-element.30.refs_0_.refs_9_, f32[1024,768]{1,0:T(8,128)S(1)} %get-tuple-element.32.refs_1_.refs_10_, ...), custom_call_target="tpu_custom_call" | custom-call | flops 1000 | bytes 1000 | tf_op jit(solution)/shard_map/local_first/pallas_call | solution.py:41
  33.4 1.6 %collective-permute-start.8 = (bf16[1024,768]{1,0:T(8,128)(2,1)S(1)}, bf16[1024,768]{1,0:T(8,128)(2,1)S(1)}, u32[]{:S(2)}, u32[]{:S(2)}) collective-permute-start(bf16[1024,768]{1,0:T(8,128)(2,1)S(1)} %get-tuple-element.50), channel_id=1, source_target_pairs={{0,1},{1,0},{2,3},{3,2},{4,5},{5,4},{6,7},{7,6},{8,9},{9,8},{10,11... | collective-permute-start | bytes 4718600 | tf_op jit(solution)/shard_map/ppermute | solution.py:537
  35.0 9.0 %collective-permute-done.4.refs_1_ = bf16[1024,768]{1,0:T(8,128)(2,1)S(1)} collective-permute-done((bf16[1024,768]{1,0:T(8,128)(2,1)S(1)}, bf16[1024,768]{1,0:T(8,128)(2,1)S(1)}, u32[]{:S(2)}, u32[]{:S(2)}) %collective-permute-start.4) | collective-permute-done | bytes 1572896 | tf_op jit(solution)/shard_map/ppermute | solution.py:537
  44.0 1.2 %first_image.1 = (f32[1152,768]{1,0:T(8,128)S(1)}, bf16[384,768]{1,0:T(8,128)(2,1)S(1)}, bf16[384,768]{1,0:T(8,128)(2,1)S(1)}, bf16[384,768]{1,0:T(8,128)(2,1)S(1)}) custom-call(f32[1152,768]{1,0:T(8,128)S(1)} %get-tuple-element.38.part, bf16[128,768]{1,0:T(8,128)(2,1)S(1)} %collective-permute-done.3.refs_3_.refs_0_, ...), custom_call_target="tpu_custom_call" | custom-call | flops 99999997952 | bytes 1000 | tf_op jit(solution)/shard_map/first_image/pallas_call | solution.py:41
  45.2 2.9 %collective-permute-start.5 = (bf16[384,768]{1,0:T(8,128)(2,1)S(1)}, bf16[384,768]{1,0:T(8,128)(2,1)S(1)}, u32[]{:S(2)}, u32[]{:S(2)}) collective-permute-start(bf16[384,768]{1,0:T(8,128)(2,1)S(1)} %get-tuple-element.41.refs_0_.refs_1_), channel_id=1, source_target_pairs={{0,30},{2,0},{4,2},{6,4},{8,6},{10,8},{12,10},{14,12},{16,14},{18,... | collective-permute-start | bytes 1769480 | tf_op jit(solution)/shard_map/ppermute | solution.py:531
  48.1 2.2 %collective-permute-start.6 = (bf16[384,768]{1,0:T(8,128)(2,1)S(1)}, bf16[384,768]{1,0:T(8,128)(2,1)S(1)}, u32[]{:S(2)}, u32[]{:S(2)}) collective-permute-start(bf16[384,768]{1,0:T(8,128)(2,1)S(1)} %get-tuple-element.42.refs_1_.refs_2_), channel_id=1, source_target_pairs={{0,30},{2,0},{4,2},{6,4},{8,6},{10,8},{12,10},{14,12},{16,14},{18,... | collective-permute-start | bytes 1769480 | tf_op jit(solution)/shard_map/ppermute | solution.py:531
  50.4 0.1 collective-permute-start.7
  50.4 1.8 %collective-permute-start.9 = (bf16[128,768]{1,0:T(8,128)(2,1)S(1)}, bf16[128,768]{1,0:T(8,128)(2,1)S(1)}, u32[]{:S(2)}, u32[]{:S(2)}) collective-permute-start(bf16[128,768]{1,0:T(8,128)(2,1)S(1)} %get-tuple-element.52), channel_id=1, source_target_pairs={{0,1},{1,0},{2,3},{3,2},{4,5},{5,4},{6,7},{7,6},{8,9},{9,8},{10,11... | collective-permute-start | bytes 589832 | tf_op jit(solution)/shard_map/ppermute | solution.py:537
  52.2 10.2 %transform.3.refs_7_ = bf16[3,384,768]{2,1,0:T(8,128)(2,1)S(1)} custom-call(bf16[384,768]{1,0:T(8,128)(2,1)S(1)} %get-tuple-element.41.refs_0_.refs_1_, bf16[384,768]{1,0:T(8,128)(2,1)S(1)} %get-tuple-element.42.refs_1_.refs_2_, bf16[384,768]{1,0:T(8,128)(2,1)S(1)} %get-tuple-element.43.refs_2_.refs_3_, bf16[3,3,384,768]{3,2,1,0:T(8,128)(2,1)} %bitcast.14, ...), custom_call_target="tpu_custom_call" | custom-call | flops 1000 | bytes 1000 | tf_op jit(solution)/shard_map/transform/pallas_call | solution.py:41
  62.4 0.0 collective-permute-done.5.refs_4_
  62.4 0.0 collective-permute-done.6.refs_5_
  62.4 5.8 %collective-permute-done.7.refs_6_ = bf16[384,768]{1,0:T(8,128)(2,1)S(1)} collective-permute-done((bf16[384,768]{1,0:T(8,128)(2,1)S(1)}, bf16[384,768]{1,0:T(8,128)(2,1)S(1)}, u32[]{:S(2)}, u32[]{:S(2)}) %collective-permute-start.7) | collective-permute-done | bytes 589856 | tf_op jit(solution)/shard_map/ppermute | solution.py:531
  68.2 3.7 %local_last.1 = (f32[1152,768]{1,0:T(8,128)S(1)}, f32[384,768]{1,0:T(8,128)S(1)}, f32[8,128]{1,0:T(8,128)S(1)}) custom-call(f32[1]{0:T(128)S(6)} %copy.8.advect, f32[1152,768]{1,0:T(8,128)S(1)} %get-tuple-element.40.refs_0_.u1, bf16[384,768]{1,0:T(8,128)(2,1)S(1)} %get-tuple-element.41.refs_0_.refs_1_, ...), custom_call_target="tpu_custom_call" | custom-call | flops 1000 | bytes 1000 | tf_op jit(solution)/shard_map/local_last/pallas_call | solution.py:41
  71.9 5.8 %collective-permute-done.8.refs_2_ = bf16[1024,768]{1,0:T(8,128)(2,1)S(1)} collective-permute-done((bf16[1024,768]{1,0:T(8,128)(2,1)S(1)}, bf16[1024,768]{1,0:T(8,128)(2,1)S(1)}, u32[]{:S(2)}, u32[]{:S(2)}) %collective-permute-start.8) | collective-permute-done | bytes 1572896 | tf_op jit(solution)/shard_map/ppermute | solution.py:537
  77.7 1.6 %second_image.2 = (f32[1024,768]{1,0:T(8,128)S(1)}, f32[8,128]{1,0:T(8,128)S(1)}) custom-call(f32[384,768]{1,0:T(8,128)S(1)} %get-tuple-element.47.scale, f32[1152,768]{1,0:T(8,128)S(1)} %get-tuple-element.40.refs_0_.u1, f32[1152,768]{1,0:T(8,128)S(1)} %get-tuple-element.48.part, f32[8,128]{1,0:T(8,128)S(1)} %get-tuple-element.49.before, ...), custom_call_target="tpu_custom_call" | custom-call | flops 1000 | bytes 1000 | tf_op jit(solution)/shard_map/second_image/pallas_call | solution.py:41
  79.3 2.0 %collective-permute-done.9.refs_2_ = bf16[128,768]{1,0:T(8,128)(2,1)S(1)} collective-permute-done((bf16[128,768]{1,0:T(8,128)(2,1)S(1)}, bf16[128,768]{1,0:T(8,128)(2,1)S(1)}, u32[]{:S(2)}, u32[]{:S(2)}) %collective-permute-start.9) | collective-permute-done | bytes 196640 | tf_op jit(solution)/shard_map/ppermute | solution.py:537
  81.2 0.3 second_image.3
  81.5 13.0 %all_to_all.11 = f32[32,1,128]{2,1,0:T(1,128)S(1)} all-to-all(f32[32,1,128]{2,1,0:T(1,128)S(1)} %bitcast.10), channel_id=1, replica_groups=mesh['seg'=16,'rad'=2] {'rad','seg'}, dimensions={0} | all-to-all | bytes 32768 | tf_op jit(solution)/shard_map/all_to_all | solution.py:578
  94.5 2.3 %combine.1 = (f32[1152,768]{1,0:T(8,128)}, f32[6]{0:T(128)}) custom-call(f32[32,128]{1,0:T(8,128)S(1)} %bitcast.9, f32[1152,768]{1,0:T(8,128)S(1)} %get-tuple-element.40.refs_0_.u1, f32[128,768]{1,0:T(8,128)S(1)} %get-tuple-element.30.refs_0_.refs_9_, f32[1024,768]{1,0:T(8,128)S(1)} %get-tuple-element.32.refs_1_.refs_10_, ...), custom_call_target="tpu_custom_call" | custom-call | flops 1000 | bytes 1000 | tf_op jit(solution)/shard_map/combine/pallas_call | solution.py:41
Async XLA Ops:
  1.7 10.9 %collective-permute-start.3 = (bf16[128,768]{1,0:T(8,128)(2,1)S(1)}, bf16[128,768]{1,0:T(8,128)(2,1)S(1)}, u32[]{:S(2)}, u32[]{:S(2)}) collective-permute-start(bf16[128,768]{1,0:T(8,128)(2,1)S(1)} %get-tuple-element.31.refs_0_), channel_id=1, source_target_pairs={{0,1},{1,0},{2,3},{3,2},{4,5},{5,4},{6,7},{7,6},{8,9},{9,8},{10,11... | collective-permute-start | bytes 589832 | tf_op jit(solution)/shard_map/ppermute | solution.py:537
  6.6 37.4 %collective-permute-start.4 = (bf16[1024,768]{1,0:T(8,128)(2,1)S(1)}, bf16[1024,768]{1,0:T(8,128)(2,1)S(1)}, u32[]{:S(2)}, u32[]{:S(2)}) collective-permute-start(bf16[1024,768]{1,0:T(8,128)(2,1)S(1)} %get-tuple-element.39), channel_id=1, source_target_pairs={{0,1},{1,0},{2,3},{3,2},{4,5},{5,4},{6,7},{7,6},{8,9},{9,8},{10,11... | collective-permute-start | bytes 4718600 | tf_op jit(solution)/shard_map/ppermute | solution.py:537
  6.7 20.4 %collective-permute-start = (bf16[384,768]{1,0:T(8,128)(2,1)S(1)}, bf16[384,768]{1,0:T(8,128)(2,1)S(1)}, u32[]{:S(2)}, u32[]{:S(2)}) collective-permute-start(bf16[384,768]{1,0:T(8,128)(2,1)S(1)} %get-tuple-element.33.refs_0_.refs_2_), channel_id=1, source_target_pairs={{0,30},{2,0},{4,2},{6,4},{8,6},{10,8},{12,10},{14,12},{16,14},{18,... | collective-permute-start | bytes 1769480 | tf_op jit(solution)/shard_map/ppermute | solution.py:531
  10.6 16.5 %collective-permute-start.1 = (bf16[384,768]{1,0:T(8,128)(2,1)S(1)}, bf16[384,768]{1,0:T(8,128)(2,1)S(1)}, u32[]{:S(2)}, u32[]{:S(2)}) collective-permute-start(bf16[384,768]{1,0:T(8,128)(2,1)S(1)} %get-tuple-element.34.refs_1_.refs_3_), channel_id=1, source_target_pairs={{0,30},{2,0},{4,2},{6,4},{8,6},{10,8},{12,10},{14,12},{16,14},{18,... | collective-permute-start | bytes 1769480 | tf_op jit(solution)/shard_map/ppermute | solution.py:531
  11.8 18.8 %collective-permute-start.2 = (bf16[384,768]{1,0:T(8,128)(2,1)S(1)}, bf16[384,768]{1,0:T(8,128)(2,1)S(1)}, u32[]{:S(2)}, u32[]{:S(2)}) collective-permute-start(bf16[384,768]{1,0:T(8,128)(2,1)S(1)} %get-tuple-element.35.refs_2_.refs_4_), channel_id=1, source_target_pairs={{0,30},{2,0},{4,2},{6,4},{8,6},{10,8},{12,10},{14,12},{16,14},{18,... | collective-permute-start | bytes 1769480 | tf_op jit(solution)/shard_map/ppermute | solution.py:531
  33.4 44.3 %collective-permute-start.8 = (bf16[1024,768]{1,0:T(8,128)(2,1)S(1)}, bf16[1024,768]{1,0:T(8,128)(2,1)S(1)}, u32[]{:S(2)}, u32[]{:S(2)}) collective-permute-start(bf16[1024,768]{1,0:T(8,128)(2,1)S(1)} %get-tuple-element.50), channel_id=1, source_target_pairs={{0,1},{1,0},{2,3},{3,2},{4,5},{5,4},{6,7},{7,6},{8,9},{9,8},{10,11... | collective-permute-start | bytes 4718600 | tf_op jit(solution)/shard_map/ppermute | solution.py:537
  45.2 17.1 %collective-permute-start.5 = (bf16[384,768]{1,0:T(8,128)(2,1)S(1)}, bf16[384,768]{1,0:T(8,128)(2,1)S(1)}, u32[]{:S(2)}, u32[]{:S(2)}) collective-permute-start(bf16[384,768]{1,0:T(8,128)(2,1)S(1)} %get-tuple-element.41.refs_0_.refs_1_), channel_id=1, source_target_pairs={{0,30},{2,0},{4,2},{6,4},{8,6},{10,8},{12,10},{14,12},{16,14},{18,... | collective-permute-start | bytes 1769480 | tf_op jit(solution)/shard_map/ppermute | solution.py:531
  48.1 14.2 %collective-permute-start.6 = (bf16[384,768]{1,0:T(8,128)(2,1)S(1)}, bf16[384,768]{1,0:T(8,128)(2,1)S(1)}, u32[]{:S(2)}, u32[]{:S(2)}) collective-permute-start(bf16[384,768]{1,0:T(8,128)(2,1)S(1)} %get-tuple-element.42.refs_1_.refs_2_), channel_id=1, source_target_pairs={{0,30},{2,0},{4,2},{6,4},{8,6},{10,8},{12,10},{14,12},{16,14},{18,... | collective-permute-start | bytes 1769480 | tf_op jit(solution)/shard_map/ppermute | solution.py:531
  50.4 17.8 %collective-permute-start.7 = (bf16[384,768]{1,0:T(8,128)(2,1)S(1)}, bf16[384,768]{1,0:T(8,128)(2,1)S(1)}, u32[]{:S(2)}, u32[]{:S(2)}) collective-permute-start(bf16[384,768]{1,0:T(8,128)(2,1)S(1)} %get-tuple-element.43.refs_2_.refs_3_), channel_id=1, source_target_pairs={{0,30},{2,0},{4,2},{6,4},{8,6},{10,8},{12,10},{14,12},{16,14},{18,... | collective-permute-start | bytes 1769480 | tf_op jit(solution)/shard_map/ppermute | solution.py:531
  50.4 30.8 %collective-permute-start.9 = (bf16[128,768]{1,0:T(8,128)(2,1)S(1)}, bf16[128,768]{1,0:T(8,128)(2,1)S(1)}, u32[]{:S(2)}, u32[]{:S(2)}) collective-permute-start(bf16[128,768]{1,0:T(8,128)(2,1)S(1)} %get-tuple-element.52), channel_id=1, source_target_pairs={{0,1},{1,0},{2,3},{3,2},{4,5},{5,4},{6,7},{7,6},{8,9},{9,8},{10,11... | collective-permute-start | bytes 589832 | tf_op jit(solution)/shard_map/ppermute | solution.py:537

commit v7 on v6

--- a/solution.py
+++ b/solution.py
@@ -23,7 +23,7 @@
 BAND = 16
 LONG = 10**11
 MEDIUM = 15 * 10**9
-CHUNK = 32
+CHUNK = 128
 EARLY_ROWS = 128
 LATE_ROWS = 128
 

time: 97 us -> 96.8 us (level)
  no operation moved by 1% of the time
where the time goes in v7:
time: 96.8 us; the launch traced here: 96.6 us
  Pallas kernels  39.3 us (41%)
  waiting for transfers between devices  26.1 us (27%)
  starting transfers between devices  16.8 us (17%)
  blocking collectives  13 us (13%)
  between operations  1.38 us (1%)
    pallas_call x10, Pallas kernels, kernel_call(): pl.pallas_call(body, out_shape=outs, in_specs=in_specs, scratch_shapes=li...  39.3 us
    ppermute x4, waiting for transfers between devices, neighbour_planes(): return [lax.ppermute(value, axis, [(0, 1), (1, 0)])]  16.7 us
    all_to_all x1, blocking collectives, on_device(): grams = lax.all_to_all(gram, ('rad', 'seg'), 0, 0)  13 us
    ppermute x6, starting transfers between devices, shifted(): lax.ppermute(value, axis, [(i, (i + steps) % count) for i in range(count)])  10.4 us
    ppermute x6, waiting for transfers between devices, shifted(): lax.ppermute(value, axis, [(i, (i + steps) % count) for i in range(count)])  9.36 us
    ppermute x4, starting transfers between devices, neighbour_planes(): return [lax.ppermute(value, axis, [(0, 1), (1, 0)])]  6.46 us
  transfers between devices with their start and end apart: 10, of which 5 were waited for; matrix products, arithmetic and copies ran while one was open for 0% of the time, Pallas kernels for 37%

profile of v7, /device:TPU:0, one launch (start us, length us, event | category | flops | bytes accessed | tf_op | source)
XLA Modules:
  0.0 96.6 jit_solution(15009200747615480068)
XLA Ops:
  0.6 1.0 %take_rows.2 = (f32[128,768]{1,0:T(8,128)S(1)}, bf16[128,768]{1,0:T(8,128)(2,1)S(1)}) custom-call(f32[1152,768]{1,0:T(8,128)} %bitcast.11), custom_call_target="tpu_custom_call" | custom-call | flops 1000 | bytes 1000 | tf_op jit(solution)/shard_map/take_rows/pallas_call | solution.py:41
  1.7 3.0 %collective-permute-start.3 = (bf16[128,768]{1,0:T(8,128)(2,1)S(1)}, bf16[128,768]{1,0:T(8,128)(2,1)S(1)}, u32[]{:S(2)}, u32[]{:S(2)}) collective-permute-start(bf16[128,768]{1,0:T(8,128)(2,1)S(1)} %get-tuple-element.31.refs_0_), channel_id=1, source_target_pairs={{0,1},{1,0},{2,3},{3,2},{4,5},{5,4},{6,7},{7,6},{8,9},{9,8},{10,11... | collective-permute-start | bytes 589832 | tf_op jit(solution)/shard_map/ppermute | solution.py:537
  4.7 1.9 %take_rows.3 = (f32[1024,768]{1,0:T(8,128)S(1)}, bf16[1024,768]{1,0:T(8,128)(2,1)S(1)}, bf16[384,768]{1,0:T(8,128)(2,1)S(1)}, bf16[384,768]{1,0:T(8,128)(2,1)S(1)}, bf16[384,768]{1,0:T(8,128)(2,1)S(1)}) custom-call(f32[1152,768]{1,0:T(8,128)} %bitcast.12, bf16[128,768]{1,0:T(8,128)(2,1)S(1)} %get-tuple-element.31.refs_0_), custom_call_target="tpu_custom_call" | custom-call | flops 1000 | bytes 1000 | tf_op jit(solution)/shard_map/take_rows/pallas_call | solution.py:41
  6.6 0.1 collective-permute-start.4
  6.7 3.9 %collective-permute-start = (bf16[384,768]{1,0:T(8,128)(2,1)S(1)}, bf16[384,768]{1,0:T(8,128)(2,1)S(1)}, u32[]{:S(2)}, u32[]{:S(2)}) collective-permute-start(bf16[384,768]{1,0:T(8,128)(2,1)S(1)} %get-tuple-element.33.refs_0_.refs_2_), channel_id=1, source_target_pairs={{0,30},{2,0},{4,2},{6,4},{8,6},{10,8},{12,10},{14,12},{16,14},{18,... | collective-permute-start | bytes 1769480 | tf_op jit(solution)/shard_map/ppermute | solution.py:531
  10.6 1.2 %collective-permute-start.1 = (bf16[384,768]{1,0:T(8,128)(2,1)S(1)}, bf16[384,768]{1,0:T(8,128)(2,1)S(1)}, u32[]{:S(2)}, u32[]{:S(2)}) collective-permute-start(bf16[384,768]{1,0:T(8,128)(2,1)S(1)} %get-tuple-element.34.refs_1_.refs_3_), channel_id=1, source_target_pairs={{0,30},{2,0},{4,2},{6,4},{8,6},{10,8},{12,10},{14,12},{16,14},{18,... | collective-permute-start | bytes 1769480 | tf_op jit(solution)/shard_map/ppermute | solution.py:531
  11.8 0.0 collective-permute-start.2
  12.5 0.0 collective-permute-done.3.refs_3_.refs_0_
  12.5 14.5 %transform.2 = (bf16[3,384,768]{2,1,0:T(8,128)(2,1)S(1)}, bf16[768,768]{1,0:T(8,128)(2,1)}, bf16[384,384]{1,0:T(8,128)(2,1)}, bf16[768,768]{1,0:T(8,128)(2,1)}, bf16[384,384]{1,0:T(8,128)(2,1)S(1)}) custom-call(bf16[384,768]{1,0:T(8,128)(2,1)S(1)} %get-tuple-element.33.refs_0_.refs_2_, bf16[384,768]{1,0:T(8,128)(2,1)S(1)} %get-tuple-element.34.refs_1_.refs_3_, ...), custom_call_target="tpu_custom_call" | custom-call | flops 15000000512 | bytes 1000 | tf_op jit(solution)/shard_map/transform/pallas_call | solution.py:41
  27.1 0.0 collective-permute-done.refs_5_
  27.1 0.0 collective-permute-done.1.refs_6_
  27.1 3.6 %collective-permute-done.2.refs_7_ = bf16[384,768]{1,0:T(8,128)(2,1)S(1)} collective-permute-done((bf16[384,768]{1,0:T(8,128)(2,1)S(1)}, bf16[384,768]{1,0:T(8,128)(2,1)S(1)}, u32[]{:S(2)}, u32[]{:S(2)}) %collective-permute-start.2) | collective-permute-done | bytes 589856 | tf_op jit(solution)/shard_map/ppermute | solution.py:531
  30.6 2.8 %local_first.1 = (f32[1152,768]{1,0:T(8,128)S(1)}, bf16[1024,768]{1,0:T(8,128)(2,1)S(1)}, bf16[128,768]{1,0:T(8,128)(2,1)S(1)}) custom-call(f32[1]{0:T(128)S(6)} %copy.8.advect, f32[128,768]{1,0:T(8,128)S(1)} %get-tuple-element.30.refs_0_.refs_9_, f32[1024,768]{1,0:T(8,128)S(1)} %get-tuple-element.32.refs_1_.refs_10_, ...), custom_call_target="tpu_custom_call" | custom-call | flops 1000 | bytes 1000 | tf_op jit(solution)/shard_map/local_first/pallas_call | solution.py:41
  33.4 1.6 %collective-permute-start.8 = (bf16[1024,768]{1,0:T(8,128)(2,1)S(1)}, bf16[1024,768]{1,0:T(8,128)(2,1)S(1)}, u32[]{:S(2)}, u32[]{:S(2)}) collective-permute-start(bf16[1024,768]{1,0:T(8,128)(2,1)S(1)} %get-tuple-element.50), channel_id=1, source_target_pairs={{0,1},{1,0},{2,3},{3,2},{4,5},{5,4},{6,7},{7,6},{8,9},{9,8},{10,11... | collective-permute-start | bytes 4718600 | tf_op jit(solution)/shard_map/ppermute | solution.py:537
  35.0 9.0 %collective-permute-done.4.refs_1_ = bf16[1024,768]{1,0:T(8,128)(2,1)S(1)} collective-permute-done((bf16[1024,768]{1,0:T(8,128)(2,1)S(1)}, bf16[1024,768]{1,0:T(8,128)(2,1)S(1)}, u32[]{:S(2)}, u32[]{:S(2)}) %collective-permute-start.4) | collective-permute-done | bytes 1572896 | tf_op jit(solution)/shard_map/ppermute | solution.py:537
  44.0 1.2 %first_image.1 = (f32[1152,768]{1,0:T(8,128)S(1)}, bf16[384,768]{1,0:T(8,128)(2,1)S(1)}, bf16[384,768]{1,0:T(8,128)(2,1)S(1)}, bf16[384,768]{1,0:T(8,128)(2,1)S(1)}) custom-call(f32[1152,768]{1,0:T(8,128)S(1)} %get-tuple-element.38.part, bf16[128,768]{1,0:T(8,128)(2,1)S(1)} %collective-permute-done.3.refs_3_.refs_0_, ...), custom_call_target="tpu_custom_call" | custom-call | flops 99999997952 | bytes 1000 | tf_op jit(solution)/shard_map/first_image/pallas_call | solution.py:41
  45.2 2.9 %collective-permute-start.5 = (bf16[384,768]{1,0:T(8,128)(2,1)S(1)}, bf16[384,768]{1,0:T(8,128)(2,1)S(1)}, u32[]{:S(2)}, u32[]{:S(2)}) collective-permute-start(bf16[384,768]{1,0:T(8,128)(2,1)S(1)} %get-tuple-element.41.refs_0_.refs_1_), channel_id=1, source_target_pairs={{0,30},{2,0},{4,2},{6,4},{8,6},{10,8},{12,10},{14,12},{16,14},{18,... | collective-permute-start | bytes 1769480 | tf_op jit(solution)/shard_map/ppermute | solution.py:531
  48.1 2.2 %collective-permute-start.6 = (bf16[384,768]{1,0:T(8,128)(2,1)S(1)}, bf16[384,768]{1,0:T(8,128)(2,1)S(1)}, u32[]{:S(2)}, u32[]{:S(2)}) collective-permute-start(bf16[384,768]{1,0:T(8,128)(2,1)S(1)} %get-tuple-element.42.refs_1_.refs_2_), channel_id=1, source_target_pairs={{0,30},{2,0},{4,2},{6,4},{8,6},{10,8},{12,10},{14,12},{16,14},{18,... | collective-permute-start | bytes 1769480 | tf_op jit(solution)/shard_map/ppermute | solution.py:531
  50.4 0.1 collective-permute-start.7
  50.4 1.8 %collective-permute-start.9 = (bf16[128,768]{1,0:T(8,128)(2,1)S(1)}, bf16[128,768]{1,0:T(8,128)(2,1)S(1)}, u32[]{:S(2)}, u32[]{:S(2)}) collective-permute-start(bf16[128,768]{1,0:T(8,128)(2,1)S(1)} %get-tuple-element.52), channel_id=1, source_target_pairs={{0,1},{1,0},{2,3},{3,2},{4,5},{5,4},{6,7},{7,6},{8,9},{9,8},{10,11... | collective-permute-start | bytes 589832 | tf_op jit(solution)/shard_map/ppermute | solution.py:537
  52.2 10.2 %transform.3.refs_7_ = bf16[3,384,768]{2,1,0:T(8,128)(2,1)S(1)} custom-call(bf16[384,768]{1,0:T(8,128)(2,1)S(1)} %get-tuple-element.41.refs_0_.refs_1_, bf16[384,768]{1,0:T(8,128)(2,1)S(1)} %get-tuple-element.42.refs_1_.refs_2_, bf16[384,768]{1,0:T(8,128)(2,1)S(1)} %get-tuple-element.43.refs_2_.refs_3_, bf16[3,3,384,768]{3,2,1,0:T(8,128)(2,1)} %bitcast.14, ...), custom_call_target="tpu_custom_call" | custom-call | flops 1000 | bytes 1000 | tf_op jit(solution)/shard_map/transform/pallas_call | solution.py:41
  62.4 0.0 collective-permute-done.5.refs_4_
  62.4 0.0 collective-permute-done.6.refs_5_
  62.4 5.8 %collective-permute-done.7.refs_6_ = bf16[384,768]{1,0:T(8,128)(2,1)S(1)} collective-permute-done((bf16[384,768]{1,0:T(8,128)(2,1)S(1)}, bf16[384,768]{1,0:T(8,128)(2,1)S(1)}, u32[]{:S(2)}, u32[]{:S(2)}) %collective-permute-start.7) | collective-permute-done | bytes 589856 | tf_op jit(solution)/shard_map/ppermute | solution.py:531
  68.2 3.7 %local_last.1 = (f32[1152,768]{1,0:T(8,128)S(1)}, f32[384,768]{1,0:T(8,128)S(1)}, f32[8,128]{1,0:T(8,128)S(1)}) custom-call(f32[1]{0:T(128)S(6)} %copy.8.advect, f32[1152,768]{1,0:T(8,128)S(1)} %get-tuple-element.40.refs_0_.u1, bf16[384,768]{1,0:T(8,128)(2,1)S(1)} %get-tuple-element.41.refs_0_.refs_1_, ...), custom_call_target="tpu_custom_call" | custom-call | flops 1000 | bytes 1000 | tf_op jit(solution)/shard_map/local_last/pallas_call | solution.py:41
  71.9 5.8 %collective-permute-done.8.refs_2_ = bf16[1024,768]{1,0:T(8,128)(2,1)S(1)} collective-permute-done((bf16[1024,768]{1,0:T(8,128)(2,1)S(1)}, bf16[1024,768]{1,0:T(8,128)(2,1)S(1)}, u32[]{:S(2)}, u32[]{:S(2)}) %collective-permute-start.8) | collective-permute-done | bytes 1572896 | tf_op jit(solution)/shard_map/ppermute | solution.py:537
  77.7 1.6 %second_image.2 = (f32[1024,768]{1,0:T(8,128)S(1)}, f32[8,128]{1,0:T(8,128)S(1)}) custom-call(f32[384,768]{1,0:T(8,128)S(1)} %get-tuple-element.47.scale, f32[1152,768]{1,0:T(8,128)S(1)} %get-tuple-element.40.refs_0_.u1, f32[1152,768]{1,0:T(8,128)S(1)} %get-tuple-element.48.part, f32[8,128]{1,0:T(8,128)S(1)} %get-tuple-element.49.before, ...), custom_call_target="tpu_custom_call" | custom-call | flops 1000 | bytes 1000 | tf_op jit(solution)/shard_map/second_image/pallas_call | solution.py:41
  79.3 2.0 %collective-permute-done.9.refs_2_ = bf16[128,768]{1,0:T(8,128)(2,1)S(1)} collective-permute-done((bf16[128,768]{1,0:T(8,128)(2,1)S(1)}, bf16[128,768]{1,0:T(8,128)(2,1)S(1)}, u32[]{:S(2)}, u32[]{:S(2)}) %collective-permute-start.9) | collective-permute-done | bytes 196640 | tf_op jit(solution)/shard_map/ppermute | solution.py:537
  81.2 0.3 second_image.3
  81.5 13.0 %all_to_all.11 = f32[32,1,128]{2,1,0:T(1,128)S(1)} all-to-all(f32[32,1,128]{2,1,0:T(1,128)S(1)} %bitcast.10), channel_id=1, replica_groups=mesh['seg'=16,'rad'=2] {'rad','seg'}, dimensions={0} | all-to-all | bytes 32768 | tf_op jit(solution)/shard_map/all_to_all | solution.py:578
  94.5 2.1 %combine.1 = (f32[1152,768]{1,0:T(8,128)}, f32[6]{0:T(128)}) custom-call(f32[32,128]{1,0:T(8,128)S(1)} %bitcast.9, f32[1152,768]{1,0:T(8,128)S(1)} %get-tuple-element.40.refs_0_.u1, f32[128,768]{1,0:T(8,128)S(1)} %get-tuple-element.30.refs_0_.refs_9_, f32[1024,768]{1,0:T(8,128)S(1)} %get-tuple-element.32.refs_1_.refs_10_, ...), custom_call_target="tpu_custom_call" | custom-call | flops 1000 | bytes 1000 | tf_op jit(solution)/shard_map/combine/pallas_call | solution.py:41
Async XLA Ops:
  1.7 10.9 %collective-permute-start.3 = (bf16[128,768]{1,0:T(8,128)(2,1)S(1)}, bf16[128,768]{1,0:T(8,128)(2,1)S(1)}, u32[]{:S(2)}, u32[]{:S(2)}) collective-permute-start(bf16[128,768]{1,0:T(8,128)(2,1)S(1)} %get-tuple-element.31.refs_0_), channel_id=1, source_target_pairs={{0,1},{1,0},{2,3},{3,2},{4,5},{5,4},{6,7},{7,6},{8,9},{9,8},{10,11... | collective-permute-start | bytes 589832 | tf_op jit(solution)/shard_map/ppermute | solution.py:537
  6.6 37.4 %collective-permute-start.4 = (bf16[1024,768]{1,0:T(8,128)(2,1)S(1)}, bf16[1024,768]{1,0:T(8,128)(2,1)S(1)}, u32[]{:S(2)}, u32[]{:S(2)}) collective-permute-start(bf16[1024,768]{1,0:T(8,128)(2,1)S(1)} %get-tuple-element.39), channel_id=1, source_target_pairs={{0,1},{1,0},{2,3},{3,2},{4,5},{5,4},{6,7},{7,6},{8,9},{9,8},{10,11... | collective-permute-start | bytes 4718600 | tf_op jit(solution)/shard_map/ppermute | solution.py:537
  6.7 20.4 %collective-permute-start = (bf16[384,768]{1,0:T(8,128)(2,1)S(1)}, bf16[384,768]{1,0:T(8,128)(2,1)S(1)}, u32[]{:S(2)}, u32[]{:S(2)}) collective-permute-start(bf16[384,768]{1,0:T(8,128)(2,1)S(1)} %get-tuple-element.33.refs_0_.refs_2_), channel_id=1, source_target_pairs={{0,30},{2,0},{4,2},{6,4},{8,6},{10,8},{12,10},{14,12},{16,14},{18,... | collective-permute-start | bytes 1769480 | tf_op jit(solution)/shard_map/ppermute | solution.py:531
  10.6 16.5 %collective-permute-start.1 = (bf16[384,768]{1,0:T(8,128)(2,1)S(1)}, bf16[384,768]{1,0:T(8,128)(2,1)S(1)}, u32[]{:S(2)}, u32[]{:S(2)}) collective-permute-start(bf16[384,768]{1,0:T(8,128)(2,1)S(1)} %get-tuple-element.34.refs_1_.refs_3_), channel_id=1, source_target_pairs={{0,30},{2,0},{4,2},{6,4},{8,6},{10,8},{12,10},{14,12},{16,14},{18,... | collective-permute-start | bytes 1769480 | tf_op jit(solution)/shard_map/ppermute | solution.py:531
  11.8 18.8 %collective-permute-start.2 = (bf16[384,768]{1,0:T(8,128)(2,1)S(1)}, bf16[384,768]{1,0:T(8,128)(2,1)S(1)}, u32[]{:S(2)}, u32[]{:S(2)}) collective-permute-start(bf16[384,768]{1,0:T(8,128)(2,1)S(1)} %get-tuple-element.35.refs_2_.refs_4_), channel_id=1, source_target_pairs={{0,30},{2,0},{4,2},{6,4},{8,6},{10,8},{12,10},{14,12},{16,14},{18,... | collective-permute-start | bytes 1769480 | tf_op jit(solution)/shard_map/ppermute | solution.py:531
  33.4 44.3 %collective-permute-start.8 = (bf16[1024,768]{1,0:T(8,128)(2,1)S(1)}, bf16[1024,768]{1,0:T(8,128)(2,1)S(1)}, u32[]{:S(2)}, u32[]{:S(2)}) collective-permute-start(bf16[1024,768]{1,0:T(8,128)(2,1)S(1)} %get-tuple-element.50), channel_id=1, source_target_pairs={{0,1},{1,0},{2,3},{3,2},{4,5},{5,4},{6,7},{7,6},{8,9},{9,8},{10,11... | collective-permute-start | bytes 4718600 | tf_op jit(solution)/shard_map/ppermute | solution.py:537
  45.2 17.1 %collective-permute-start.5 = (bf16[384,768]{1,0:T(8,128)(2,1)S(1)}, bf16[384,768]{1,0:T(8,128)(2,1)S(1)}, u32[]{:S(2)}, u32[]{:S(2)}) collective-permute-start(bf16[384,768]{1,0:T(8,128)(2,1)S(1)} %get-tuple-element.41.refs_0_.refs_1_), channel_id=1, source_target_pairs={{0,30},{2,0},{4,2},{6,4},{8,6},{10,8},{12,10},{14,12},{16,14},{18,... | collective-permute-start | bytes 1769480 | tf_op jit(solution)/shard_map/ppermute | solution.py:531
  48.1 14.2 %collective-permute-start.6 = (bf16[384,768]{1,0:T(8,128)(2,1)S(1)}, bf16[384,768]{1,0:T(8,128)(2,1)S(1)}, u32[]{:S(2)}, u32[]{:S(2)}) collective-permute-start(bf16[384,768]{1,0:T(8,128)(2,1)S(1)} %get-tuple-element.42.refs_1_.refs_2_), channel_id=1, source_target_pairs={{0,30},{2,0},{4,2},{6,4},{8,6},{10,8},{12,10},{14,12},{16,14},{18,... | collective-permute-start | bytes 1769480 | tf_op jit(solution)/shard_map/ppermute | solution.py:531
  50.4 17.8 %collective-permute-start.7 = (bf16[384,768]{1,0:T(8,128)(2,1)S(1)}, bf16[384,768]{1,0:T(8,128)(2,1)S(1)}, u32[]{:S(2)}, u32[]{:S(2)}) collective-permute-start(bf16[384,768]{1,0:T(8,128)(2,1)S(1)} %get-tuple-element.43.refs_2_.refs_3_), channel_id=1, source_target_pairs={{0,30},{2,0},{4,2},{6,4},{8,6},{10,8},{12,10},{14,12},{16,14},{18,... | collective-permute-start | bytes 1769480 | tf_op jit(solution)/shard_map/ppermute | solution.py:531
  50.4 30.8 %collective-permute-start.9 = (bf16[128,768]{1,0:T(8,128)(2,1)S(1)}, bf16[128,768]{1,0:T(8,128)(2,1)S(1)}, u32[]{:S(2)}, u32[]{:S(2)}) collective-permute-start(bf16[128,768]{1,0:T(8,128)(2,1)S(1)} %get-tuple-element.52), channel_id=1, source_target_pairs={{0,1},{1,0},{2,3},{3,2},{4,5},{5,4},{6,7},{7,6},{8,9},{9,8},{10,11... | collective-permute-start | bytes 589832 | tf_op jit(solution)/shard_map/ppermute | solution.py:537

commit v8 on v5

--- a/solution.py
+++ b/solution.py
@@ -24,6 +24,7 @@
 LONG = 10**11
 MEDIUM = 15 * 10**9
 CHUNK = 64
+STEP = 64
 EARLY_ROWS = 128
 LATE_ROWS = 128
 
@@ -294,9 +295,13 @@
     return F32(1.0) / (F32(1.0) + F32(VISC_AXIAL) * fk * fk + turning)
 
 
+def one_tile(value):
+    value = sum(value[r : r + 8] for r in range(0, value.shape[0], 8))
+    return sum(value[:, k : k + 128] for k in range(0, value.shape[1], 128))
+
+
 def add_tile(acc, n, value):
-    value = sum(value[r : r + 8] for r in range(0, value.shape[0], 8))
-    acc[n] += sum(value[:, k : k + 128] for k in range(0, value.shape[1], 128))
+    acc[n] += one_tile(value)
 
 
 def local_kernel(counts, last, paired, advect, *refs):
@@ -426,19 +431,25 @@
     modes_m = scale.shape[0]
     acc[...] = jnp.zeros_like(acc)
 
-    def step(row, shift):
-        at = pl.ds(pl.multiple_of(shift + row % modes_m, BAND), BAND)
-        near = added([[p] for p in planes], row - first, shift)
-        x2 = read([part], row, shift) + near * scale[at, :]
-        write([out], row - first, shift, x2)
-        for n, x in enumerate((read(u0, row, shift), read([u1], row, shift), x2)):
-            add_tile(acc, n, x * x2)
+    def step(start, i):
+        shift = pl.multiple_of(i * STEP, STEP)
+        totals = [None] * 3
+        for row in range(start, start + STEP, BAND):
+            at = pl.ds(pl.multiple_of(shift + row % modes_m, BAND), BAND)
+            near = added([[p] for p in planes], row - first, shift)
+            x2 = read([part], row, shift) + near * scale[at, :]
+            write([out], row - first, shift, x2)
+            for n, x in enumerate((read(u0, row, shift), read([u1], row, shift), x2)):
+                value = one_tile(x * x2)
+                totals[n] = value if totals[n] is None else totals[n] + value
+        for n in range(3):
+            acc[n] += totals[n]
 
     end = first + out.shape[0]
     starts = {first, *starts_of(u0), *range(0, end, modes_m)}
     starts = [r for r in sorted(starts) if first <= r < end]
     for lo, hi in zip(starts, starts[1:] + [end]):
-        for_bands(lo, hi, functools.partial(step, lo))
+        pl.loop(0, (hi - lo) // STEP)(functools.partial(step, lo))
 
     rows = [jnp.sum(acc[n], axis=0, keepdims=True) for n in range(3)]
     total = before[...] + jnp.concatenate([jnp.zeros((3, 128), F32), *rows, jnp.zeros((2, 128), F32)], axis=0)

time: 96.9 us -> 96.8 us (level)
  no operation moved by 1% of the time
where the time goes in v8:
time: 96.8 us; the launch traced here: 96.6 us
  Pallas kernels  39 us (40%)
  waiting for transfers between devices  26.4 us (27%)
  starting transfers between devices  16.8 us (17%)
  blocking collectives  13 us (13%)
  between operations  1.38 us (1%)
    pallas_call x10, Pallas kernels, kernel_call(): pl.pallas_call(body, out_shape=outs, in_specs=in_specs, scratch_shapes=li...  39 us
    ppermute x4, waiting for transfers between devices, neighbour_planes(): return [lax.ppermute(value, axis, [(0, 1), (1, 0)])]  17 us
    all_to_all x1, blocking collectives, on_device(): grams = lax.all_to_all(gram, ('rad', 'seg'), 0, 0)  13 us
    ppermute x6, starting transfers between devices, shifted(): lax.ppermute(value, axis, [(i, (i + steps) % count) for i in range(count)])  10.4 us
    ppermute x6, waiting for transfers between devices, shifted(): lax.ppermute(value, axis, [(i, (i + steps) % count) for i in range(count)])  9.36 us
    ppermute x4, starting transfers between devices, neighbour_planes(): return [lax.ppermute(value, axis, [(0, 1), (1, 0)])]  6.46 us
  transfers between devices with their start and end apart: 10, of which 5 were waited for; matrix products, arithmetic and copies ran while one was open for 0% of the time, Pallas kernels for 37%

profile of v8, /device:TPU:0, one launch (start us, length us, event | category | flops | bytes accessed | tf_op | source)
XLA Modules:
  0.0 96.6 jit_solution(13499867704065179357)
XLA Ops:
  0.6 1.0 %take_rows.2 = (f32[128,768]{1,0:T(8,128)S(1)}, bf16[128,768]{1,0:T(8,128)(2,1)S(1)}) custom-call(f32[1152,768]{1,0:T(8,128)} %bitcast.11), custom_call_target="tpu_custom_call" | custom-call | flops 1000 | bytes 1000 | tf_op jit(solution)/shard_map/take_rows/pallas_call | solution.py:42
  1.7 3.0 %collective-permute-start.3 = (bf16[128,768]{1,0:T(8,128)(2,1)S(1)}, bf16[128,768]{1,0:T(8,128)(2,1)S(1)}, u32[]{:S(2)}, u32[]{:S(2)}) collective-permute-start(bf16[128,768]{1,0:T(8,128)(2,1)S(1)} %get-tuple-element.31.refs_0_), channel_id=1, source_target_pairs={{0,1},{1,0},{2,3},{3,2},{4,5},{5,4},{6,7},{7,6},{8,9},{9,8},{10,11... | collective-permute-start | bytes 589832 | tf_op jit(solution)/shard_map/ppermute | solution.py:548
  4.7 1.9 %take_rows.3 = (f32[1024,768]{1,0:T(8,128)S(1)}, bf16[1024,768]{1,0:T(8,128)(2,1)S(1)}, bf16[384,768]{1,0:T(8,128)(2,1)S(1)}, bf16[384,768]{1,0:T(8,128)(2,1)S(1)}, bf16[384,768]{1,0:T(8,128)(2,1)S(1)}) custom-call(f32[1152,768]{1,0:T(8,128)} %bitcast.12, bf16[128,768]{1,0:T(8,128)(2,1)S(1)} %get-tuple-element.31.refs_0_), custom_call_target="tpu_custom_call" | custom-call | flops 1000 | bytes 1000 | tf_op jit(solution)/shard_map/take_rows/pallas_call | solution.py:42
  6.6 0.1 collective-permute-start.4
  6.7 3.9 %collective-permute-start = (bf16[384,768]{1,0:T(8,128)(2,1)S(1)}, bf16[384,768]{1,0:T(8,128)(2,1)S(1)}, u32[]{:S(2)}, u32[]{:S(2)}) collective-permute-start(bf16[384,768]{1,0:T(8,128)(2,1)S(1)} %get-tuple-element.33.refs_0_.refs_2_), channel_id=1, source_target_pairs={{0,30},{2,0},{4,2},{6,4},{8,6},{10,8},{12,10},{14,12},{16,14},{18,... | collective-permute-start | bytes 1769480 | tf_op jit(solution)/shard_map/ppermute | solution.py:542
  10.6 1.2 %collective-permute-start.1 = (bf16[384,768]{1,0:T(8,128)(2,1)S(1)}, bf16[384,768]{1,0:T(8,128)(2,1)S(1)}, u32[]{:S(2)}, u32[]{:S(2)}) collective-permute-start(bf16[384,768]{1,0:T(8,128)(2,1)S(1)} %get-tuple-element.34.refs_1_.refs_3_), channel_id=1, source_target_pairs={{0,30},{2,0},{4,2},{6,4},{8,6},{10,8},{12,10},{14,12},{16,14},{18,... | collective-permute-start | bytes 1769480 | tf_op jit(solution)/shard_map/ppermute | solution.py:542
  11.8 0.0 collective-permute-start.2
  12.5 0.0 collective-permute-done.3.refs_3_.refs_0_
  12.5 14.5 %transform.2 = (bf16[3,384,768]{2,1,0:T(8,128)(2,1)S(1)}, bf16[768,768]{1,0:T(8,128)(2,1)}, bf16[384,384]{1,0:T(8,128)(2,1)}, bf16[768,768]{1,0:T(8,128)(2,1)}, bf16[384,384]{1,0:T(8,128)(2,1)S(1)}) custom-call(bf16[384,768]{1,0:T(8,128)(2,1)S(1)} %get-tuple-element.33.refs_0_.refs_2_, bf16[384,768]{1,0:T(8,128)(2,1)S(1)} %get-tuple-element.34.refs_1_.refs_3_, ...), custom_call_target="tpu_custom_call" | custom-call | flops 15000000512 | bytes 1000 | tf_op jit(solution)/shard_map/transform/pallas_call | solution.py:42
  27.1 0.0 collective-permute-done.refs_5_
  27.1 0.0 collective-permute-done.1.refs_6_
  27.1 3.6 %collective-permute-done.2.refs_7_ = bf16[384,768]{1,0:T(8,128)(2,1)S(1)} collective-permute-done((bf16[384,768]{1,0:T(8,128)(2,1)S(1)}, bf16[384,768]{1,0:T(8,128)(2,1)S(1)}, u32[]{:S(2)}, u32[]{:S(2)}) %collective-permute-start.2) | collective-permute-done | bytes 589856 | tf_op jit(solution)/shard_map/ppermute | solution.py:542
  30.6 2.8 %local_first.1 = (f32[1152,768]{1,0:T(8,128)S(1)}, bf16[1024,768]{1,0:T(8,128)(2,1)S(1)}, bf16[128,768]{1,0:T(8,128)(2,1)S(1)}) custom-call(f32[1]{0:T(128)S(6)} %copy.8.advect, f32[128,768]{1,0:T(8,128)S(1)} %get-tuple-element.30.refs_0_.refs_9_, f32[1024,768]{1,0:T(8,128)S(1)} %get-tuple-element.32.refs_1_.refs_10_, ...), custom_call_target="tpu_custom_call" | custom-call | flops 1000 | bytes 1000 | tf_op jit(solution)/shard_map/local_first/pallas_call | solution.py:42
  33.4 1.6 %collective-permute-start.8 = (bf16[1024,768]{1,0:T(8,128)(2,1)S(1)}, bf16[1024,768]{1,0:T(8,128)(2,1)S(1)}, u32[]{:S(2)}, u32[]{:S(2)}) collective-permute-start(bf16[1024,768]{1,0:T(8,128)(2,1)S(1)} %get-tuple-element.50), channel_id=1, source_target_pairs={{0,1},{1,0},{2,3},{3,2},{4,5},{5,4},{6,7},{7,6},{8,9},{9,8},{10,11... | collective-permute-start | bytes 4718600 | tf_op jit(solution)/shard_map/ppermute | solution.py:548
  35.0 9.0 %collective-permute-done.4.refs_1_ = bf16[1024,768]{1,0:T(8,128)(2,1)S(1)} collective-permute-done((bf16[1024,768]{1,0:T(8,128)(2,1)S(1)}, bf16[1024,768]{1,0:T(8,128)(2,1)S(1)}, u32[]{:S(2)}, u32[]{:S(2)}) %collective-permute-start.4) | collective-permute-done | bytes 1572896 | tf_op jit(solution)/shard_map/ppermute | solution.py:548
  44.0 1.2 %first_image.1 = (f32[1152,768]{1,0:T(8,128)S(1)}, bf16[384,768]{1,0:T(8,128)(2,1)S(1)}, bf16[384,768]{1,0:T(8,128)(2,1)S(1)}, bf16[384,768]{1,0:T(8,128)(2,1)S(1)}) custom-call(f32[1152,768]{1,0:T(8,128)S(1)} %get-tuple-element.38.part, bf16[128,768]{1,0:T(8,128)(2,1)S(1)} %collective-permute-done.3.refs_3_.refs_0_, ...), custom_call_target="tpu_custom_call" | custom-call | flops 99999997952 | bytes 1000 | tf_op jit(solution)/shard_map/first_image/pallas_call | solution.py:42
  45.2 2.9 %collective-permute-start.5 = (bf16[384,768]{1,0:T(8,128)(2,1)S(1)}, bf16[384,768]{1,0:T(8,128)(2,1)S(1)}, u32[]{:S(2)}, u32[]{:S(2)}) collective-permute-start(bf16[384,768]{1,0:T(8,128)(2,1)S(1)} %get-tuple-element.41.refs_0_.refs_1_), channel_id=1, source_target_pairs={{0,30},{2,0},{4,2},{6,4},{8,6},{10,8},{12,10},{14,12},{16,14},{18,... | collective-permute-start | bytes 1769480 | tf_op jit(solution)/shard_map/ppermute | solution.py:542
  48.1 2.2 %collective-permute-start.6 = (bf16[384,768]{1,0:T(8,128)(2,1)S(1)}, bf16[384,768]{1,0:T(8,128)(2,1)S(1)}, u32[]{:S(2)}, u32[]{:S(2)}) collective-permute-start(bf16[384,768]{1,0:T(8,128)(2,1)S(1)} %get-tuple-element.42.refs_1_.refs_2_), channel_id=1, source_target_pairs={{0,30},{2,0},{4,2},{6,4},{8,6},{10,8},{12,10},{14,12},{16,14},{18,... | collective-permute-start | bytes 1769480 | tf_op jit(solution)/shard_map/ppermute | solution.py:542
  50.4 0.1 collective-permute-start.7
  50.4 1.8 %collective-permute-start.9 = (bf16[128,768]{1,0:T(8,128)(2,1)S(1)}, bf16[128,768]{1,0:T(8,128)(2,1)S(1)}, u32[]{:S(2)}, u32[]{:S(2)}) collective-permute-start(bf16[128,768]{1,0:T(8,128)(2,1)S(1)} %get-tuple-element.52), channel_id=1, source_target_pairs={{0,1},{1,0},{2,3},{3,2},{4,5},{5,4},{6,7},{7,6},{8,9},{9,8},{10,11... | collective-permute-start | bytes 589832 | tf_op jit(solution)/shard_map/ppermute | solution.py:548
  52.2 10.2 %transform.3.refs_7_ = bf16[3,384,768]{2,1,0:T(8,128)(2,1)S(1)} custom-call(bf16[384,768]{1,0:T(8,128)(2,1)S(1)} %get-tuple-element.41.refs_0_.refs_1_, bf16[384,768]{1,0:T(8,128)(2,1)S(1)} %get-tuple-element.42.refs_1_.refs_2_, bf16[384,768]{1,0:T(8,128)(2,1)S(1)} %get-tuple-element.43.refs_2_.refs_3_, bf16[3,3,384,768]{3,2,1,0:T(8,128)(2,1)} %bitcast.14, ...), custom_call_target="tpu_custom_call" | custom-call | flops 1000 | bytes 1000 | tf_op jit(solution)/shard_map/transform/pallas_call | solution.py:42
  62.4 0.0 collective-permute-done.5.refs_4_
  62.4 0.0 collective-permute-done.6.refs_5_
  62.4 5.8 %collective-permute-done.7.refs_6_ = bf16[384,768]{1,0:T(8,128)(2,1)S(1)} collective-permute-done((bf16[384,768]{1,0:T(8,128)(2,1)S(1)}, bf16[384,768]{1,0:T(8,128)(2,1)S(1)}, u32[]{:S(2)}, u32[]{:S(2)}) %collective-permute-start.7) | collective-permute-done | bytes 589856 | tf_op jit(solution)/shard_map/ppermute | solution.py:542
  68.2 3.7 %local_last.1 = (f32[1152,768]{1,0:T(8,128)S(1)}, f32[384,768]{1,0:T(8,128)S(1)}, f32[8,128]{1,0:T(8,128)S(1)}) custom-call(f32[1]{0:T(128)S(6)} %copy.8.advect, f32[1152,768]{1,0:T(8,128)S(1)} %get-tuple-element.40.refs_0_.u1, bf16[384,768]{1,0:T(8,128)(2,1)S(1)} %get-tuple-element.41.refs_0_.refs_1_, ...), custom_call_target="tpu_custom_call" | custom-call | flops 1000 | bytes 1000 | tf_op jit(solution)/shard_map/local_last/pallas_call | solution.py:42
  71.9 5.8 %collective-permute-done.8.refs_2_ = bf16[1024,768]{1,0:T(8,128)(2,1)S(1)} collective-permute-done((bf16[1024,768]{1,0:T(8,128)(2,1)S(1)}, bf16[1024,768]{1,0:T(8,128)(2,1)S(1)}, u32[]{:S(2)}, u32[]{:S(2)}) %collective-permute-start.8) | collective-permute-done | bytes 1572896 | tf_op jit(solution)/shard_map/ppermute | solution.py:548
  77.7 1.3 %second_image.2 = (f32[1024,768]{1,0:T(8,128)S(1)}, f32[8,128]{1,0:T(8,128)S(1)}) custom-call(f32[384,768]{1,0:T(8,128)S(1)} %get-tuple-element.47.scale, f32[1152,768]{1,0:T(8,128)S(1)} %get-tuple-element.40.refs_0_.u1, f32[1152,768]{1,0:T(8,128)S(1)} %get-tuple-element.48.part, f32[8,128]{1,0:T(8,128)S(1)} %get-tuple-element.49.before, ...), custom_call_target="tpu_custom_call" | custom-call | flops 1000 | bytes 1000 | tf_op jit(solution)/shard_map/second_image/pallas_call | solution.py:42
  79.0 2.3 %collective-permute-done.9.refs_2_ = bf16[128,768]{1,0:T(8,128)(2,1)S(1)} collective-permute-done((bf16[128,768]{1,0:T(8,128)(2,1)S(1)}, bf16[128,768]{1,0:T(8,128)(2,1)S(1)}, u32[]{:S(2)}, u32[]{:S(2)}) %collective-permute-start.9) | collective-permute-done | bytes 196640 | tf_op jit(solution)/shard_map/ppermute | solution.py:548
  81.2 0.3 second_image.3
  81.5 13.0 %all_to_all.11 = f32[32,1,128]{2,1,0:T(1,128)S(1)} all-to-all(f32[32,1,128]{2,1,0:T(1,128)S(1)} %bitcast.10), channel_id=1, replica_groups=mesh['seg'=16,'rad'=2] {'rad','seg'}, dimensions={0} | all-to-all | bytes 32768 | tf_op jit(solution)/shard_map/all_to_all | solution.py:589
  94.5 2.1 %combine.1 = (f32[1152,768]{1,0:T(8,128)}, f32[6]{0:T(128)}) custom-call(f32[32,128]{1,0:T(8,128)S(1)} %bitcast.9, f32[1152,768]{1,0:T(8,128)S(1)} %get-tuple-element.40.refs_0_.u1, f32[128,768]{1,0:T(8,128)S(1)} %get-tuple-element.30.refs_0_.refs_9_, f32[1024,768]{1,0:T(8,128)S(1)} %get-tuple-element.32.refs_1_.refs_10_, ...), custom_call_target="tpu_custom_call" | custom-call | flops 1000 | bytes 1000 | tf_op jit(solution)/shard_map/combine/pallas_call | solution.py:42
Async XLA Ops:
  1.7 10.9 %collective-permute-start.3 = (bf16[128,768]{1,0:T(8,128)(2,1)S(1)}, bf16[128,768]{1,0:T(8,128)(2,1)S(1)}, u32[]{:S(2)}, u32[]{:S(2)}) collective-permute-start(bf16[128,768]{1,0:T(8,128)(2,1)S(1)} %get-tuple-element.31.refs_0_), channel_id=1, source_target_pairs={{0,1},{1,0},{2,3},{3,2},{4,5},{5,4},{6,7},{7,6},{8,9},{9,8},{10,11... | collective-permute-start | bytes 589832 | tf_op jit(solution)/shard_map/ppermute | solution.py:548
  6.6 37.4 %collective-permute-start.4 = (bf16[1024,768]{1,0:T(8,128)(2,1)S(1)}, bf16[1024,768]{1,0:T(8,128)(2,1)S(1)}, u32[]{:S(2)}, u32[]{:S(2)}) collective-permute-start(bf16[1024,768]{1,0:T(8,128)(2,1)S(1)} %get-tuple-element.39), channel_id=1, source_target_pairs={{0,1},{1,0},{2,3},{3,2},{4,5},{5,4},{6,7},{7,6},{8,9},{9,8},{10,11... | collective-permute-start | bytes 4718600 | tf_op jit(solution)/shard_map/ppermute | solution.py:548
  6.7 20.4 %collective-permute-start = (bf16[384,768]{1,0:T(8,128)(2,1)S(1)}, bf16[384,768]{1,0:T(8,128)(2,1)S(1)}, u32[]{:S(2)}, u32[]{:S(2)}) collective-permute-start(bf16[384,768]{1,0:T(8,128)(2,1)S(1)} %get-tuple-element.33.refs_0_.refs_2_), channel_id=1, source_target_pairs={{0,30},{2,0},{4,2},{6,4},{8,6},{10,8},{12,10},{14,12},{16,14},{18,... | collective-permute-start | bytes 1769480 | tf_op jit(solution)/shard_map/ppermute | solution.py:542
  10.6 16.5 %collective-permute-start.1 = (bf16[384,768]{1,0:T(8,128)(2,1)S(1)}, bf16[384,768]{1,0:T(8,128)(2,1)S(1)}, u32[]{:S(2)}, u32[]{:S(2)}) collective-permute-start(bf16[384,768]{1,0:T(8,128)(2,1)S(1)} %get-tuple-element.34.refs_1_.refs_3_), channel_id=1, source_target_pairs={{0,30},{2,0},{4,2},{6,4},{8,6},{10,8},{12,10},{14,12},{16,14},{18,... | collective-permute-start | bytes 1769480 | tf_op jit(solution)/shard_map/ppermute | solution.py:542
  11.8 18.8 %collective-permute-start.2 = (bf16[384,768]{1,0:T(8,128)(2,1)S(1)}, bf16[384,768]{1,0:T(8,128)(2,1)S(1)}, u32[]{:S(2)}, u32[]{:S(2)}) collective-permute-start(bf16[384,768]{1,0:T(8,128)(2,1)S(1)} %get-tuple-element.35.refs_2_.refs_4_), channel_id=1, source_target_pairs={{0,30},{2,0},{4,2},{6,4},{8,6},{10,8},{12,10},{14,12},{16,14},{18,... | collective-permute-start | bytes 1769480 | tf_op jit(solution)/shard_map/ppermute | solution.py:542
  33.4 44.3 %collective-permute-start.8 = (bf16[1024,768]{1,0:T(8,128)(2,1)S(1)}, bf16[1024,768]{1,0:T(8,128)(2,1)S(1)}, u32[]{:S(2)}, u32[]{:S(2)}) collective-permute-start(bf16[1024,768]{1,0:T(8,128)(2,1)S(1)} %get-tuple-element.50), channel_id=1, source_target_pairs={{0,1},{1,0},{2,3},{3,2},{4,5},{5,4},{6,7},{7,6},{8,9},{9,8},{10,11... | collective-permute-start | bytes 4718600 | tf_op jit(solution)/shard_map/ppermute | solution.py:548
  45.2 17.1 %collective-permute-start.5 = (bf16[384,768]{1,0:T(8,128)(2,1)S(1)}, bf16[384,768]{1,0:T(8,128)(2,1)S(1)}, u32[]{:S(2)}, u32[]{:S(2)}) collective-permute-start(bf16[384,768]{1,0:T(8,128)(2,1)S(1)} %get-tuple-element.41.refs_0_.refs_1_), channel_id=1, source_target_pairs={{0,30},{2,0},{4,2},{6,4},{8,6},{10,8},{12,10},{14,12},{16,14},{18,... | collective-permute-start | bytes 1769480 | tf_op jit(solution)/shard_map/ppermute | solution.py:542
  48.1 14.2 %collective-permute-start.6 = (bf16[384,768]{1,0:T(8,128)(2,1)S(1)}, bf16[384,768]{1,0:T(8,128)(2,1)S(1)}, u32[]{:S(2)}, u32[]{:S(2)}) collective-permute-start(bf16[384,768]{1,0:T(8,128)(2,1)S(1)} %get-tuple-element.42.refs_1_.refs_2_), channel_id=1, source_target_pairs={{0,30},{2,0},{4,2},{6,4},{8,6},{10,8},{12,10},{14,12},{16,14},{18,... | collective-permute-start | bytes 1769480 | tf_op jit(solution)/shard_map/ppermute | solution.py:542
  50.4 17.8 %collective-permute-start.7 = (bf16[384,768]{1,0:T(8,128)(2,1)S(1)}, bf16[384,768]{1,0:T(8,128)(2,1)S(1)}, u32[]{:S(2)}, u32[]{:S(2)}) collective-permute-start(bf16[384,768]{1,0:T(8,128)(2,1)S(1)} %get-tuple-element.43.refs_2_.refs_3_), channel_id=1, source_target_pairs={{0,30},{2,0},{4,2},{6,4},{8,6},{10,8},{12,10},{14,12},{16,14},{18,... | collective-permute-start | bytes 1769480 | tf_op jit(solution)/shard_map/ppermute | solution.py:542
  50.4 30.8 %collective-permute-start.9 = (bf16[128,768]{1,0:T(8,128)(2,1)S(1)}, bf16[128,768]{1,0:T(8,128)(2,1)S(1)}, u32[]{:S(2)}, u32[]{:S(2)}) collective-permute-start(bf16[128,768]{1,0:T(8,128)(2,1)S(1)} %get-tuple-element.52), channel_id=1, source_target_pairs={{0,1},{1,0},{2,3},{3,2},{4,5},{5,4},{6,7},{7,6},{8,9},{9,8},{10,11... | collective-permute-start | bytes 589832 | tf_op jit(solution)/shard_map/ppermute | solution.py:548

commit v9 on v8

--- a/solution.py
+++ b/solution.py
@@ -26,7 +26,7 @@
 CHUNK = 64
 STEP = 64
 EARLY_ROWS = 128
-LATE_ROWS = 128
+LATE_ROWS = 64
 
 IN_SMEM = pl.BlockSpec(memory_space=pltpu.SMEM)
 IN_VMEM = pl.BlockSpec(memory_space=pltpu.VMEM)

time: 96.8 us -> 97 us (level)
  no operation moved by 1% of the time
where the time goes in v9:
time: 97 us; the launch traced here: 96.8 us
  Pallas kernels  39 us (40%)
  waiting for transfers between devices  26.3 us (27%)
  starting transfers between devices  16.8 us (17%)
  blocking collectives  13.3 us (14%)
  between operations  1.38 us (1%)
    pallas_call x10, Pallas kernels, kernel_call(): pl.pallas_call(body, out_shape=outs, in_specs=in_specs, scratch_shapes=li...  39 us
    ppermute x4, waiting for transfers between devices, neighbour_planes(): return [lax.ppermute(value, axis, [(0, 1), (1, 0)])]  16.9 us
    all_to_all x1, blocking collectives, on_device(): grams = lax.all_to_all(gram, ('rad', 'seg'), 0, 0)  13.3 us
    ppermute x6, starting transfers between devices, shifted(): lax.ppermute(value, axis, [(i, (i + steps) % count) for i in range(count)])  10.4 us
    ppermute x6, waiting for transfers between devices, shifted(): lax.ppermute(value, axis, [(i, (i + steps) % count) for i in range(count)])  9.36 us
    ppermute x4, starting transfers between devices, neighbour_planes(): return [lax.ppermute(value, axis, [(0, 1), (1, 0)])]  6.46 us
  transfers between devices with their start and end apart: 10, of which 5 were waited for; matrix products, arithmetic and copies ran while one was open for 0% of the time, Pallas kernels for 37%

profile of v9, /device:TPU:0, one launch (start us, length us, event | category | flops | bytes accessed | tf_op | source)
XLA Modules:
  0.0 96.8 jit_solution(11264359739190400331)
XLA Ops:
  0.6 1.0 %take_rows.2 = (f32[128,768]{1,0:T(8,128)S(1)}, bf16[128,768]{1,0:T(8,128)(2,1)S(1)}) custom-call(f32[1152,768]{1,0:T(8,128)} %bitcast.11), custom_call_target="tpu_custom_call" | custom-call | flops 1000 | bytes 1000 | tf_op jit(solution)/shard_map/take_rows/pallas_call | solution.py:42
  1.7 3.0 %collective-permute-start.3 = (bf16[128,768]{1,0:T(8,128)(2,1)S(1)}, bf16[128,768]{1,0:T(8,128)(2,1)S(1)}, u32[]{:S(2)}, u32[]{:S(2)}) collective-permute-start(bf16[128,768]{1,0:T(8,128)(2,1)S(1)} %get-tuple-element.31.refs_0_), channel_id=1, source_target_pairs={{0,1},{1,0},{2,3},{3,2},{4,5},{5,4},{6,7},{7,6},{8,9},{9,8},{10,11... | collective-permute-start | bytes 589832 | tf_op jit(solution)/shard_map/ppermute | solution.py:548
  4.7 1.9 %take_rows.3 = (f32[1024,768]{1,0:T(8,128)S(1)}, bf16[1024,768]{1,0:T(8,128)(2,1)S(1)}, bf16[384,768]{1,0:T(8,128)(2,1)S(1)}, bf16[384,768]{1,0:T(8,128)(2,1)S(1)}, bf16[384,768]{1,0:T(8,128)(2,1)S(1)}) custom-call(f32[1152,768]{1,0:T(8,128)} %bitcast.12, bf16[128,768]{1,0:T(8,128)(2,1)S(1)} %get-tuple-element.31.refs_0_), custom_call_target="tpu_custom_call" | custom-call | flops 1000 | bytes 1000 | tf_op jit(solution)/shard_map/take_rows/pallas_call | solution.py:42
  6.6 0.1 collective-permute-start.4
  6.7 3.9 %collective-permute-start = (bf16[384,768]{1,0:T(8,128)(2,1)S(1)}, bf16[384,768]{1,0:T(8,128)(2,1)S(1)}, u32[]{:S(2)}, u32[]{:S(2)}) collective-permute-start(bf16[384,768]{1,0:T(8,128)(2,1)S(1)} %get-tuple-element.33.refs_0_.refs_2_), channel_id=1, source_target_pairs={{0,30},{2,0},{4,2},{6,4},{8,6},{10,8},{12,10},{14,12},{16,14},{18,... | collective-permute-start | bytes 1769480 | tf_op jit(solution)/shard_map/ppermute | solution.py:542
  10.6 1.2 %collective-permute-start.1 = (bf16[384,768]{1,0:T(8,128)(2,1)S(1)}, bf16[384,768]{1,0:T(8,128)(2,1)S(1)}, u32[]{:S(2)}, u32[]{:S(2)}) collective-permute-start(bf16[384,768]{1,0:T(8,128)(2,1)S(1)} %get-tuple-element.34.refs_1_.refs_3_), channel_id=1, source_target_pairs={{0,30},{2,0},{4,2},{6,4},{8,6},{10,8},{12,10},{14,12},{16,14},{18,... | collective-permute-start | bytes 1769480 | tf_op jit(solution)/shard_map/ppermute | solution.py:542
  11.8 0.0 collective-permute-start.2
  12.5 0.0 collective-permute-done.3.refs_3_.refs_0_
  12.5 14.5 %transform.2 = (bf16[3,384,768]{2,1,0:T(8,128)(2,1)S(1)}, bf16[768,768]{1,0:T(8,128)(2,1)}, bf16[384,384]{1,0:T(8,128)(2,1)}, bf16[768,768]{1,0:T(8,128)(2,1)}, bf16[384,384]{1,0:T(8,128)(2,1)S(1)}) custom-call(bf16[384,768]{1,0:T(8,128)(2,1)S(1)} %get-tuple-element.33.refs_0_.refs_2_, bf16[384,768]{1,0:T(8,128)(2,1)S(1)} %get-tuple-element.34.refs_1_.refs_3_, ...), custom_call_target="tpu_custom_call" | custom-call | flops 15000000512 | bytes 1000 | tf_op jit(solution)/shard_map/transform/pallas_call | solution.py:42
  27.1 0.0 collective-permute-done.refs_5_
  27.1 0.0 collective-permute-done.1.refs_6_
  27.1 3.6 %collective-permute-done.2.refs_7_ = bf16[384,768]{1,0:T(8,128)(2,1)S(1)} collective-permute-done((bf16[384,768]{1,0:T(8,128)(2,1)S(1)}, bf16[384,768]{1,0:T(8,128)(2,1)S(1)}, u32[]{:S(2)}, u32[]{:S(2)}) %collective-permute-start.2) | collective-permute-done | bytes 589856 | tf_op jit(solution)/shard_map/ppermute | solution.py:542
  30.6 2.8 %local_first.1 = (f32[1152,768]{1,0:T(8,128)S(1)}, bf16[1088,768]{1,0:T(8,128)(2,1)S(1)}, bf16[64,768]{1,0:T(8,128)(2,1)S(1)}) custom-call(f32[1]{0:T(128)S(6)} %copy.8.advect, f32[128,768]{1,0:T(8,128)S(1)} %get-tuple-element.30.refs_0_.refs_9_, f32[1024,768]{1,0:T(8,128)S(1)} %get-tuple-element.32.refs_1_.refs_10_, ...), custom_call_target="tpu_custom_call" | custom-call | flops 1000 | bytes 1000 | tf_op jit(solution)/shard_map/local_first/pallas_call | solution.py:42
  33.4 1.6 %collective-permute-start.8 = (bf16[1088,768]{1,0:T(8,128)(2,1)S(1)}, bf16[1088,768]{1,0:T(8,128)(2,1)S(1)}, u32[]{:S(2)}, u32[]{:S(2)}) collective-permute-start(bf16[1088,768]{1,0:T(8,128)(2,1)S(1)} %get-tuple-element.50), channel_id=1, source_target_pairs={{0,1},{1,0},{2,3},{3,2},{4,5},{5,4},{6,7},{7,6},{8,9},{9,8},{10,11... | collective-permute-start | bytes 5013512 | tf_op jit(solution)/shard_map/ppermute | solution.py:548
  35.0 9.0 %collective-permute-done.4.refs_1_ = bf16[1024,768]{1,0:T(8,128)(2,1)S(1)} collective-permute-done((bf16[1024,768]{1,0:T(8,128)(2,1)S(1)}, bf16[1024,768]{1,0:T(8,128)(2,1)S(1)}, u32[]{:S(2)}, u32[]{:S(2)}) %collective-permute-start.4) | collective-permute-done | bytes 1572896 | tf_op jit(solution)/shard_map/ppermute | solution.py:548
  44.0 1.2 %first_image.1 = (f32[1152,768]{1,0:T(8,128)S(1)}, bf16[384,768]{1,0:T(8,128)(2,1)S(1)}, bf16[384,768]{1,0:T(8,128)(2,1)S(1)}, bf16[384,768]{1,0:T(8,128)(2,1)S(1)}) custom-call(f32[1152,768]{1,0:T(8,128)S(1)} %get-tuple-element.38.part, bf16[128,768]{1,0:T(8,128)(2,1)S(1)} %collective-permute-done.3.refs_3_.refs_0_, ...), custom_call_target="tpu_custom_call" | custom-call | flops 99999997952 | bytes 1000 | tf_op jit(solution)/shard_map/first_image/pallas_call | solution.py:42
  45.2 2.9 %collective-permute-start.5 = (bf16[384,768]{1,0:T(8,128)(2,1)S(1)}, bf16[384,768]{1,0:T(8,128)(2,1)S(1)}, u32[]{:S(2)}, u32[]{:S(2)}) collective-permute-start(bf16[384,768]{1,0:T(8,128)(2,1)S(1)} %get-tuple-element.41.refs_0_.refs_1_), channel_id=1, source_target_pairs={{0,30},{2,0},{4,2},{6,4},{8,6},{10,8},{12,10},{14,12},{16,14},{18,... | collective-permute-start | bytes 1769480 | tf_op jit(solution)/shard_map/ppermute | solution.py:542
  48.1 2.2 %collective-permute-start.6 = (bf16[384,768]{1,0:T(8,128)(2,1)S(1)}, bf16[384,768]{1,0:T(8,128)(2,1)S(1)}, u32[]{:S(2)}, u32[]{:S(2)}) collective-permute-start(bf16[384,768]{1,0:T(8,128)(2,1)S(1)} %get-tuple-element.42.refs_1_.refs_2_), channel_id=1, source_target_pairs={{0,30},{2,0},{4,2},{6,4},{8,6},{10,8},{12,10},{14,12},{16,14},{18,... | collective-permute-start | bytes 1769480 | tf_op jit(solution)/shard_map/ppermute | solution.py:542
  50.4 0.1 collective-permute-start.7
  50.4 1.8 %collective-permute-start.9 = (bf16[64,768]{1,0:T(8,128)(2,1)S(1)}, bf16[64,768]{1,0:T(8,128)(2,1)S(1)}, u32[]{:S(2)}, u32[]{:S(2)}) collective-permute-start(bf16[64,768]{1,0:T(8,128)(2,1)S(1)} %get-tuple-element.52), channel_id=1, source_target_pairs={{0,1},{1,0},{2,3},{3,2},{4,5},{5,4},{6,7},{7,6},{8,9},{9,8},{10,11... | collective-permute-start | bytes 294920 | tf_op jit(solution)/shard_map/ppermute | solution.py:548
  52.2 10.2 %transform.3.refs_7_ = bf16[3,384,768]{2,1,0:T(8,128)(2,1)S(1)} custom-call(bf16[384,768]{1,0:T(8,128)(2,1)S(1)} %get-tuple-element.41.refs_0_.refs_1_, bf16[384,768]{1,0:T(8,128)(2,1)S(1)} %get-tuple-element.42.refs_1_.refs_2_, bf16[384,768]{1,0:T(8,128)(2,1)S(1)} %get-tuple-element.43.refs_2_.refs_3_, bf16[3,3,384,768]{3,2,1,0:T(8,128)(2,1)} %bitcast.14, ...), custom_call_target="tpu_custom_call" | custom-call | flops 1000 | bytes 1000 | tf_op jit(solution)/shard_map/transform/pallas_call | solution.py:42
  62.4 0.0 collective-permute-done.5.refs_4_
  62.4 0.0 collective-permute-done.6.refs_5_
  62.4 5.8 %collective-permute-done.7.refs_6_ = bf16[384,768]{1,0:T(8,128)(2,1)S(1)} collective-permute-done((bf16[384,768]{1,0:T(8,128)(2,1)S(1)}, bf16[384,768]{1,0:T(8,128)(2,1)S(1)}, u32[]{:S(2)}, u32[]{:S(2)}) %collective-permute-start.7) | collective-permute-done | bytes 589856 | tf_op jit(solution)/shard_map/ppermute | solution.py:542
  68.2 3.7 %local_last.1 = (f32[1152,768]{1,0:T(8,128)S(1)}, f32[384,768]{1,0:T(8,128)S(1)}, f32[8,128]{1,0:T(8,128)S(1)}) custom-call(f32[1]{0:T(128)S(6)} %copy.8.advect, f32[1152,768]{1,0:T(8,128)S(1)} %get-tuple-element.40.refs_0_.u1, bf16[384,768]{1,0:T(8,128)(2,1)S(1)} %get-tuple-element.41.refs_0_.refs_1_, ...), custom_call_target="tpu_custom_call" | custom-call | flops 1000 | bytes 1000 | tf_op jit(solution)/shard_map/local_last/pallas_call | solution.py:42
  71.9 7.9 %collective-permute-done.8.refs_2_ = bf16[1088,768]{1,0:T(8,128)(2,1)S(1)} collective-permute-done((bf16[1088,768]{1,0:T(8,128)(2,1)S(1)}, bf16[1088,768]{1,0:T(8,128)(2,1)S(1)}, u32[]{:S(2)}, u32[]{:S(2)}) %collective-permute-start.8) | collective-permute-done | bytes 1671200 | tf_op jit(solution)/shard_map/ppermute | solution.py:548
  79.8 1.3 %second_image.2 = (f32[1088,768]{1,0:T(8,128)S(1)}, f32[8,128]{1,0:T(8,128)S(1)}) custom-call(f32[384,768]{1,0:T(8,128)S(1)} %get-tuple-element.47.scale, f32[1152,768]{1,0:T(8,128)S(1)} %get-tuple-element.40.refs_0_.u1, f32[1152,768]{1,0:T(8,128)S(1)} %get-tuple-element.48.part, f32[8,128]{1,0:T(8,128)S(1)} %get-tuple-element.49.before, ...), custom_call_target="tpu_custom_call" | custom-call | flops 1000 | bytes 1000 | tf_op jit(solution)/shard_map/second_image/pallas_call | solution.py:42
  81.1 0.1 collective-permute-done.9.refs_2_
  81.2 0.2 second_image.3
  81.4 13.3 %all_to_all.11 = f32[32,1,128]{2,1,0:T(1,128)S(1)} all-to-all(f32[32,1,128]{2,1,0:T(1,128)S(1)} %bitcast.10), channel_id=1, replica_groups=mesh['seg'=16,'rad'=2] {'rad','seg'}, dimensions={0} | all-to-all | bytes 32768 | tf_op jit(solution)/shard_map/all_to_all | solution.py:589
  94.7 2.1 %combine.1 = (f32[1152,768]{1,0:T(8,128)}, f32[6]{0:T(128)}) custom-call(f32[32,128]{1,0:T(8,128)S(1)} %bitcast.9, f32[1152,768]{1,0:T(8,128)S(1)} %get-tuple-element.40.refs_0_.u1, f32[128,768]{1,0:T(8,128)S(1)} %get-tuple-element.30.refs_0_.refs_9_, f32[1024,768]{1,0:T(8,128)S(1)} %get-tuple-element.32.refs_1_.refs_10_, ...), custom_call_target="tpu_custom_call" | custom-call | flops 1000 | bytes 1000 | tf_op jit(solution)/shard_map/combine/pallas_call | solution.py:42
Async XLA Ops:
  1.7 10.9 %collective-permute-start.3 = (bf16[128,768]{1,0:T(8,128)(2,1)S(1)}, bf16[128,768]{1,0:T(8,128)(2,1)S(1)}, u32[]{:S(2)}, u32[]{:S(2)}) collective-permute-start(bf16[128,768]{1,0:T(8,128)(2,1)S(1)} %get-tuple-element.31.refs_0_), channel_id=1, source_target_pairs={{0,1},{1,0},{2,3},{3,2},{4,5},{5,4},{6,7},{7,6},{8,9},{9,8},{10,11... | collective-permute-start | bytes 589832 | tf_op jit(solution)/shard_map/ppermute | solution.py:548
  6.6 37.4 %collective-permute-start.4 = (bf16[1024,768]{1,0:T(8,128)(2,1)S(1)}, bf16[1024,768]{1,0:T(8,128)(2,1)S(1)}, u32[]{:S(2)}, u32[]{:S(2)}) collective-permute-start(bf16[1024,768]{1,0:T(8,128)(2,1)S(1)} %get-tuple-element.39), channel_id=1, source_target_pairs={{0,1},{1,0},{2,3},{3,2},{4,5},{5,4},{6,7},{7,6},{8,9},{9,8},{10,11... | collective-permute-start | bytes 4718600 | tf_op jit(solution)/shard_map/ppermute | solution.py:548
  6.7 20.4 %collective-permute-start = (bf16[384,768]{1,0:T(8,128)(2,1)S(1)}, bf16[384,768]{1,0:T(8,128)(2,1)S(1)}, u32[]{:S(2)}, u32[]{:S(2)}) collective-permute-start(bf16[384,768]{1,0:T(8,128)(2,1)S(1)} %get-tuple-element.33.refs_0_.refs_2_), channel_id=1, source_target_pairs={{0,30},{2,0},{4,2},{6,4},{8,6},{10,8},{12,10},{14,12},{16,14},{18,... | collective-permute-start | bytes 1769480 | tf_op jit(solution)/shard_map/ppermute | solution.py:542
  10.6 16.5 %collective-permute-start.1 = (bf16[384,768]{1,0:T(8,128)(2,1)S(1)}, bf16[384,768]{1,0:T(8,128)(2,1)S(1)}, u32[]{:S(2)}, u32[]{:S(2)}) collective-permute-start(bf16[384,768]{1,0:T(8,128)(2,1)S(1)} %get-tuple-element.34.refs_1_.refs_3_), channel_id=1, source_target_pairs={{0,30},{2,0},{4,2},{6,4},{8,6},{10,8},{12,10},{14,12},{16,14},{18,... | collective-permute-start | bytes 1769480 | tf_op jit(solution)/shard_map/ppermute | solution.py:542
  11.8 18.8 %collective-permute-start.2 = (bf16[384,768]{1,0:T(8,128)(2,1)S(1)}, bf16[384,768]{1,0:T(8,128)(2,1)S(1)}, u32[]{:S(2)}, u32[]{:S(2)}) collective-permute-start(bf16[384,768]{1,0:T(8,128)(2,1)S(1)} %get-tuple-element.35.refs_2_.refs_4_), channel_id=1, source_target_pairs={{0,30},{2,0},{4,2},{6,4},{8,6},{10,8},{12,10},{14,12},{16,14},{18,... | collective-permute-start | bytes 1769480 | tf_op jit(solution)/shard_map/ppermute | solution.py:542
  33.4 46.4 %collective-permute-start.8 = (bf16[1088,768]{1,0:T(8,128)(2,1)S(1)}, bf16[1088,768]{1,0:T(8,128)(2,1)S(1)}, u32[]{:S(2)}, u32[]{:S(2)}) collective-permute-start(bf16[1088,768]{1,0:T(8,128)(2,1)S(1)} %get-tuple-element.50), channel_id=1, source_target_pairs={{0,1},{1,0},{2,3},{3,2},{4,5},{5,4},{6,7},{7,6},{8,9},{9,8},{10,11... | collective-permute-start | bytes 5013512 | tf_op jit(solution)/shard_map/ppermute | solution.py:548
  45.2 17.1 %collective-permute-start.5 = (bf16[384,768]{1,0:T(8,128)(2,1)S(1)}, bf16[384,768]{1,0:T(8,128)(2,1)S(1)}, u32[]{:S(2)}, u32[]{:S(2)}) collective-permute-start(bf16[384,768]{1,0:T(8,128)(2,1)S(1)} %get-tuple-element.41.refs_0_.refs_1_), channel_id=1, source_target_pairs={{0,30},{2,0},{4,2},{6,4},{8,6},{10,8},{12,10},{14,12},{16,14},{18,... | collective-permute-start | bytes 1769480 | tf_op jit(solution)/shard_map/ppermute | solution.py:542
  48.1 14.2 %collective-permute-start.6 = (bf16[384,768]{1,0:T(8,128)(2,1)S(1)}, bf16[384,768]{1,0:T(8,128)(2,1)S(1)}, u32[]{:S(2)}, u32[]{:S(2)}) collective-permute-start(bf16[384,768]{1,0:T(8,128)(2,1)S(1)} %get-tuple-element.42.refs_1_.refs_2_), channel_id=1, source_target_pairs={{0,30},{2,0},{4,2},{6,4},{8,6},{10,8},{12,10},{14,12},{16,14},{18,... | collective-permute-start | bytes 1769480 | tf_op jit(solution)/shard_map/ppermute | solution.py:542
  50.4 17.8 %collective-permute-start.7 = (bf16[384,768]{1,0:T(8,128)(2,1)S(1)}, bf16[384,768]{1,0:T(8,128)(2,1)S(1)}, u32[]{:S(2)}, u32[]{:S(2)}) collective-permute-start(bf16[384,768]{1,0:T(8,128)(2,1)S(1)} %get-tuple-element.43.refs_2_.refs_3_), channel_id=1, source_target_pairs={{0,30},{2,0},{4,2},{6,4},{8,6},{10,8},{12,10},{14,12},{16,14},{18,... | collective-permute-start | bytes 1769480 | tf_op jit(solution)/shard_map/ppermute | solution.py:542
  50.4 30.8 %collective-permute-start.9 = (bf16[64,768]{1,0:T(8,128)(2,1)S(1)}, bf16[64,768]{1,0:T(8,128)(2,1)S(1)}, u32[]{:S(2)}, u32[]{:S(2)}) collective-permute-start(bf16[64,768]{1,0:T(8,128)(2,1)S(1)} %get-tuple-element.52), channel_id=1, source_target_pairs={{0,1},{1,0},{2,3},{3,2},{4,5},{5,4},{6,7},{7,6},{8,9},{9,8},{10,11... | collective-permute-start | bytes 294920 | tf_op jit(solution)/shard_map/ppermute | solution.py:548

commit v10 on v8

--- a/solution.py
+++ b/solution.py
@@ -23,7 +23,7 @@
 BAND = 16
 LONG = 10**11
 MEDIUM = 15 * 10**9
-CHUNK = 64
+CHUNK = 128
 STEP = 64
 EARLY_ROWS = 128
 LATE_ROWS = 128

time: 96.8 us -> 96.8 us (level)
  no operation moved by 1% of the time
where the time goes in v10:
time: 96.8 us; the launch traced here: 96.6 us
  Pallas kernels  39 us (40%)
  waiting for transfers between devices  26.4 us (27%)
  starting transfers between devices  16.8 us (17%)
  blocking collectives  13 us (13%)
  between operations  1.38 us (1%)
    pallas_call x10, Pallas kernels, kernel_call(): pl.pallas_call(body, out_shape=outs, in_specs=in_specs, scratch_shapes=li...  39 us
    ppermute x4, waiting for transfers between devices, neighbour_planes(): return [lax.ppermute(value, axis, [(0, 1), (1, 0)])]  17 us
    all_to_all x1, blocking collectives, on_device(): grams = lax.all_to_all(gram, ('rad', 'seg'), 0, 0)  13 us
    ppermute x6, starting transfers between devices, shifted(): lax.ppermute(value, axis, [(i, (i + steps) % count) for i in range(count)])  10.4 us
    ppermute x6, waiting for transfers between devices, shifted(): lax.ppermute(value, axis, [(i, (i + steps) % count) for i in range(count)])  9.36 us
    ppermute x4, starting transfers between devices, neighbour_planes(): return [lax.ppermute(value, axis, [(0, 1), (1, 0)])]  6.46 us
  transfers between devices with their start and end apart: 10, of which 5 were waited for; matrix products, arithmetic and copies ran while one was open for 0% of the time, Pallas kernels for 37%

profile of v10, /device:TPU:0, one launch (start us, length us, event | category | flops | bytes accessed | tf_op | source)
XLA Modules:
  0.0 96.6 jit_solution(9271482971464256209)
XLA Ops:
  0.6 1.0 %take_rows.2 = (f32[128,768]{1,0:T(8,128)S(1)}, bf16[128,768]{1,0:T(8,128)(2,1)S(1)}) custom-call(f32[1152,768]{1,0:T(8,128)} %bitcast.11), custom_call_target="tpu_custom_call" | custom-call | flops 1000 | bytes 1000 | tf_op jit(solution)/shard_map/take_rows/pallas_call | solution.py:42
  1.7 3.0 %collective-permute-start.3 = (bf16[128,768]{1,0:T(8,128)(2,1)S(1)}, bf16[128,768]{1,0:T(8,128)(2,1)S(1)}, u32[]{:S(2)}, u32[]{:S(2)}) collective-permute-start(bf16[128,768]{1,0:T(8,128)(2,1)S(1)} %get-tuple-element.31.refs_0_), channel_id=1, source_target_pairs={{0,1},{1,0},{2,3},{3,2},{4,5},{5,4},{6,7},{7,6},{8,9},{9,8},{10,11... | collective-permute-start | bytes 589832 | tf_op jit(solution)/shard_map/ppermute | solution.py:548
  4.7 1.9 %take_rows.3 = (f32[1024,768]{1,0:T(8,128)S(1)}, bf16[1024,768]{1,0:T(8,128)(2,1)S(1)}, bf16[384,768]{1,0:T(8,128)(2,1)S(1)}, bf16[384,768]{1,0:T(8,128)(2,1)S(1)}, bf16[384,768]{1,0:T(8,128)(2,1)S(1)}) custom-call(f32[1152,768]{1,0:T(8,128)} %bitcast.12, bf16[128,768]{1,0:T(8,128)(2,1)S(1)} %get-tuple-element.31.refs_0_), custom_call_target="tpu_custom_call" | custom-call | flops 1000 | bytes 1000 | tf_op jit(solution)/shard_map/take_rows/pallas_call | solution.py:42
  6.6 0.1 collective-permute-start.4
  6.7 3.9 %collective-permute-start = (bf16[384,768]{1,0:T(8,128)(2,1)S(1)}, bf16[384,768]{1,0:T(8,128)(2,1)S(1)}, u32[]{:S(2)}, u32[]{:S(2)}) collective-permute-start(bf16[384,768]{1,0:T(8,128)(2,1)S(1)} %get-tuple-element.33.refs_0_.refs_2_), channel_id=1, source_target_pairs={{0,30},{2,0},{4,2},{6,4},{8,6},{10,8},{12,10},{14,12},{16,14},{18,... | collective-permute-start | bytes 1769480 | tf_op jit(solution)/shard_map/ppermute | solution.py:542
  10.6 1.2 %collective-permute-start.1 = (bf16[384,768]{1,0:T(8,128)(2,1)S(1)}, bf16[384,768]{1,0:T(8,128)(2,1)S(1)}, u32[]{:S(2)}, u32[]{:S(2)}) collective-permute-start(bf16[384,768]{1,0:T(8,128)(2,1)S(1)} %get-tuple-element.34.refs_1_.refs_3_), channel_id=1, source_target_pairs={{0,30},{2,0},{4,2},{6,4},{8,6},{10,8},{12,10},{14,12},{16,14},{18,... | collective-permute-start | bytes 1769480 | tf_op jit(solution)/shard_map/ppermute | solution.py:542
  11.8 0.0 collective-permute-start.2
  12.5 0.0 collective-permute-done.3.refs_3_.refs_0_
  12.5 14.5 %transform.2 = (bf16[3,384,768]{2,1,0:T(8,128)(2,1)S(1)}, bf16[768,768]{1,0:T(8,128)(2,1)}, bf16[384,384]{1,0:T(8,128)(2,1)}, bf16[768,768]{1,0:T(8,128)(2,1)}, bf16[384,384]{1,0:T(8,128)(2,1)S(1)}) custom-call(bf16[384,768]{1,0:T(8,128)(2,1)S(1)} %get-tuple-element.33.refs_0_.refs_2_, bf16[384,768]{1,0:T(8,128)(2,1)S(1)} %get-tuple-element.34.refs_1_.refs_3_, ...), custom_call_target="tpu_custom_call" | custom-call | flops 15000000512 | bytes 1000 | tf_op jit(solution)/shard_map/transform/pallas_call | solution.py:42
  27.1 0.0 collective-permute-done.refs_5_
  27.1 0.0 collective-permute-done.1.refs_6_
  27.1 3.6 %collective-permute-done.2.refs_7_ = bf16[384,768]{1,0:T(8,128)(2,1)S(1)} collective-permute-done((bf16[384,768]{1,0:T(8,128)(2,1)S(1)}, bf16[384,768]{1,0:T(8,128)(2,1)S(1)}, u32[]{:S(2)}, u32[]{:S(2)}) %collective-permute-start.2) | collective-permute-done | bytes 589856 | tf_op jit(solution)/shard_map/ppermute | solution.py:542
  30.6 2.8 %local_first.1 = (f32[1152,768]{1,0:T(8,128)S(1)}, bf16[1024,768]{1,0:T(8,128)(2,1)S(1)}, bf16[128,768]{1,0:T(8,128)(2,1)S(1)}) custom-call(f32[1]{0:T(128)S(6)} %copy.8.advect, f32[128,768]{1,0:T(8,128)S(1)} %get-tuple-element.30.refs_0_.refs_9_, f32[1024,768]{1,0:T(8,128)S(1)} %get-tuple-element.32.refs_1_.refs_10_, ...), custom_call_target="tpu_custom_call" | custom-call | flops 1000 | bytes 1000 | tf_op jit(solution)/shard_map/local_first/pallas_call | solution.py:42
  33.4 1.6 %collective-permute-start.8 = (bf16[1024,768]{1,0:T(8,128)(2,1)S(1)}, bf16[1024,768]{1,0:T(8,128)(2,1)S(1)}, u32[]{:S(2)}, u32[]{:S(2)}) collective-permute-start(bf16[1024,768]{1,0:T(8,128)(2,1)S(1)} %get-tuple-element.50), channel_id=1, source_target_pairs={{0,1},{1,0},{2,3},{3,2},{4,5},{5,4},{6,7},{7,6},{8,9},{9,8},{10,11... | collective-permute-start | bytes 4718600 | tf_op jit(solution)/shard_map/ppermute | solution.py:548
  35.0 9.0 %collective-permute-done.4.refs_1_ = bf16[1024,768]{1,0:T(8,128)(2,1)S(1)} collective-permute-done((bf16[1024,768]{1,0:T(8,128)(2,1)S(1)}, bf16[1024,768]{1,0:T(8,128)(2,1)S(1)}, u32[]{:S(2)}, u32[]{:S(2)}) %collective-permute-start.4) | collective-permute-done | bytes 1572896 | tf_op jit(solution)/shard_map/ppermute | solution.py:548
  44.0 1.2 %first_image.1 = (f32[1152,768]{1,0:T(8,128)S(1)}, bf16[384,768]{1,0:T(8,128)(2,1)S(1)}, bf16[384,768]{1,0:T(8,128)(2,1)S(1)}, bf16[384,768]{1,0:T(8,128)(2,1)S(1)}) custom-call(f32[1152,768]{1,0:T(8,128)S(1)} %get-tuple-element.38.part, bf16[128,768]{1,0:T(8,128)(2,1)S(1)} %collective-permute-done.3.refs_3_.refs_0_, ...), custom_call_target="tpu_custom_call" | custom-call | flops 99999997952 | bytes 1000 | tf_op jit(solution)/shard_map/first_image/pallas_call | solution.py:42
  45.2 2.9 %collective-permute-start.5 = (bf16[384,768]{1,0:T(8,128)(2,1)S(1)}, bf16[384,768]{1,0:T(8,128)(2,1)S(1)}, u32[]{:S(2)}, u32[]{:S(2)}) collective-permute-start(bf16[384,768]{1,0:T(8,128)(2,1)S(1)} %get-tuple-element.41.refs_0_.refs_1_), channel_id=1, source_target_pairs={{0,30},{2,0},{4,2},{6,4},{8,6},{10,8},{12,10},{14,12},{16,14},{18,... | collective-permute-start | bytes 1769480 | tf_op jit(solution)/shard_map/ppermute | solution.py:542
  48.1 2.2 %collective-permute-start.6 = (bf16[384,768]{1,0:T(8,128)(2,1)S(1)}, bf16[384,768]{1,0:T(8,128)(2,1)S(1)}, u32[]{:S(2)}, u32[]{:S(2)}) collective-permute-start(bf16[384,768]{1,0:T(8,128)(2,1)S(1)} %get-tuple-element.42.refs_1_.refs_2_), channel_id=1, source_target_pairs={{0,30},{2,0},{4,2},{6,4},{8,6},{10,8},{12,10},{14,12},{16,14},{18,... | collective-permute-start | bytes 1769480 | tf_op jit(solution)/shard_map/ppermute | solution.py:542
  50.4 0.1 collective-permute-start.7
  50.4 1.8 %collective-permute-start.9 = (bf16[128,768]{1,0:T(8,128)(2,1)S(1)}, bf16[128,768]{1,0:T(8,128)(2,1)S(1)}, u32[]{:S(2)}, u32[]{:S(2)}) collective-permute-start(bf16[128,768]{1,0:T(8,128)(2,1)S(1)} %get-tuple-element.52), channel_id=1, source_target_pairs={{0,1},{1,0},{2,3},{3,2},{4,5},{5,4},{6,7},{7,6},{8,9},{9,8},{10,11... | collective-permute-start | bytes 589832 | tf_op jit(solution)/shard_map/ppermute | solution.py:548
  52.2 10.2 %transform.3.refs_7_ = bf16[3,384,768]{2,1,0:T(8,128)(2,1)S(1)} custom-call(bf16[384,768]{1,0:T(8,128)(2,1)S(1)} %get-tuple-element.41.refs_0_.refs_1_, bf16[384,768]{1,0:T(8,128)(2,1)S(1)} %get-tuple-element.42.refs_1_.refs_2_, bf16[384,768]{1,0:T(8,128)(2,1)S(1)} %get-tuple-element.43.refs_2_.refs_3_, bf16[3,3,384,768]{3,2,1,0:T(8,128)(2,1)} %bitcast.14, ...), custom_call_target="tpu_custom_call" | custom-call | flops 1000 | bytes 1000 | tf_op jit(solution)/shard_map/transform/pallas_call | solution.py:42
  62.4 0.0 collective-permute-done.5.refs_4_
  62.4 0.0 collective-permute-done.6.refs_5_
  62.4 5.8 %collective-permute-done.7.refs_6_ = bf16[384,768]{1,0:T(8,128)(2,1)S(1)} collective-permute-done((bf16[384,768]{1,0:T(8,128)(2,1)S(1)}, bf16[384,768]{1,0:T(8,128)(2,1)S(1)}, u32[]{:S(2)}, u32[]{:S(2)}) %collective-permute-start.7) | collective-permute-done | bytes 589856 | tf_op jit(solution)/shard_map/ppermute | solution.py:542
  68.2 3.7 %local_last.1 = (f32[1152,768]{1,0:T(8,128)S(1)}, f32[384,768]{1,0:T(8,128)S(1)}, f32[8,128]{1,0:T(8,128)S(1)}) custom-call(f32[1]{0:T(128)S(6)} %copy.8.advect, f32[1152,768]{1,0:T(8,128)S(1)} %get-tuple-element.40.refs_0_.u1, bf16[384,768]{1,0:T(8,128)(2,1)S(1)} %get-tuple-element.41.refs_0_.refs_1_, ...), custom_call_target="tpu_custom_call" | custom-call | flops 1000 | bytes 1000 | tf_op jit(solution)/shard_map/local_last/pallas_call | solution.py:42
  71.9 5.8 %collective-permute-done.8.refs_2_ = bf16[1024,768]{1,0:T(8,128)(2,1)S(1)} collective-permute-done((bf16[1024,768]{1,0:T(8,128)(2,1)S(1)}, bf16[1024,768]{1,0:T(8,128)(2,1)S(1)}, u32[]{:S(2)}, u32[]{:S(2)}) %collective-permute-start.8) | collective-permute-done | bytes 1572896 | tf_op jit(solution)/shard_map/ppermute | solution.py:548
  77.7 1.3 %second_image.2 = (f32[1024,768]{1,0:T(8,128)S(1)}, f32[8,128]{1,0:T(8,128)S(1)}) custom-call(f32[384,768]{1,0:T(8,128)S(1)} %get-tuple-element.47.scale, f32[1152,768]{1,0:T(8,128)S(1)} %get-tuple-element.40.refs_0_.u1, f32[1152,768]{1,0:T(8,128)S(1)} %get-tuple-element.48.part, f32[8,128]{1,0:T(8,128)S(1)} %get-tuple-element.49.before, ...), custom_call_target="tpu_custom_call" | custom-call | flops 1000 | bytes 1000 | tf_op jit(solution)/shard_map/second_image/pallas_call | solution.py:42
  79.0 2.3 %collective-permute-done.9.refs_2_ = bf16[128,768]{1,0:T(8,128)(2,1)S(1)} collective-permute-done((bf16[128,768]{1,0:T(8,128)(2,1)S(1)}, bf16[128,768]{1,0:T(8,128)(2,1)S(1)}, u32[]{:S(2)}, u32[]{:S(2)}) %collective-permute-start.9) | collective-permute-done | bytes 196640 | tf_op jit(solution)/shard_map/ppermute | solution.py:548
  81.2 0.3 second_image.3
  81.5 13.0 %all_to_all.11 = f32[32,1,128]{2,1,0:T(1,128)S(1)} all-to-all(f32[32,1,128]{2,1,0:T(1,128)S(1)} %bitcast.10), channel_id=1, replica_groups=mesh['seg'=16,'rad'=2] {'rad','seg'}, dimensions={0} | all-to-all | bytes 32768 | tf_op jit(solution)/shard_map/all_to_all | solution.py:589
  94.5 2.1 %combine.1 = (f32[1152,768]{1,0:T(8,128)}, f32[6]{0:T(128)}) custom-call(f32[32,128]{1,0:T(8,128)S(1)} %bitcast.9, f32[1152,768]{1,0:T(8,128)S(1)} %get-tuple-element.40.refs_0_.u1, f32[128,768]{1,0:T(8,128)S(1)} %get-tuple-element.30.refs_0_.refs_9_, f32[1024,768]{1,0:T(8,128)S(1)} %get-tuple-element.32.refs_1_.refs_10_, ...), custom_call_target="tpu_custom_call" | custom-call | flops 1000 | bytes 1000 | tf_op jit(solution)/shard_map/combine/pallas_call | solution.py:42
Async XLA Ops:
  1.7 10.9 %collective-permute-start.3 = (bf16[128,768]{1,0:T(8,128)(2,1)S(1)}, bf16[128,768]{1,0:T(8,128)(2,1)S(1)}, u32[]{:S(2)}, u32[]{:S(2)}) collective-permute-start(bf16[128,768]{1,0:T(8,128)(2,1)S(1)} %get-tuple-element.31.refs_0_), channel_id=1, source_target_pairs={{0,1},{1,0},{2,3},{3,2},{4,5},{5,4},{6,7},{7,6},{8,9},{9,8},{10,11... | collective-permute-start | bytes 589832 | tf_op jit(solution)/shard_map/ppermute | solution.py:548
  6.6 37.4 %collective-permute-start.4 = (bf16[1024,768]{1,0:T(8,128)(2,1)S(1)}, bf16[1024,768]{1,0:T(8,128)(2,1)S(1)}, u32[]{:S(2)}, u32[]{:S(2)}) collective-permute-start(bf16[1024,768]{1,0:T(8,128)(2,1)S(1)} %get-tuple-element.39), channel_id=1, source_target_pairs={{0,1},{1,0},{2,3},{3,2},{4,5},{5,4},{6,7},{7,6},{8,9},{9,8},{10,11... | collective-permute-start | bytes 4718600 | tf_op jit(solution)/shard_map/ppermute | solution.py:548
  6.7 20.4 %collective-permute-start = (bf16[384,768]{1,0:T(8,128)(2,1)S(1)}, bf16[384,768]{1,0:T(8,128)(2,1)S(1)}, u32[]{:S(2)}, u32[]{:S(2)}) collective-permute-start(bf16[384,768]{1,0:T(8,128)(2,1)S(1)} %get-tuple-element.33.refs_0_.refs_2_), channel_id=1, source_target_pairs={{0,30},{2,0},{4,2},{6,4},{8,6},{10,8},{12,10},{14,12},{16,14},{18,... | collective-permute-start | bytes 1769480 | tf_op jit(solution)/shard_map/ppermute | solution.py:542
  10.6 16.5 %collective-permute-start.1 = (bf16[384,768]{1,0:T(8,128)(2,1)S(1)}, bf16[384,768]{1,0:T(8,128)(2,1)S(1)}, u32[]{:S(2)}, u32[]{:S(2)}) collective-permute-start(bf16[384,768]{1,0:T(8,128)(2,1)S(1)} %get-tuple-element.34.refs_1_.refs_3_), channel_id=1, source_target_pairs={{0,30},{2,0},{4,2},{6,4},{8,6},{10,8},{12,10},{14,12},{16,14},{18,... | collective-permute-start | bytes 1769480 | tf_op jit(solution)/shard_map/ppermute | solution.py:542
  11.8 18.8 %collective-permute-start.2 = (bf16[384,768]{1,0:T(8,128)(2,1)S(1)}, bf16[384,768]{1,0:T(8,128)(2,1)S(1)}, u32[]{:S(2)}, u32[]{:S(2)}) collective-permute-start(bf16[384,768]{1,0:T(8,128)(2,1)S(1)} %get-tuple-element.35.refs_2_.refs_4_), channel_id=1, source_target_pairs={{0,30},{2,0},{4,2},{6,4},{8,6},{10,8},{12,10},{14,12},{16,14},{18,... | collective-permute-start | bytes 1769480 | tf_op jit(solution)/shard_map/ppermute | solution.py:542
  33.4 44.3 %collective-permute-start.8 = (bf16[1024,768]{1,0:T(8,128)(2,1)S(1)}, bf16[1024,768]{1,0:T(8,128)(2,1)S(1)}, u32[]{:S(2)}, u32[]{:S(2)}) collective-permute-start(bf16[1024,768]{1,0:T(8,128)(2,1)S(1)} %get-tuple-element.50), channel_id=1, source_target_pairs={{0,1},{1,0},{2,3},{3,2},{4,5},{5,4},{6,7},{7,6},{8,9},{9,8},{10,11... | collective-permute-start | bytes 4718600 | tf_op jit(solution)/shard_map/ppermute | solution.py:548
  45.2 17.1 %collective-permute-start.5 = (bf16[384,768]{1,0:T(8,128)(2,1)S(1)}, bf16[384,768]{1,0:T(8,128)(2,1)S(1)}, u32[]{:S(2)}, u32[]{:S(2)}) collective-permute-start(bf16[384,768]{1,0:T(8,128)(2,1)S(1)} %get-tuple-element.41.refs_0_.refs_1_), channel_id=1, source_target_pairs={{0,30},{2,0},{4,2},{6,4},{8,6},{10,8},{12,10},{14,12},{16,14},{18,... | collective-permute-start | bytes 1769480 | tf_op jit(solution)/shard_map/ppermute | solution.py:542
  48.1 14.2 %collective-permute-start.6 = (bf16[384,768]{1,0:T(8,128)(2,1)S(1)}, bf16[384,768]{1,0:T(8,128)(2,1)S(1)}, u32[]{:S(2)}, u32[]{:S(2)}) collective-permute-start(bf16[384,768]{1,0:T(8,128)(2,1)S(1)} %get-tuple-element.42.refs_1_.refs_2_), channel_id=1, source_target_pairs={{0,30},{2,0},{4,2},{6,4},{8,6},{10,8},{12,10},{14,12},{16,14},{18,... | collective-permute-start | bytes 1769480 | tf_op jit(solution)/shard_map/ppermute | solution.py:542
  50.4 17.8 %collective-permute-start.7 = (bf16[384,768]{1,0:T(8,128)(2,1)S(1)}, bf16[384,768]{1,0:T(8,128)(2,1)S(1)}, u32[]{:S(2)}, u32[]{:S(2)}) collective-permute-start(bf16[384,768]{1,0:T(8,128)(2,1)S(1)} %get-tuple-element.43.refs_2_.refs_3_), channel_id=1, source_target_pairs={{0,30},{2,0},{4,2},{6,4},{8,6},{10,8},{12,10},{14,12},{16,14},{18,... | collective-permute-start | bytes 1769480 | tf_op jit(solution)/shard_map/ppermute | solution.py:542
  50.4 30.8 %collective-permute-start.9 = (bf16[128,768]{1,0:T(8,128)(2,1)S(1)}, bf16[128,768]{1,0:T(8,128)(2,1)S(1)}, u32[]{:S(2)}, u32[]{:S(2)}) collective-permute-start(bf16[128,768]{1,0:T(8,128)(2,1)S(1)} %get-tuple-element.52), channel_id=1, source_target_pairs={{0,1},{1,0},{2,3},{3,2},{4,5},{5,4},{6,7},{7,6},{8,9},{9,8},{10,11... | collective-permute-start | bytes 589832 | tf_op jit(solution)/shard_map/ppermute | solution.py:548
